TPU v7x, 512 devices: a whole 4x8x8 slice. The times are simulated.
512 devices in a mesh: bn: 32 (over x, y), grp: 16 (over z, core).
Axes of the slice: x: 4, y: 8, z: 8, core: 2. Of those that a mesh axis runs over, the one named last changes fastest.
Arguments:
- block_input: bfloat16 [16, 32, 29, 29, 176], P('grp', 'bn'), may hold values from -180 to 180
- cotangent: bfloat16 [16, 32, 29, 29, 176], P('grp', 'bn'), may hold values from -70 to 70
- w_expand: bfloat16 [176, 1056], replicated, may hold values from -0.4375 to 0.4375
- gain_expand: float32 [1056], replicated, may hold values from 0.1 to 1.9
- shift_expand: float32 [1056], replicated, may hold values from -3 to 3
- w_depth: bfloat16 [25, 1056], replicated, may hold values from -1.25 to 1.25
- gain_depth: float32 [1056], replicated, may hold values from 0.1 to 1.9
- shift_depth: float32 [1056], replicated, may hold values from -3 to 3
- w_reduce: bfloat16 [1056, 44], replicated, may hold values from -0.1875 to 0.1875
- b_reduce: float32 [44], replicated, may hold values from -4 to 4
- w_restore: bfloat16 [44, 1056], replicated, may hold values from -0.875 to 0.875
- b_restore: float32 [1056], replicated, may hold values from -4 to 4
- w_project: bfloat16 [1056, 176], replicated, may hold values from -0.1875 to 0.1875
- gain_project: float32 [176], replicated, may hold values from 0.1 to 1.9
- upper_grads: float32 [512, 131072], P(('bn', 'grp')), may hold values from -1 to 1
Outputs:
- input_grad: bfloat16 [16, 32, 29, 29, 176], P('grp', 'bn')
- grad_expand: float32 [176, 1056], replicated
- grad_gain_expand: float32 [1056], replicated
- grad_shift_expand: float32 [1056], replicated
- grad_depth: float32 [25, 1056], replicated
- grad_gain_depth: float32 [1056], replicated
- grad_shift_depth: float32 [1056], replicated
- grad_reduce: float32 [1056, 44], replicated
- grad_b_reduce: float32 [44], replicated
- grad_restore: float32 [44, 1056], replicated
- grad_b_restore: float32 [1056], replicated
- grad_project: float32 [1056, 176], replicated
- grad_gain_project: float32 [176], replicated
- upper_summed: float32 [131072], replicated
All inputs are finite; a program needn't handle non-finite values.
Results may differ from a plain program's by a relative error of at most 0.0054.
Values sent between devices are 32-bit elements; how exact they have to be, the bound alone decides.
No kernel may reach another device: no remote copies, remote signals or barrier semaphores. Data moves between devices by JAX's collectives and lax.ppermute only.
A program may use at most 64 MiB of HBM per device.

v0:
```python
import jax
import jax.numpy as jnp
from jax import lax
from jax.sharding import PartitionSpec as P

KER = 5


EPSILON = 0.001
exact_precision = lax.Precision.HIGHEST


def silu_slope(values):
    logistic = jax.nn.sigmoid(values)
    return logistic * (1.0 + values * (1.0 - logistic))


def pad_map(field):
    margin = KER // 2
    return jnp.pad(field, ((0, 0), (margin, margin), (margin, margin), (0, 0)))


def depthwise(field, kernel):
    extent = field.shape[1]
    padded = pad_map(field)
    summed = jnp.zeros(field.shape, jnp.float32)
    for row_off in range(KER):
        for col_off in range(KER):
            window = padded[:, row_off : row_off + extent, col_off : col_off + extent, :].astype(
                jnp.float32
            )
            summed = summed + window * kernel[row_off * KER + col_off].astype(jnp.float32)
    return summed


def depth_input_grad(grad_out, kernel):
    extent = grad_out.shape[1]
    margin = KER // 2
    padded = pad_map(grad_out)
    summed = jnp.zeros(grad_out.shape, jnp.float32)
    for row_off in range(KER):
        for col_off in range(KER):
            row_start = 2 * margin - row_off
            col_start = 2 * margin - col_off
            window = padded[:, row_start : row_start + extent, col_start : col_start + extent, :]
            summed = summed + window * kernel[row_off * KER + col_off].astype(jnp.float32)
    return summed


def depth_kernel_grad(field, grad_out):
    extent = field.shape[1]
    padded = pad_map(field)
    columns = []
    for row_off in range(KER):
        for col_off in range(KER):
            window = padded[:, row_off : row_off + extent, col_off : col_off + extent, :].astype(
                jnp.float32
            )
            columns.append(jnp.sum(window * grad_out, axis=(0, 1, 2)))
    return jnp.stack(columns)


def group_rows(values):
    return values.shape[0] * values.shape[1] * values.shape[2] * lax.axis_size("bn")


def group_norm(values):
    row_count = group_rows(values)
    center = lax.psum(jnp.sum(values, axis=(0, 1, 2)), "bn") / row_count
    spread = lax.psum(jnp.sum(jnp.square(values - center), axis=(0, 1, 2)), "bn") / row_count
    scaling = lax.rsqrt(spread + EPSILON)
    return ((values - center) * scaling, scaling)


def norm_back(grad_normed, normed, scaling):
    row_count = group_rows(normed)
    first, second = lax.psum(
        (jnp.sum(grad_normed, axis=(0, 1, 2)), jnp.sum(grad_normed * normed, axis=(0, 1, 2))), "bn"
    )
    return scaling * (grad_normed - first / row_count - normed * (second / row_count))


def per_device(
    block_input,
    cotangent,
    w_expand,
    gain_expand,
    shift_expand,
    w_depth,
    gain_depth,
    shift_depth,
    w_reduce,
    b_reduce,
    w_restore,
    b_restore,
    w_project,
    gain_project,
    upper_grads,
):
    images = block_input[0]
    incoming = cotangent[0].astype(jnp.float32)
    extent = images.shape[1]
    pre_expand = jnp.dot(images, w_expand, preferred_element_type=jnp.float32)
    normed_one, scale_one = group_norm(pre_expand)
    act_one = normed_one * gain_expand + shift_expand
    expanded = jax.nn.silu(act_one).astype(jnp.bfloat16)
    pre_depth = depthwise(expanded, w_depth)
    normed_two, scale_two = group_norm(pre_depth)
    act_two = normed_two * gain_depth + shift_depth
    activated = jax.nn.silu(act_two).astype(jnp.bfloat16)
    pooled = jnp.mean(activated.astype(jnp.float32), axis=(1, 2))
    logit_reduce = (
        jnp.dot(pooled, w_reduce.astype(jnp.float32), precision=exact_precision) + b_reduce
    )
    squeezed = jax.nn.silu(logit_reduce)
    logit_restore = (
        jnp.dot(squeezed, w_restore.astype(jnp.float32), precision=exact_precision) + b_restore
    )
    excite = jax.nn.sigmoid(logit_restore)
    hidden = (activated.astype(jnp.float32) * excite[:, None, None, :]).astype(jnp.bfloat16)
    pre_project = jnp.dot(hidden, w_project, preferred_element_type=jnp.float32)
    normed_three, scale_three = group_norm(pre_project)
    grad_gain_project = jnp.sum(incoming * normed_three, axis=(0, 1, 2))
    grad_pre_project = norm_back(incoming * gain_project, normed_three, scale_three).astype(
        jnp.bfloat16
    )
    grad_project = jnp.dot(
        hidden.reshape(-1, hidden.shape[-1]).T,
        grad_pre_project.reshape(-1, grad_pre_project.shape[-1]),
        preferred_element_type=jnp.float32,
    )
    grad_hidden = jnp.dot(grad_pre_project, w_project.T, preferred_element_type=jnp.float32)
    grad_excite = jnp.sum(grad_hidden * activated.astype(jnp.float32), axis=(1, 2))
    grad_logit_restore = grad_excite * excite * (1.0 - excite)
    grad_restore = jnp.dot(squeezed.T, grad_logit_restore, precision=exact_precision)
    grad_b_restore = jnp.sum(grad_logit_restore, axis=0)
    grad_squeezed = jnp.dot(
        grad_logit_restore, w_restore.astype(jnp.float32).T, precision=exact_precision
    )
    grad_logit_reduce = grad_squeezed * silu_slope(logit_reduce)
    grad_reduce = jnp.dot(pooled.T, grad_logit_reduce, precision=exact_precision)
    grad_b_reduce = jnp.sum(grad_logit_reduce, axis=0)
    grad_pooled = jnp.dot(
        grad_logit_reduce, w_reduce.astype(jnp.float32).T, precision=exact_precision
    )
    grad_activated = grad_hidden * excite[:, None, None, :] + grad_pooled[:, None, None, :] / (
        extent * extent
    )
    grad_act_two = grad_activated * silu_slope(act_two)
    grad_shift_depth = jnp.sum(grad_act_two, axis=(0, 1, 2))
    grad_gain_depth = jnp.sum(grad_act_two * normed_two, axis=(0, 1, 2))
    grad_pre_depth = norm_back(grad_act_two * gain_depth, normed_two, scale_two)
    grad_depth = depth_kernel_grad(expanded, grad_pre_depth)
    grad_expanded = depth_input_grad(grad_pre_depth, w_depth)
    grad_act_one = grad_expanded * silu_slope(act_one)
    grad_shift_expand = jnp.sum(grad_act_one, axis=(0, 1, 2))
    grad_gain_expand = jnp.sum(grad_act_one * normed_one, axis=(0, 1, 2))
    grad_pre_expand = norm_back(grad_act_one * gain_expand, normed_one, scale_one).astype(
        jnp.bfloat16
    )
    grad_expand = jnp.dot(
        images.reshape(-1, images.shape[-1]).T,
        grad_pre_expand.reshape(-1, grad_pre_expand.shape[-1]),
        preferred_element_type=jnp.float32,
    )
    input_grad = (
        incoming + jnp.dot(grad_pre_expand, w_expand.T, preferred_element_type=jnp.float32)
    ).astype(jnp.bfloat16)
    summed = lax.psum(
        (
            upper_grads[0],
            grad_expand,
            grad_gain_expand,
            grad_shift_expand,
            grad_depth,
            grad_gain_depth,
            grad_shift_depth,
            grad_reduce,
            grad_b_reduce,
            grad_restore,
            grad_b_restore,
            grad_project,
            grad_gain_project,
        ),
        ("bn", "grp"),
    )
    upper_summed = summed[0]
    window_sums = summed[1:]
    images_total = images.shape[0] * lax.axis_size("bn") * lax.axis_size("grp")
    scaled = [piece / images_total for piece in window_sums]
    return (
        input_grad[None],
        scaled[0],
        scaled[1],
        scaled[2],
        scaled[3],
        scaled[4],
        scaled[5],
        scaled[6],
        scaled[7],
        scaled[8],
        scaled[9],
        scaled[10],
        scaled[11],
        upper_summed,
    )


def solution(mesh):
    return jax.shard_map(
        per_device,
        mesh=mesh,
        in_specs=(
            P("grp", "bn", None, None, None),
            P("grp", "bn", None, None, None),
            P(),
            P(),
            P(),
            P(),
            P(),
            P(),
            P(),
            P(),
            P(),
            P(),
            P(),
            P(),
            P(("bn", "grp"), None),
        ),
        out_specs=(
            P("grp", "bn", None, None, None),
            P(),
            P(),
            P(),
            P(),
            P(),
            P(),
            P(),
            P(),
            P(),
            P(),
            P(),
            P(),
            P(),
        ),
        check_vma=False,
    )
```

profile of v0, /device:TPU:1, one launch (start us, length us, event | category | flops | bytes accessed | tf_op | source)
XLA Modules:
  0.0 1250.6 jit_solution(4917659274947953306)
XLA Ops:
  11.3 3.9 fusion.148
  15.1 63.5 %psum.175 = f32[1056]{0:T(1024)S(1)} all-reduce(f32[1056]{0:T(1024)S(1)} %get-tuple-element.100), channel_id=1, replica_groups=mesh['bn'=32,'grp'=16] {'bn'}, use_global_device_ids=true, to_apply=%region_1.0 | all-reduce | flops 1056 | bytes 8448 | tf_op jit(solution)/shard_map/psum | solution.py:69
  81.4 57.1 %psum.176 = f32[1056]{0:T(1024)S(1)} all-reduce(f32[1056]{0:T(1024)S(1)} %multiply_reduce_fusion.3), channel_id=1, replica_groups=mesh['bn'=32,'grp'=16] {'bn'}, use_global_device_ids=true, to_apply=%region_3.0 | all-reduce | flops 1056 | bytes 8448 | tf_op jit(solution)/shard_map/psum | solution.py:70
  138.6 3.7 fusion.160
  142.6 19.3 %fusion.146 = (f32[1056]{0:T(1024)S(1)}, f32[1,29,29,1056]{3,2,1,0:T(8,128)}) fusion(f32[1056]{0:T(1024)S(1)} %get-tuple-element.72, f32[1056]{0:T(1024)S(1)} %get-tuple-element.73, f32[1056]{0:T(1024)S(1)} %get-tuple-element.50, f32[1056]{0:T(1024)S(1)} %get-tuple-element.51, f32[1056]{0:T(1024)S(1)} %get-tuple-element.52, f32[1056]{0:T(1024)S(1)} %get-tuple-element.53, ...), kind=kLoop, calls=%fused_computation.322 | loop fusion | flops 74599008 | bytes 9007680 | tf_op jit(solution)/shard_map/reduce_sum | solution.py:69
  161.9 58.1 %psum.177 = f32[1056]{0:T(1024)S(1)} all-reduce(f32[1056]{0:T(1024)S(1)} %get-tuple-element.98), channel_id=1, replica_groups=mesh['bn'=32,'grp'=16] {'bn'}, use_global_device_ids=true, to_apply=%region_5.6 | all-reduce | flops 1056 | bytes 8448 | tf_op jit(solution)/shard_map/psum | solution.py:69
  220.0 2.7 multiply_reduce_fusion.2
  222.8 57.2 %psum.178 = f32[1056]{0:T(1024)S(1)} all-reduce(f32[1056]{0:T(1024)S(1)} %multiply_reduce_fusion.2), channel_id=1, replica_groups=mesh['bn'=32,'grp'=16] {'bn'}, use_global_device_ids=true, to_apply=%region_7.8 | all-reduce | flops 1056 | bytes 8448 | tf_op jit(solution)/shard_map/psum | solution.py:70
  280.1 3.8 convert_reduce_fusion
  287.0 57.3 %psum.179 = f32[176]{0:T(256)S(1)} all-reduce(f32[176]{0:T(256)S(1)} %get-tuple-element.102), channel_id=1, replica_groups=mesh['bn'=32,'grp'=16] {'bn'}, use_global_device_ids=true, to_apply=%region_10.11 | all-reduce | flops 176 | bytes 1408 | tf_op jit(solution)/shard_map/psum | solution.py:69
  345.7 56.2 %psum.180 = f32[176]{0:T(256)S(1)} all-reduce(f32[176]{0:T(256)S(1)} %multiply_reduce_fusion.6), channel_id=1, replica_groups=mesh['bn'=32,'grp'=16] {'bn'}, use_global_device_ids=true, to_apply=%region_12.13 | all-reduce | flops 176 | bytes 1408 | tf_op jit(solution)/shard_map/psum | solution.py:70
  404.2 57.3 %all-reduce.6 = (f32[176]{0:T(256)S(1)}, f32[176]{0:T(256)S(1)}) all-reduce(f32[176]{0:T(256)S(1)} %get-tuple-element.48, f32[176]{0:T(256)S(1)} %fusion.133), channel_id=1, replica_groups=mesh['bn'=32,'grp'=16] {'bn'}, use_global_device_ids=true, to_apply=%region_16.17 | all-reduce | flops 352 | bytes 2816 | tf_op jit(solution)/shard_map/psum | solution.py:77
  463.2 3.3 convolution_bitcast_fusion
  468.7 6.2 multiply_reduce_fusion
  474.9 110.3 %all-reduce.5 = (f32[1056]{0:T(1024)}, f32[1056]{0:T(1024)}) all-reduce(f32[1056]{0:T(1024)} %get-tuple-element.15, f32[1056]{0:T(1024)} %get-tuple-element.43), channel_id=1, replica_groups=mesh['bn'=32,'grp'=16] {'bn'}, use_global_device_ids=true, to_apply=%region_21.22 | all-reduce | flops 2112 | bytes 16896 | tf_op jit(solution)/shard_map/psum | solution.py:77
  586.5 18.8 %fusion.50 = (f32[1056]{0:T(1024)}, f32[1056]{0:T(1024)}, f32[1056]{0:T(1024)}, f32[1056]{0:T(1024)}, f32[1056]{0:T(1024)}, /*index=5*/f32[1056]{0:T(1024)}, f32...) fusion(bf16[1,29,29,1056]{3,2,1,0:T(8,128)(2,1)S(1)} %fusion.16, ...), kind=kLoop, calls=%fused_computation.151 | loop fusion | flops 54154848 | bytes 12530496 | tf_op jit(solution)/shard_map/reduce_sum | solution.py:59
  607.4 6.9 fusion.29
  614.5 61.3 %fusion.105 = (f32[1056]{0:T(1024)S(1)}, f32[1056]{0:T(1024)S(1)}, f32[1056]{0:T(1024)S(1)}, f32[1056]{0:T(1024)S(1)}, f32[1,29,29,1056]{3,2,1,0:T(8,128)}) fusion(f32[29,29,1056]{2,1,0:T(8,128)} %get-tuple-element.101, f32[1056]{0:T(1024)S(1)} %add_rsqrt_fusion.1, f32[1056]{0:T(1024)S(1)} %broadcast_multiply_fusion.19, f32[1056]{0:T(1024)} %param.18, ...), kind=kLoop, calls=%fused_computation.209 | loop fusion | flops 60386304 | bytes 12359552 | tf_op jit(solution)/shard_map/reduce_sum | solution.py:157
  677.2 110.1 %all-reduce.4 = (f32[1056]{0:T(1024)S(1)}, f32[1056]{0:T(1024)S(1)}) all-reduce(f32[1056]{0:T(1024)S(1)} %get-tuple-element.17, f32[1056]{0:T(1024)S(1)} %get-tuple-element.42), channel_id=1, replica_groups=mesh['bn'=32,'grp'=16] {'bn'}, use_global_device_ids=true, to_apply=%region_25.26 | all-reduce | flops 2112 | bytes 16896 | tf_op jit(solution)/shard_map/psum | solution.py:77
  787.3 6.0 fusion.103
  793.3 2.9 reshape.454
  800.5 255.0 %all-reduce.2 = (f32[1056]{0:T(1024)S(1)}, f32[1056]{0:T(1024)S(1)}, f32[1056]{0:T(1024)S(1)}, f32[1056]{0:T(1024)S(1)}, f32[44]{0:T(128)S(1)}, /*index=5*/f32[1056]{0:T(1024)S(1)}, f32[176]{0:T(256)S(1)}) all-reduce(f32[1056]{0:T(1024)S(1)} %get-tuple-element.16, ...), channel_id=1, replica_groups=mesh['bn'=32,'grp'=16] {'bn','grp'}, use_global_device_ids=true, to_apply=%region_28.29 | all-reduce | flops 5500 | bytes 44000 | tf_op jit(solution)/shard_map/psum | solution.py:169
  1059.6 3.2 fusion.118
  1062.8 171.1 %all-reduce.9.cloned.1.call-done = (f32[176,1056]{1,0:T(8,128)}, f32[25,1056]{1,0:T(8,128)}, f32[1056,44]{0,1:T(8,128)}, f32[44,1056]{1,0:T(8,128)}, f32[1056,176]{0,1:T(8,128)}, /*index=5*/f32[131072]{0:T(1024)}) async-done(((f32[176,1056]{1,0:T(8,128)}, f32[25,1056]{1,0:T(8,128)}, f32[1056,44]{0,1:T(8,128)}, f32[44,1056]{1,0:T(8,128)}, f32[1056,176]{0,1:T(8,128)}, /*index=5*/f32[131072]{0:T(1024)}), ...) | async-done | bytes 2488464 | tf_op jit(solution)/shard_map/psum | solution.py:169
  (253 shorter events, 39.7 us)
Async XLA Ops:
  7.2 278.1 %copy-start = (bf16[1056,176]{0,1:T(8,128)(2,1)S(1)}, bf16[1056,176]{0,1:T(8,128)(2,1)}, u32[]{:S(2)}) copy-start(bf16[1056,176]{0,1:T(8,128)(2,1)} %param.27) | copy-start | bytes 1115140
  7.2 1226.7 %all-reduce.9.cloned.1.call-start = ((), (), s32[]{:S(2)}) async-start(), calls=%async_computation | async-start | bytes 5472256 | tf_op jit(solution)/shard_map/psum | solution.py:169
  8.2 134.1 %copy-start.24 = (f32[1056]{0:T(1024)}, f32[1056]{0:T(1024)S(1)}, u32[]{:S(2)}) copy-start(f32[1056]{0:T(1024)S(1)} %get-tuple-element.68) | copy-start | bytes 12676
  8.2 134.1 %copy-start.25 = (f32[1056]{0:T(1024)}, f32[1056]{0:T(1024)S(1)}, u32[]{:S(2)}) copy-start(f32[1056]{0:T(1024)S(1)} %get-tuple-element.69) | copy-start | bytes 12676
  8.2 134.1 %copy-start.26 = (f32[1056]{0:T(1024)}, f32[1056]{0:T(1024)S(1)}, u32[]{:S(2)}) copy-start(f32[1056]{0:T(1024)S(1)} %get-tuple-element.70) | copy-start | bytes 12676
  8.2 134.1 %copy-start.27 = (f32[1056]{0:T(1024)}, f32[1056]{0:T(1024)S(1)}, u32[]{:S(2)}) copy-start(f32[1056]{0:T(1024)S(1)} %get-tuple-element.71) | copy-start | bytes 12676
  8.2 134.1 %copy-start.28 = (f32[1056]{0:T(1024)}, f32[1056]{0:T(1024)S(1)}, u32[]{:S(2)}) copy-start(f32[1056]{0:T(1024)S(1)} %get-tuple-element.72) | copy-start | bytes 12676
  8.3 134.1 %copy-start.29 = (f32[1056]{0:T(1024)}, f32[1056]{0:T(1024)S(1)}, u32[]{:S(2)}) copy-start(f32[1056]{0:T(1024)S(1)} %get-tuple-element.73) | copy-start | bytes 12676
  9.8 132.6 %copy-start.30 = (f32[1056]{0:T(1024)}, f32[1056]{0:T(1024)S(1)}, u32[]{:S(2)}) copy-start(f32[1056]{0:T(1024)S(1)} %get-tuple-element.49) | copy-start | bytes 12676
  9.8 132.6 %copy-start.31 = (f32[1056]{0:T(1024)}, f32[1056]{0:T(1024)S(1)}, u32[]{:S(2)}) copy-start(f32[1056]{0:T(1024)S(1)} %get-tuple-element.50) | copy-start | bytes 12676
  9.8 132.6 %copy-start.32 = (f32[1056]{0:T(1024)}, f32[1056]{0:T(1024)S(1)}, u32[]{:S(2)}) copy-start(f32[1056]{0:T(1024)S(1)} %get-tuple-element.51) | copy-start | bytes 12676
  9.8 132.6 %copy-start.33 = (f32[1056]{0:T(1024)}, f32[1056]{0:T(1024)S(1)}, u32[]{:S(2)}) copy-start(f32[1056]{0:T(1024)S(1)} %get-tuple-element.52) | copy-start | bytes 12676
  9.8 132.6 %copy-start.34 = (f32[1056]{0:T(1024)}, f32[1056]{0:T(1024)S(1)}, u32[]{:S(2)}) copy-start(f32[1056]{0:T(1024)S(1)} %get-tuple-element.53) | copy-start | bytes 12676
  9.9 132.6 %copy-start.35 = (f32[1056]{0:T(1024)}, f32[1056]{0:T(1024)S(1)}, u32[]{:S(2)}) copy-start(f32[1056]{0:T(1024)S(1)} %get-tuple-element.54) | copy-start | bytes 12676
  9.9 132.6 %copy-start.36 = (f32[1056]{0:T(1024)}, f32[1056]{0:T(1024)S(1)}, u32[]{:S(2)}) copy-start(f32[1056]{0:T(1024)S(1)} %get-tuple-element.55) | copy-start | bytes 12676
  9.9 132.6 %copy-start.37 = (f32[1056]{0:T(1024)}, f32[1056]{0:T(1024)S(1)}, u32[]{:S(2)}) copy-start(f32[1056]{0:T(1024)S(1)} %get-tuple-element.56) | copy-start | bytes 12676
  9.9 132.6 %copy-start.38 = (f32[1056]{0:T(1024)}, f32[1056]{0:T(1024)S(1)}, u32[]{:S(2)}) copy-start(f32[1056]{0:T(1024)S(1)} %get-tuple-element.57) | copy-start | bytes 12676
  9.9 132.6 %copy-start.39 = (f32[1056]{0:T(1024)}, f32[1056]{0:T(1024)S(1)}, u32[]{:S(2)}) copy-start(f32[1056]{0:T(1024)S(1)} %get-tuple-element.58) | copy-start | bytes 12676
  9.9 132.6 %copy-start.40 = (f32[1056]{0:T(1024)}, f32[1056]{0:T(1024)S(1)}, u32[]{:S(2)}) copy-start(f32[1056]{0:T(1024)S(1)} %get-tuple-element.59) | copy-start | bytes 12676
  9.9 132.6 %copy-start.41 = (f32[1056]{0:T(1024)}, f32[1056]{0:T(1024)S(1)}, u32[]{:S(2)}) copy-start(f32[1056]{0:T(1024)S(1)} %get-tuple-element.60) | copy-start | bytes 12676
  9.9 132.6 %copy-start.42 = (f32[1056]{0:T(1024)}, f32[1056]{0:T(1024)S(1)}, u32[]{:S(2)}) copy-start(f32[1056]{0:T(1024)S(1)} %get-tuple-element.61) | copy-start | bytes 12676
  284.9 182.5 %copy-start.49 = (f32[1056]{0:T(1024)}, f32[1056]{0:T(1024)S(1)}, u32[]{:S(2)}) copy-start(f32[1056]{0:T(1024)S(1)} %add_divide_fusion.2) | copy-start | bytes 12676
  468.7 138.6 %slice-start = ((s8[4276224]{0:T(1024)(128)(4,1)}), s8[81920]{0:T(1024)(128)(4,1)S(1)}, s32[]{:S(2)}) async-start(s8[4276224]{0:T(1024)(128)(4,1)} %bitcast.129), calls=%async_computation.1 | async-start | bytes 163840
  614.5 172.7 %copy-start.9 = (f32[1056]{0:T(1024)S(1)}, f32[1056]{0:T(1024)}, u32[]{:S(2)}) copy-start(f32[1056]{0:T(1024)} %param.18) | copy-start | bytes 12676
  (65 other events, 3508.1 us)
Sparse Core Ops, SparseCore 0:
  800.6 433.2 all-reduce.8
where the time goes:
time: 1250 us
  blocking collectives  882 us (71%)
  waiting for transfers between devices  171 us (14%)
  other arithmetic  155 us (12%)
  matrix products  15.9 us (1%)
  between operations  15.6 us (1%)
    psum x3, blocking collectives, norm_back(): lax.psum((jnp.sum(grad_normed, axis=(0, 1, 2)), jnp.sum(grad_normed * nor...  278 us
    psum x1, blocking collectives, per_device(): lax.psum((upper_grads[0], grad_expand, grad_gain_expand, grad_shift_expan...  255 us
    psum x3, blocking collectives, group_norm(): center = lax.psum(jnp.sum(values, axis=(0, 1, 2)), 'bn') / row_count  179 us
    psum x1, waiting for transfers between devices, per_device(): lax.psum((upper_grads[0], grad_expand, grad_gain_expand, grad_shift_expan...  171 us
    psum x3, blocking collectives, group_norm(): lax.psum(jnp.sum(jnp.square(values - center), axis=(0, 1, 2)), 'bn')  171 us
    reduce_sum x1, other arithmetic, per_device(): grad_gain_expand = jnp.sum(grad_act_one * normed_one, axis=(0, 1, 2))  61.3 us
    reduce_sum x2, other arithmetic, depth_kernel_grad(): columns.append(jnp.sum(window * grad_out, axis=(0, 1, 2)))  25.7 us
  transfers between devices with their start and end apart: 1, of which 1 were waited for; matrix products, arithmetic and copies ran while one was open for 1% of the time, Pallas kernels for 0%

commit v1 on v0

--- a/solution.py
+++ b/solution.py
@@ -1,7 +1,7 @@
 import jax
 import jax.numpy as jnp
 from jax import lax
-from jax.sharding import PartitionSpec as P
+from jax.sharding import Mesh, PartitionSpec as P
 
 KER = 5
 
@@ -60,24 +60,52 @@
     return jnp.stack(columns)
 
 
+AXES = ("x", "y", "z", "core")
+GROUP = ("x", "y")
+
+
 def group_rows(values):
-    return values.shape[0] * values.shape[1] * values.shape[2] * lax.axis_size("bn")
-
-
-def group_norm(values):
-    row_count = group_rows(values)
-    center = lax.psum(jnp.sum(values, axis=(0, 1, 2)), "bn") / row_count
-    spread = lax.psum(jnp.sum(jnp.square(values - center), axis=(0, 1, 2)), "bn") / row_count
+    return values.shape[0] * values.shape[1] * values.shape[2] * lax.axis_size(GROUP)
+
+
+def local_moments(values):
+    mean = jnp.mean(values, axis=(0, 1, 2))
+    spread = jnp.mean(jnp.square(values - mean), axis=(0, 1, 2))
+    return mean, spread
+
+
+def merge_moments(means, spreads):
+    center = jnp.mean(means, axis=0)
+    return center, jnp.mean(spreads + jnp.square(means - center), axis=0)
+
+
+def gather_by_exchange(vector):
+    size = lax.axis_size(GROUP)
+    tiled = jnp.broadcast_to(vector[None], (size,) + vector.shape)
+    return lax.all_to_all(tiled, GROUP, 0, 0, tiled=True)
+
+
+def ring_parts(vector, axis):
+    size = lax.axis_size(axis)
+    return [vector] + [
+        lax.ppermute(vector, axis, [(i, (i + step) % size) for i in range(size)])
+        for step in range(1, size)
+    ]
+
+
+def doubling_sum(vector):
+    for axis in GROUP:
+        size = lax.axis_size(axis)
+        step = 1
+        while step < size:
+            vector = vector + lax.ppermute(vector, axis, [(i, i ^ step) for i in range(size)])
+            step *= 2
+    return vector
+
+
+def rows_to_norm(values, center, spread):
     scaling = lax.rsqrt(spread + EPSILON)
     return ((values - center) * scaling, scaling)
-
-
-def norm_back(grad_normed, normed, scaling):
-    row_count = group_rows(normed)
-    first, second = lax.psum(
-        (jnp.sum(grad_normed, axis=(0, 1, 2)), jnp.sum(grad_normed * normed, axis=(0, 1, 2))), "bn"
-    )
-    return scaling * (grad_normed - first / row_count - normed * (second / row_count))
 
 
 def per_device(
@@ -97,15 +125,21 @@
     gain_project,
     upper_grads,
 ):
+    upper_summed = lax.psum(upper_grads[0], AXES)
     images = block_input[0]
     incoming = cotangent[0].astype(jnp.float32)
     extent = images.shape[1]
     pre_expand = jnp.dot(images, w_expand, preferred_element_type=jnp.float32)
-    normed_one, scale_one = group_norm(pre_expand)
+    hid = pre_expand.shape[-1]
+    gathered = gather_by_exchange(jnp.stack(local_moments(pre_expand)))
+    center_one, spread_one = merge_moments(gathered[:, 0], gathered[:, 1])
+    normed_one, scale_one = rows_to_norm(pre_expand, center_one, spread_one)
     act_one = normed_one * gain_expand + shift_expand
     expanded = jax.nn.silu(act_one).astype(jnp.bfloat16)
     pre_depth = depthwise(expanded, w_depth)
-    normed_two, scale_two = group_norm(pre_depth)
+    gathered = lax.all_gather(jnp.concatenate(local_moments(pre_depth)), GROUP)
+    center_two, spread_two = merge_moments(gathered[:, :hid], gathered[:, hid:])
+    normed_two, scale_two = rows_to_norm(pre_depth, center_two, spread_two)
     act_two = normed_two * gain_depth + shift_depth
     activated = jax.nn.silu(act_two).astype(jnp.bfloat16)
     pooled = jnp.mean(activated.astype(jnp.float32), axis=(1, 2))
@@ -119,11 +153,24 @@
     excite = jax.nn.sigmoid(logit_restore)
     hidden = (activated.astype(jnp.float32) * excite[:, None, None, :]).astype(jnp.bfloat16)
     pre_project = jnp.dot(hidden, w_project, preferred_element_type=jnp.float32)
-    normed_three, scale_three = group_norm(pre_project)
+    row_count = group_rows(pre_project)
+    mean_three, spread_three = local_moments(pre_project)
+    cot_sum = jnp.sum(incoming, axis=(0, 1, 2))
+    cot_dev = jnp.sum(incoming * (pre_project - mean_three), axis=(0, 1, 2))
+    packed = jnp.stack([mean_three, spread_three, cot_sum, cot_dev])
+    for axis in GROUP:
+        parts = jnp.stack(ring_parts(packed, axis))
+        center, spread = merge_moments(parts[:, 0], parts[:, 1])
+        dev = jnp.sum(parts[:, 3] + parts[:, 2] * (parts[:, 0] - center), axis=0)
+        packed = jnp.stack([center, spread, jnp.sum(parts[:, 2], axis=0), dev])
+    normed_three, scale_three = rows_to_norm(pre_project, packed[0], packed[1])
+    second = packed[3] * scale_three
     grad_gain_project = jnp.sum(incoming * normed_three, axis=(0, 1, 2))
-    grad_pre_project = norm_back(incoming * gain_project, normed_three, scale_three).astype(
-        jnp.bfloat16
-    )
+    grad_pre_project = (
+        scale_three
+        * gain_project
+        * (incoming - packed[2] / row_count - normed_three * (second / row_count))
+    ).astype(jnp.bfloat16)
     grad_project = jnp.dot(
         hidden.reshape(-1, hidden.shape[-1]).T,
         grad_pre_project.reshape(-1, grad_pre_project.shape[-1]),
@@ -149,15 +196,22 @@
     grad_act_two = grad_activated * silu_slope(act_two)
     grad_shift_depth = jnp.sum(grad_act_two, axis=(0, 1, 2))
     grad_gain_depth = jnp.sum(grad_act_two * normed_two, axis=(0, 1, 2))
-    grad_pre_depth = norm_back(grad_act_two * gain_depth, normed_two, scale_two)
+    sums = doubling_sum(jnp.concatenate([grad_shift_depth, grad_gain_depth]))
+    grad_pre_depth = (scale_two * gain_depth) * (
+        grad_act_two - sums[:hid] / row_count - normed_two * (sums[hid:] / row_count)
+    )
     grad_depth = depth_kernel_grad(expanded, grad_pre_depth)
     grad_expanded = depth_input_grad(grad_pre_depth, w_depth)
     grad_act_one = grad_expanded * silu_slope(act_one)
     grad_shift_expand = jnp.sum(grad_act_one, axis=(0, 1, 2))
     grad_gain_expand = jnp.sum(grad_act_one * normed_one, axis=(0, 1, 2))
-    grad_pre_expand = norm_back(grad_act_one * gain_expand, normed_one, scale_one).astype(
-        jnp.bfloat16
-    )
+    sums = jnp.concatenate([grad_shift_expand, grad_gain_expand])
+    for axis in GROUP:
+        sums = lax.psum(sums, axis)
+    grad_pre_expand = (
+        (scale_one * gain_expand)
+        * (grad_act_one - sums[:hid] / row_count - normed_one * (sums[hid:] / row_count))
+    ).astype(jnp.bfloat16)
     grad_expand = jnp.dot(
         images.reshape(-1, images.shape[-1]).T,
         grad_pre_expand.reshape(-1, grad_pre_expand.shape[-1]),
@@ -166,28 +220,30 @@
     input_grad = (
         incoming + jnp.dot(grad_pre_expand, w_expand.T, preferred_element_type=jnp.float32)
     ).astype(jnp.bfloat16)
-    summed = lax.psum(
-        (
-            upper_grads[0],
-            grad_expand,
-            grad_gain_expand,
-            grad_shift_expand,
-            grad_depth,
-            grad_gain_depth,
-            grad_shift_depth,
-            grad_reduce,
-            grad_b_reduce,
-            grad_restore,
-            grad_b_restore,
-            grad_project,
-            grad_gain_project,
-        ),
-        ("bn", "grp"),
-    )
-    upper_summed = summed[0]
-    window_sums = summed[1:]
-    images_total = images.shape[0] * lax.axis_size("bn") * lax.axis_size("grp")
-    scaled = [piece / images_total for piece in window_sums]
+    pieces = (
+        grad_expand,
+        grad_gain_expand,
+        grad_shift_expand,
+        grad_depth,
+        grad_gain_depth,
+        grad_shift_depth,
+        grad_reduce,
+        grad_b_reduce,
+        grad_restore,
+        grad_b_restore,
+        grad_project,
+        grad_gain_project,
+    )
+    flat = jnp.concatenate([piece.reshape(-1) for piece in pieces])
+    flat, upper_summed = lax.optimization_barrier((flat, upper_summed))
+    flat = lax.psum(flat, AXES)
+    images_total = images.shape[0] * lax.axis_size(AXES)
+    flat = flat / images_total
+    scaled = []
+    start = 0
+    for piece in pieces:
+        scaled.append(flat[start : start + piece.size].reshape(piece.shape))
+        start += piece.size
     return (
         input_grad[None],
         scaled[0],
@@ -207,28 +263,29 @@
 
 
 def solution(mesh):
+    chips = Mesh(mesh.devices.reshape(4, 8, 8, 2), AXES)
     return jax.shard_map(
         per_device,
-        mesh=mesh,
+        mesh=chips,
         in_specs=(
-            P("grp", "bn", None, None, None),
-            P("grp", "bn", None, None, None),
-            P(),
-            P(),
-            P(),
-            P(),
-            P(),
-            P(),
-            P(),
-            P(),
-            P(),
-            P(),
-            P(),
-            P(),
-            P(("bn", "grp"), None),
+            P(("z", "core"), GROUP, None, None, None),
+            P(("z", "core"), GROUP, None, None, None),
+            P(),
+            P(),
+            P(),
+            P(),
+            P(),
+            P(),
+            P(),
+            P(),
+            P(),
+            P(),
+            P(),
+            P(),
+            P(AXES, None),
         ),
         out_specs=(
-            P("grp", "bn", None, None, None),
+            P(("z", "core"), GROUP, None, None, None),
             P(),
             P(),
             P(),

time: 1250 us -> 861 us (0.69)
  blocking collectives: 882 us -> 35.1 us
  waiting for transfers between devices: 171 us -> 539 us
  starting transfers between devices: 0.04 us -> 61.2 us
  local copies, waits for them, and re-layouts: 10.5 us -> 58.2 us
  other arithmetic: 155 us -> 131 us
    psum x10 -> x2, blocking collectives: 882 us -> 35.1 us  [per_device(): sums = lax.psum(sums, axis)]
    psum x1 -> x2, waiting for transfers between devices: 171 us -> 370 us  [the longest x1 278 us: per_device(): flat = lax.psum(flat, AXES)]
    unnamed x1 -> x4, waiting for transfers between devices: 0.02 us -> 153 us
    ppermute x0 -> x15, starting transfers between devices: none -> 50.6 us  [the longest x10 34.5 us: ring_parts(): lax.ppermute(vector, axis, [(i, (i + step) % size) for i in range(size)])]
    concatenate x0 -> x1, local copies, waits for them, and re-layouts: none -> 27.8 us  [per_device(): flat = jnp.concatenate([piece.reshape(-1) for piece in pieces])]
    div x20 -> x14, other arithmetic: 14.6 us -> 1.89 us  [the longest x1 1.68 us: per_device(): flat = flat / images_total]
    reduce_sum x7 -> x15, other arithmetic: 93.8 us -> 87 us  [the longest x1 59.3 us: per_device(): grad_shift_expand = jnp.sum(grad_act_one, axis=(0, 1, 2))]
  transfers between devices with their start and end apart: 1 -> 19, of which waited for: 1 -> 9; matrix products, arithmetic and copies ran while one was open for 1% -> 16% of each run, Pallas kernels for 0% -> 0%
where the time goes in v1:
time: 861 us; the launch traced here: 858 us
  waiting for transfers between devices  539 us (63%)
  other arithmetic  131 us (15%)
  starting transfers between devices  61.2 us (7%)
  local copies, waits for them, and re-layouts  58.2 us (7%)
  blocking collectives  35.1 us (4%)
  between operations  18.1 us (2%)
  matrix products  15.6 us (2%)
    psum x1, waiting for transfers between devices, per_device(): flat = lax.psum(flat, AXES)  278 us
    unnamed x4, waiting for transfers between devices  153 us
    psum x1, waiting for transfers between devices, per_device(): upper_summed = lax.psum(upper_grads[0], AXES)  92.2 us
    reduce_sum x1, other arithmetic, per_device(): grad_shift_expand = jnp.sum(grad_act_one, axis=(0, 1, 2))  59.3 us
    psum x2, blocking collectives, per_device(): sums = lax.psum(sums, axis)  35.1 us
    ppermute x10, starting transfers between devices, ring_parts(): lax.ppermute(vector, axis, [(i, (i + step) % size) for i in range(size)])  34.5 us
    concatenate x1, local copies, waits for them, and re-layouts, per_device(): flat = jnp.concatenate([piece.reshape(-1) for piece in pieces])  27.8 us
    reduce_sum x2, other arithmetic, depth_kernel_grad(): columns.append(jnp.sum(window * grad_out, axis=(0, 1, 2)))  24.2 us
  transfers between devices with their start and end apart: 19, of which 9 were waited for; matrix products, arithmetic and copies ran while one was open for 16% of the time, Pallas kernels for 0%

profile of v1, /device:TPU:1, one launch (start us, length us, event | category | flops | bytes accessed | tf_op | source)
XLA Modules:
  0.0 858.3 jit_solution(1347170349636362425)
XLA Ops:
  13.3 10.5 %all-to-all-start = ((f32[32,2,1056]{2,1,0:T(2,128)}), f32[32,2,1056]{2,1,0:T(2,128)S(1)}, u32[]{:S(2)}, u32[]{:S(2)}) async-start(f32[32,2,1056]{2,1,0:T(2,128)} %broadcast_in_dim.4), calls=%async_computation | async-start | bytes 589824 | tf_op jit(solution)/shard_map/all_to_all | solution.py:85
  26.4 7.4 all-to-all-done
  34.8 3.9 fusion.179
  38.9 19.3 %fusion.161 = (f32[1056]{0:T(1024)S(1)}, f32[1,29,29,1056]{3,2,1,0:T(8,128)}) fusion(f32[1056]{0:T(1024)S(1)} %get-tuple-element.114, f32[1056]{0:T(1024)S(1)} %get-tuple-element.115, f32[1056]{0:T(1024)S(1)} %get-tuple-element.92, f32[1056]{0:T(1024)S(1)} %get-tuple-element.93, f32[1056]{0:T(1024)S(1)} %get-tuple-element.94, ...), kind=kLoop, calls=%fused_computation.354 | loop fusion | flops 74599008 | bytes 9007680 | tf_op jit(solution)/shard_map/reduce_sum | solution.py:72
  62.3 153.2 %all-reduce.11.cloned.1.call-done = f32[67584]{0:T(1024)} async-done(((f32[67584]{0:T(1024)}), f32[67584]{0:T(1024)}) %all-reduce.11.cloned.1.call-update) | async-done | bytes 270352
  217.3 3.7 convert_reduce_fusion
  227.4 4.2 collective-permute-start.1
  241.9 4.4 collective-permute-start.5
  246.3 3.8 collective-permute-start.6
  250.1 5.2 collective-permute-start.7
  255.3 3.9 collective-permute-start.8
  269.1 4.1 fusion.159
  285.8 3.5 convolution_bitcast_fusion
  289.3 4.3 collective-permute-start.13
  295.0 4.4 collective-permute-start.14
  304.4 17.9 %fusion.50 = (f32[1056]{0:T(1024)S(1)}, f32[1056]{0:T(1024)S(1)}, f32[1056]{0:T(1024)S(1)}, f32[1056]{0:T(1024)S(1)}, f32[1056]{0:T(1024)S(1)}, /*index=5*/f32[1...) fusion(bf16[1,29,29,1056]{3,2,1,0:T(8,128)(2,1)S(1)} %fusion.17, ...), kind=kLoop, calls=%fused_computation.151 | loop fusion | flops 53266752 | bytes 12530496 | tf_op jit(solution)/shard_map/reduce_sum | solution.py:59
  324.5 6.3 fusion.29
  331.1 59.3 %fusion.158 = (f32[1056]{0:T(1024)S(1)}, f32[1056]{0:T(1024)S(1)}, f32[1,29,29,1056]{3,2,1,0:T(8,128)}) fusion(f32[1056]{0:T(1024)S(1)} %get-tuple-element.150, f32[29,29,1056]{2,1,0:T(8,128)} %copy-done.1, f32[1056]{0:T(1024)S(1)} %broadcast_multiply_fusion.4, f32[1056]{0:T(1024)S(1)} %copy-done.18, f32[1056]{0:T(1024)S(1)} %copy-done.14, ...), kind=kLoop, calls=%fused_computation.352 | loop fusion | flops 56836032 | bytes 10788096 | tf_op jit(solution)/shard_map/reduce_sum | solution.py:206
  391.8 12.6 %psum.28 = f32[2112]{0:T(1024)S(1)} all-reduce(f32[2112]{0:T(1024)S(1)} %pad_maximum_fusion.2), channel_id=1, replica_groups=mesh['x'=4,'y'=8,'z'=8,'core'=2] {'x'}, use_global_device_ids=true, to_apply=%region_26.27 | all-reduce | flops 2112 | bytes 16896 | tf_op jit(solution)/shard_map/psum | solution.py:210
  404.4 22.6 %psum.29 = f32[2112]{0:T(1024)S(1)} all-reduce(f32[2112]{0:T(1024)S(1)} %psum.28), channel_id=1, replica_groups=mesh['x'=4,'y'=8,'z'=8,'core'=2] {'y'}, use_global_device_ids=true, to_apply=%region_27.28 | all-reduce | flops 2112 | bytes 16896 | tf_op jit(solution)/shard_map/psum | solution.py:210
  427.1 5.9 fusion.103
  439.1 27.8 %concatenate.15 = f32[496540]{0:T(1024)} concatenate(f32[185856]{0:T(1024)} %reshape.598, f32[1056]{0:T(1024)} %copy-done.35, f32[1056]{0:T(1024)} %copy-done.34, f32[26400]{0:T(1024)} %reshape.599, f32[1056]{0:T(1024)} %copy-done.16, f32[1056]{0:T(1024)S(1)} %get-tuple-element.87, f32[46464]{0:T(1024)S(1)} %copy-done.12, f32[44]{0:T(128)S(1)} %copy-done.79, f32[46464]{0:T(1024)} %reshape.601, ...), dimensions={0} | concatenate | bytes 3972320 | tf_op jit(solution)/shard_map/concatenate | solution.py:237
  466.9 92.2 %all-reduce.7.cloned.1.call-done = f32[131072]{0:T(1024)} async-done(((f32[131072]{0:T(1024)}), f32[131072]{0:T(1024)}) %all-reduce.7.cloned.1.call-update) | async-done | bytes 524304 | tf_op jit(solution)/shard_map/psum | solution.py:128
  561.7 277.5 %all-reduce.9.cloned.1.call-done = f32[496540]{0:T(1024)} async-done(((f32[496540]{0:T(1024)}), f32[496540]{0:T(1024)}) %all-reduce.9.cloned.1.call-update) | async-done | bytes 1986176 | tf_op jit(solution)/shard_map/psum | solution.py:239
  (332 shorter events, 82.3 us)
Async XLA Ops:
  8.0 215.1 %copy-start = (bf16[1056,176]{0,1:T(8,128)(2,1)S(1)}, bf16[1056,176]{0,1:T(8,128)(2,1)}, u32[]{:S(2)}) copy-start(bf16[1056,176]{0,1:T(8,128)(2,1)} %param.27) | copy-start | bytes 1115140
  13.3 20.5 %all-to-all-start = ((f32[32,2,1056]{2,1,0:T(2,128)}), f32[32,2,1056]{2,1,0:T(2,128)S(1)}, u32[]{:S(2)}, u32[]{:S(2)}) async-start(f32[32,2,1056]{2,1,0:T(2,128)} %broadcast_in_dim.4), calls=%async_computation | async-start | bytes 589824 | tf_op jit(solution)/shard_map/all_to_all | solution.py:85
  23.9 191.6 %all-reduce.11.cloned.1.call-start = ((), (), s32[]{:S(2)}) async-start(), calls=%async_computation.3 | async-start | bytes 540672
  58.3 159.1 %copy-start.74 = (f32[1056]{0:T(1024)S(1)}, f32[1056]{0:T(1024)}, u32[]{:S(2)}) copy-start(f32[1056]{0:T(1024)} %param.22) | copy-start | bytes 12676
  61.1 160.0 %copy-start.82 = (f32[44]{0:T(128)S(1)}, f32[44]{0:T(128)}, u32[]{:S(2)}) copy-start(f32[44]{0:T(128)} %param.24) | copy-start | bytes 532
  61.1 161.8 %copy-start.19 = (bf16[44,1056]{1,0:T(8,128)(2,1)S(1)}, bf16[44,1056]{1,0:T(8,128)(2,1)}, u32[]{:S(2)}) copy-start(bf16[44,1056]{1,0:T(8,128)(2,1)} %param.25) | copy-start | bytes 278788
  61.3 161.8 %copy-start.77 = (f32[1056]{0:T(1024)S(1)}, f32[1056]{0:T(1024)}, u32[]{:S(2)}) copy-start(f32[1056]{0:T(1024)} %param.26) | copy-start | bytes 12676
  62.1 497.0 %all-reduce.7.cloned.1.call-start = ((), (), s32[]{:S(2)}) async-start(), calls=%async_computation.1 | async-start | bytes 1048576 | tf_op jit(solution)/shard_map/psum | solution.py:128
  225.3 8.9 %collective-permute-start = (f32[4,176]{1,0:T(4,128)S(1)}, f32[4,176]{1,0:T(4,128)S(1)}, u32[]{:S(2)}, u32[]{:S(2)}) collective-permute-start(f32[4,176]{1,0:T(4,128)S(1)} %get-tuple-element.156), channel_id=1, source_target_pairs={{0,128},{128,256},{256,384},{384,0},{1,129},{129,257},{257,385},{3... | collective-permute-start | bytes 8456 | tf_op jit(solution)/shard_map/ppermute | solution.py:91
  227.4 6.9 collective-permute-start.1
  231.6 4.4 collective-permute-start.2
  236.1 19.2 %collective-permute-start.3 = (f32[4,176]{1,0:T(4,128)S(1)}, f32[4,176]{1,0:T(4,128)S(1)}, u32[]{:S(2)}, u32[]{:S(2)}) collective-permute-start(f32[4,176]{1,0:T(4,128)S(1)} %get-tuple-element.153), channel_id=1, source_target_pairs={{0,16},{16,32},{32,48},{48,64},{64,80},{80,96},{96,112},{112,0},{1... | collective-permute-start | bytes 8456 | tf_op jit(solution)/shard_map/ppermute | solution.py:91
  238.7 20.5 %collective-permute-start.4 = (f32[4,176]{1,0:T(4,128)S(1)}, f32[4,176]{1,0:T(4,128)S(1)}, u32[]{:S(2)}, u32[]{:S(2)}) collective-permute-start(f32[4,176]{1,0:T(4,128)S(1)} %get-tuple-element.153), channel_id=1, source_target_pairs={{0,32},{16,48},{32,64},{48,80},{64,96},{80,112},{96,0},{112,16},{1... | collective-permute-start | bytes 8456 | tf_op jit(solution)/shard_map/ppermute | solution.py:91
  241.9 19.9 %collective-permute-start.5 = (f32[4,176]{1,0:T(4,128)S(1)}, f32[4,176]{1,0:T(4,128)S(1)}, u32[]{:S(2)}, u32[]{:S(2)}) collective-permute-start(f32[4,176]{1,0:T(4,128)S(1)} %get-tuple-element.153), channel_id=1, source_target_pairs={{0,48},{16,64},{32,80},{48,96},{64,112},{80,0},{96,16},{112,32},{1... | collective-permute-start | bytes 8456 | tf_op jit(solution)/shard_map/ppermute | solution.py:91
  246.3 15.5 %collective-permute-start.6 = (f32[4,176]{1,0:T(4,128)S(1)}, f32[4,176]{1,0:T(4,128)S(1)}, u32[]{:S(2)}, u32[]{:S(2)}) collective-permute-start(f32[4,176]{1,0:T(4,128)S(1)} %get-tuple-element.153), channel_id=1, source_target_pairs={{0,64},{16,80},{32,96},{48,112},{64,0},{80,16},{96,32},{112,48},{1... | collective-permute-start | bytes 8456 | tf_op jit(solution)/shard_map/ppermute | solution.py:91
  250.1 11.7 %collective-permute-start.7 = (f32[4,176]{1,0:T(4,128)S(1)}, f32[4,176]{1,0:T(4,128)S(1)}, u32[]{:S(2)}, u32[]{:S(2)}) collective-permute-start(f32[4,176]{1,0:T(4,128)S(1)} %get-tuple-element.153), channel_id=1, source_target_pairs={{0,80},{16,96},{32,112},{48,0},{64,16},{80,32},{96,48},{112,64},{1... | collective-permute-start | bytes 8456 | tf_op jit(solution)/shard_map/ppermute | solution.py:91
  255.3 6.5 collective-permute-start.8
  259.2 4.4 collective-permute-start.9
  273.3 4.4 collective-permute-start.10
  277.8 5.9 collective-permute-start.11
  281.3 557.9 %all-reduce.9.cloned.1.call-start = ((), (), s32[]{:S(2)}) async-start(), calls=%async_computation.2 | async-start | bytes 3973120 | tf_op jit(solution)/shard_map/psum | solution.py:239
  283.8 5.6 collective-permute-start.12
  289.3 5.6 collective-permute-start.13
  295.0 9.3 %collective-permute-start.14 = (f32[2112]{0:T(1024)S(1)}, f32[2112]{0:T(1024)S(1)}, u32[]{:S(2)}, u32[]{:S(2)}) collective-permute-start(f32[2112]{0:T(1024)S(1)} %add.339), channel_id=1, source_target_pairs={{0,64},{16,80},{32,96},{48,112},{64,0},{80,16},{96,32},{112,48},{1... | collective-permute-start | bytes 25352 | tf_op jit(solution)/shard_map/ppermute | solution.py:101
  (82 other events, 1428.0 us)
Sparse Core Ops, SparseCore 0:
  62.2 153.2 all-reduce.10
Sparse Core Ops, SparseCore 1:
  281.4 277.6 all-reduce.6
  564.6 274.5 all-reduce.8

commit v2 on v0

v2 whole, which is shorter than its diff:
```python
import functools

import jax
import jax.numpy as jnp
from jax import lax
from jax.experimental import pallas as pl
from jax.experimental.pallas import tpu as pltpu
from jax.sharding import Mesh, PartitionSpec as P

KER = 5
EPSILON = 0.001
SHAPE = (4, 8, 8, 2)
AXES = ("x", "y", "z", "core")
GROUP = ("x", "y")
PLANE = ("x", "y", "core")
SIDE = 29
WIDE = 32
ROWS = SIDE * WIDE
HALO = (SIDE + KER - 1) * WIDE
C = 176
HID = 1056
LANES = 128
CHUNKS = 9
PADDED = CHUNKS * LANES
SE = 44
SE_ROWS = 48
SPOTS = SIDE * SIDE
GAIN_ONE, SHIFT_ONE, GAIN_TWO, SHIFT_TWO, BIAS = 25, 26, 27, 28, 29
TABLE = 32
EARLY = C + 2 * SE_ROWS
EARLY_ROWS = 2560
LATE = C + TABLE
LATE_ROWS = 2048
F32 = jnp.float32
BF16 = jnp.bfloat16


def dot(left, right, left_dim=1, right_dim=0):
    return lax.dot_general(
        left, right, (((left_dim,), (right_dim,)), ((), ())), preferred_element_type=F32
    )


def logistic(values):
    return 0.5 + 0.5 * jnp.tanh(0.5 * values)


def valid_mask(lanes=LANES):
    return lax.broadcasted_iota(jnp.int32, (WIDE, lanes), 0) < SIDE


def row_at(index):
    return pl.ds(pl.multiple_of(index * WIDE, WIDE), WIDE)


def each_row(body, init, unroll=1):
    return lax.fori_loop(0, SIDE, body, init, unroll=unroll)


def col_sum(values):
    return jnp.sum(values, axis=0, keepdims=True)


def zeros(lanes=LANES):
    return jnp.zeros((WIDE, lanes), F32)


def share(pair, ref):
    ref[...] = jnp.broadcast_to(pair[None], ref.shape)


def pair_rows(first, second):
    return jnp.where(lax.broadcasted_iota(jnp.int32, (2, first.shape[1]), 0) == 0, first, second)


def spread_of(ref, mean, mask):
    def body(i, acc):
        dev = jnp.where(mask, ref[row_at(i), :] - mean, 0.0)
        return acc + dev * dev

    return col_sum(each_row(body, zeros(mean.shape[1]))) / SPOTS


def merged(gathered):
    peers = gathered.shape[0]
    total = jnp.sum(gathered, axis=0)
    center = total[0:1] / peers
    dev = jnp.sum(jnp.square(gathered[:, 0:1, :] - center[None]), axis=0)
    spread = (total[1:2] + dev) / peers
    return center, lax.rsqrt(spread + EPSILON)


def widen(map_ref, flat_ref, line_ref):
    line_ref[...] = jnp.zeros_like(line_ref)
    for i in range(SIDE):
        line_ref[i % 2, 0:SIDE, :] = map_ref[i].astype(F32)
        flat_ref[i * WIDE : (i + 1) * WIDE, :] = line_ref[i % 2].astype(BF16)


def stats_kernel(x_ref, w_ref, xpad_ref, stat_ref, pre_ref, line_ref):
    @pl.when(pl.program_id(0) == 0)
    def _():
        widen(x_ref, xpad_ref, line_ref)

    pre_ref[...] = dot(xpad_ref[...], w_ref[...])
    total = each_row(lambda i, acc: acc + pre_ref[row_at(i), :], zeros())
    mean = col_sum(total) / SPOTS
    share(pair_rows(mean, spread_of(pre_ref, mean, valid_mask())), stat_ref)


def slide(parts, sign):
    out = parts[2]
    for b in (0, 1, 3, 4):
        out = out + pltpu.roll(parts[b], (sign * (2 - b)) % WIDE, 0)
    return out


def row_taps(halo_ref, taps, i, flip):
    parts = [None] * KER
    for a in range(KER):
        source = halo_ref[row_at(i + a), :].reshape(WIDE // 8, 8, LANES)
        for b in range(KER):
            term = source * taps[((KER - 1 - a) if flip else a) * KER + b]
            parts[b] = term if parts[b] is None else parts[b] + term
    return slide([part.reshape(WIDE, LANES) for part in parts], -1 if flip else 1)


def clear_halo(ref):
    edge = jnp.zeros((2 * WIDE, LANES), F32)
    ref[0 : 2 * WIDE, :] = edge
    ref[HALO - 2 * WIDE : HALO, :] = edge


def tap_rows(table_ref):
    return [jnp.broadcast_to(table_ref[k : k + 1, :], (8, LANES)) for k in range(KER * KER)]


def forward_kernel(
    xpad_ref, w_ref, gathered_ref, table_ref, depth_ref, stat_ref, moment_ref, pre_ref, halo_ref
):
    @pl.when(pl.program_id(0) == 0)
    def _():
        clear_halo(halo_ref)

    mask = valid_mask()
    center, scale = merged(gathered_ref[...])
    moment_ref[0:1, :] = center
    moment_ref[1:2, :] = scale
    slope = scale * table_ref[GAIN_ONE : GAIN_ONE + 1, :]
    offset = table_ref[SHIFT_ONE : SHIFT_ONE + 1, :] - center * slope
    pre_ref[...] = dot(xpad_ref[...], w_ref[...])

    def activate(i, _):
        act = pre_ref[row_at(i), :] * slope + offset
        silu = (act * logistic(act)).astype(BF16).astype(F32)
        halo_ref[row_at(i + 2), :] = jnp.where(mask, silu, 0.0)
        return 0

    each_row(activate, 0)
    taps = tap_rows(table_ref)

    def filter_row(i, acc):
        out = jnp.where(mask, row_taps(halo_ref, taps, i, False), 0.0)
        depth_ref[row_at(i), :] = out
        return acc + out

    mean = col_sum(each_row(filter_row, zeros())) / SPOTS
    share(pair_rows(mean, spread_of(depth_ref, mean, mask)), stat_ref)


def lanes_at(index):
    return pl.ds(pl.multiple_of(index * LANES, LANES), LANES)


def project_kernel(
    depth_ref,
    gathered_ref,
    table_ref,
    wproject_ref,
    cot_ref,
    wreduce_ref,
    wrestore_ref,
    breduce_ref,
    brestore_ref,
    moment_ref,
    project_ref,
    cpad_ref,
    vector_ref,
    column_ref,
    stat_ref,
    act_ref,
    hidden_ref,
    line_ref,
):
    step = pl.program_id(0)
    mask = valid_mask()
    center, scale = merged(gathered_ref[...])
    moment_ref[0:1, :] = center
    moment_ref[1:2, :] = scale
    slope = scale * table_ref[GAIN_TWO : GAIN_TWO + 1, :]
    offset = table_ref[SHIFT_TWO : SHIFT_TWO + 1, :] - center * slope

    def activate(i, acc):
        act = depth_ref[row_at(i), :] * slope + offset
        silu = jnp.where(mask, act * logistic(act), 0.0).astype(BF16)
        act_ref[step, row_at(i), :] = silu
        return acc + silu.astype(F32)

    vector_ref[0:1, lanes_at(step)] = col_sum(each_row(activate, zeros())) / SPOTS

    @pl.when(step == 0)
    def _():
        widen(cot_ref, cpad_ref, line_ref)

    @pl.when(step == CHUNKS - 1)
    def _():
        pooled = vector_ref[0:1, :]
        logit = jnp.sum(wreduce_ref[...] * pooled, axis=1, keepdims=True) + breduce_ref[...]
        squeezed = logit * logistic(logit)
        column_ref[0] = logit
        column_ref[1] = squeezed
        restored = col_sum(wrestore_ref[...] * squeezed[:, 0:1]) + brestore_ref[...]
        vector_ref[1:2, :] = logistic(restored)

        def project(c, _):
            excite = vector_ref[1:2, lanes_at(c)]

            def scale_row(i, _):
                hidden_ref[row_at(i), :] = (
                    act_ref[c, row_at(i), :].astype(F32) * excite
                ).astype(BF16)
                return 0

            each_row(scale_row, 0)
            part = dot(hidden_ref[...], wproject_ref[:, lanes_at(c)], 1, 1)

            @pl.when(c == 0)
            def _():
                project_ref[...] = part

            @pl.when(c > 0)
            def _():
                project_ref[...] += part

            return 0

        lax.fori_loop(0, CHUNKS, project, 0)

        def sums(i, accs):
            values, incoming = project_ref[row_at(i), :], cpad_ref[row_at(i), :].astype(F32)
            return accs[0] + values, accs[1] + incoming

        total, cot_total = each_row(sums, (zeros(C), zeros(C)))
        mean = col_sum(total) / SPOTS

        def devs(i, accs):
            dev = jnp.where(valid_mask(C), project_ref[row_at(i), :] - mean, 0.0)
            incoming = cpad_ref[row_at(i), :].astype(F32)
            return accs[0] + dev * dev, accs[1] + incoming * dev

        square, cross = each_row(devs, (zeros(C), zeros(C)))
        row = lax.broadcasted_iota(jnp.int32, (4, C), 0)
        packed = jnp.where(
            row == 0,
            mean,
            jnp.where(
                row == 1,
                col_sum(square) / SPOTS,
                jnp.where(row == 2, col_sum(cot_total), col_sum(cross)),
            ),
        )
        share(packed, stat_ref)


def back_project_kernel(
    depth_ref,
    gathered_ref,
    table_ref,
    moment_ref,
    project_ref,
    cpad_ref,
    gain_ref,
    wproject_ref,
    vector_ref,
    column_ref,
    wreduce_ref,
    wrestore_ref,
    first_ref,
    slope_ref,
    grads_ref,
    pooled_ref,
    stat_ref,
    gpp_ref,
    hidden_ref,
    back_ref,
    sums_ref,
    gain_sum_ref,
):
    step = pl.program_id(0)
    mask = valid_mask()

    @pl.when(step == 0)
    def _():
        gathered = gathered_ref[...]
        peers = gathered.shape[0]
        count = peers * SPOTS
        total = jnp.sum(gathered, axis=0)
        center3 = total[0:1] / peers
        away = gathered[:, 0:1, :] - center3[None]
        spread = (total[1:2] + jnp.sum(jnp.square(away), axis=0)) / peers
        scale3 = lax.rsqrt(spread + EPSILON)
        cross = total[3:4] + jnp.sum(gathered[:, 2:3, :] * away, axis=0)
        first = total[2:3] / count
        second = cross * scale3 / count
        factor = scale3 * gain_ref[...]
        wide = valid_mask(C)

        def body(i, acc):
            normed = (project_ref[row_at(i), :] - center3) * scale3
            incoming = cpad_ref[row_at(i), :].astype(F32)
            grad = factor * (incoming - first - normed * second)
            gpp_ref[row_at(i), :] = jnp.where(wide, grad, 0.0).astype(BF16)
            return acc + incoming * normed

        gain_sum_ref[...] = jnp.zeros_like(gain_sum_ref)
        gain_sum_ref[0:1, 0:C] = col_sum(each_row(body, zeros(C)))
        grads_ref[CHUNKS * EARLY :, :] = jnp.zeros((EARLY_ROWS - CHUNKS * EARLY, LANES), F32)

    center, scale = moment_ref[0:1, :], moment_ref[1:2, :]
    gain = table_ref[GAIN_TWO : GAIN_TWO + 1, :]
    shift = table_ref[SHIFT_TWO : SHIFT_TWO + 1, :]
    excite = vector_ref[1:2, lanes_at(step)]
    back_ref[...] = dot(gpp_ref[...], wproject_ref[...])

    def body(i, accs):
        normed = (depth_ref[row_at(i), :] - center) * scale
        act = normed * gain + shift
        sig = logistic(act)
        silu = (act * sig).astype(BF16).astype(F32)
        slope = jnp.where(mask, sig * (1.0 + act * (1.0 - sig)), 0.0)
        hidden_ref[row_at(i), :] = jnp.where(mask, silu * excite, 0.0).astype(BF16)
        back = back_ref[row_at(i), :]
        first = back * slope
        first_ref[row_at(i), :] = first
        slope_ref[row_at(i), :] = slope
        return (
            accs[0] + back * silu,
            accs[1] + first,
            accs[2] + first * normed,
            accs[3] + slope,
            accs[4] + slope * normed,
        )

    totals = each_row(body, tuple(zeros() for _ in range(5)))
    for k in range(5):
        sums_ref[k : k + 1, lanes_at(step)] = col_sum(totals[k])
    base = pl.multiple_of(step * EARLY, 16)
    grads_ref[pl.ds(base, C), :] = dot(gpp_ref[...], hidden_ref[...], 0, 0)

    @pl.when(step == CHUNKS - 1)
    def _():
        pooled, excite = vector_ref[0:1, :], vector_ref[1:2, :]
        logit, squeezed = column_ref[0], column_ref[1]
        grad_logit = sums_ref[0:1, :] * excite * (1.0 - excite)
        grad_squeezed = jnp.sum(wrestore_ref[...] * grad_logit, axis=1, keepdims=True)
        sig = logistic(logit)
        grad_reduce = grad_squeezed * (sig * (1.0 + logit * (1.0 - sig)))
        grad_pooled = col_sum(wreduce_ref[...] * grad_reduce[:, 0:1]) / SPOTS
        pooled_ref[0:1, :] = grad_pooled
        shift_sum = excite * sums_ref[1:2, :] + grad_pooled * sums_ref[3:4, :]
        gain_sum = excite * sums_ref[2:3, :] + grad_pooled * sums_ref[4:5, :]
        share(pair_rows(shift_sum, gain_sum), stat_ref)
        lane = lax.broadcasted_iota(jnp.int32, (SE_ROWS, LANES), 1)
        row = lax.broadcasted_iota(jnp.int32, (SE_ROWS, LANES), 0)
        bias_row = col_sum(jnp.where(lane == row, grad_reduce, 0.0))
        for c in range(CHUNKS):
            cut = slice(c * LANES, (c + 1) * LANES)
            block = squeezed * grad_logit[:, cut]
            block = jnp.where(row == SE, grad_logit[:, cut], block)
            block = jnp.where(row == SE + 1, shift_sum[:, cut], block)
            block = jnp.where(row == SE + 2, gain_sum[:, cut], block)
            extra = gain_sum_ref[0:1, cut] if c < 2 else bias_row
            block = jnp.where(row == SE + 3, extra, block)
            grads_ref[c * EARLY + C : c * EARLY + C + SE_ROWS, :] = block
            grads_ref[c * EARLY + C + SE_ROWS : (c + 1) * EARLY, :] = grad_reduce * pooled[:, cut]


def back_depth_kernel(
    depth_ref,
    first_ref,
    slope_ref,
    gathered_ref,
    table_ref,
    moment_two_ref,
    moment_one_ref,
    vector_ref,
    pooled_ref,
    xpad_ref,
    w_ref,
    grad_ref,
    stat_ref,
    sums_ref,
    pre_ref,
    halo_ref,
    ghalo_ref,
    side_ref,
):
    @pl.when(pl.program_id(0) == 0)
    def _():
        clear_halo(halo_ref)
        clear_halo(ghalo_ref)

    mask = valid_mask()
    total = jnp.sum(gathered_ref[...], axis=0)
    gain = table_ref[GAIN_TWO : GAIN_TWO + 1, :]
    count = gathered_ref.shape[0] * SPOTS
    mean_first = gain * total[0:1] / count
    mean_second = gain * total[1:2] / count
    center, scale = moment_two_ref[0:1, :], moment_two_ref[1:2, :]
    excite = vector_ref[1:2, :] * gain
    pooled = pooled_ref[0:1, :] * gain
    center_one, scale_one = moment_one_ref[0:1, :], moment_one_ref[1:2, :]
    slope_one = scale_one * table_ref[GAIN_ONE : GAIN_ONE + 1, :]
    offset_one = table_ref[SHIFT_ONE : SHIFT_ONE + 1, :] - center_one * slope_one
    pre_ref[...] = dot(xpad_ref[...], w_ref[...])

    def prepare(i, _):
        normed = (depth_ref[row_at(i), :] - center) * scale
        grad = first_ref[row_at(i), :] * excite + slope_ref[row_at(i), :] * pooled
        grad = scale * (grad - mean_first - normed * mean_second)
        ghalo_ref[row_at(i + 2), :] = jnp.where(mask, grad, 0.0)
        act = pre_ref[row_at(i), :] * slope_one + offset_one
        sig = logistic(act)
        silu = (act * sig).astype(BF16).astype(F32)
        halo_ref[row_at(i + 2), :] = jnp.where(mask, silu, 0.0)
        side_ref[row_at(i), :] = jnp.where(mask, sig * (1.0 + act * (1.0 - sig)), 0.0)
        return 0

    each_row(prepare, 0)

    def kernel_grad(i, accs):
        grad = ghalo_ref[row_at(i + 2), :]
        shifted = [
            (grad if b == 2 else pltpu.roll(grad, (b - 2) % WIDE, 0)).reshape(
                WIDE // 8, 8, LANES
            )
            for b in range(KER)
        ]
        accs = list(accs)
        for a in range(KER):
            field = halo_ref[row_at(i + a), :].reshape(WIDE // 8, 8, LANES)
            for b in range(KER):
                accs[a * KER + b] = accs[a * KER + b] + jnp.sum(field * shifted[b], axis=0)
        return tuple(accs)

    start = tuple(jnp.zeros((8, LANES), F32) for _ in range(KER * KER))
    accs = each_row(kernel_grad, start)
    for k in range(KER * KER):
        sums_ref[k : k + 1, :] = col_sum(accs[k])
    taps = tap_rows(table_ref)

    def input_grad(i, accs):
        grad = row_taps(ghalo_ref, taps, i, True) * side_ref[row_at(i), :]
        grad_ref[row_at(i), :] = grad
        normed = (pre_ref[row_at(i), :] - center_one) * scale_one
        return accs[0] + grad, accs[1] + grad * normed

    shift_sum, gain_sum = (col_sum(a) for a in each_row(input_grad, (zeros(), zeros())))
    share(pair_rows(shift_sum, gain_sum), stat_ref)
    sums_ref[KER * KER : TABLE, :] = jnp.zeros((TABLE - KER * KER, LANES), F32)
    sums_ref[25:26, :] = shift_sum
    sums_ref[26:27, :] = gain_sum


def back_expand_kernel(
    grad_ref,
    gathered_ref,
    table_ref,
    moment_ref,
    xpad_ref,
    w_ref,
    sums_ref,
    cpad_ref,
    out_ref,
    grads_ref,
    pre_ref,
    gpe_ref,
    acc_ref,
):
    step = pl.program_id(0)
    mask = valid_mask()
    total = jnp.sum(gathered_ref[...], axis=0)
    count = gathered_ref.shape[0] * SPOTS
    mean_first, mean_second = total[0:1] / count, total[1:2] / count
    center, scale = moment_ref[0:1, :], moment_ref[1:2, :]
    factor = scale * table_ref[GAIN_ONE : GAIN_ONE + 1, :]
    pre_ref[...] = dot(xpad_ref[...], w_ref[...])

    def body(i, _):
        normed = (pre_ref[row_at(i), :] - center) * scale
        grad = factor * (grad_ref[row_at(i), :] - mean_first - normed * mean_second)
        gpe_ref[row_at(i), :] = jnp.where(mask, grad, 0.0).astype(BF16)
        return 0

    each_row(body, 0)
    base = pl.multiple_of(step * LATE, 16)
    grads_ref[pl.ds(base, C), :] = dot(xpad_ref[...], gpe_ref[...], 0, 0)
    grads_ref[pl.ds(pl.multiple_of(base + C, 16), TABLE), :] = sums_ref[...]
    part = dot(gpe_ref[...], w_ref[...], 1, 1)

    @pl.when(step == 0)
    def _():
        acc_ref[...] = cpad_ref[...].astype(F32) + part
        grads_ref[CHUNKS * LATE :, :] = jnp.zeros((LATE_ROWS - CHUNKS * LATE, LANES), F32)

    @pl.when(step > 0)
    def _():
        acc_ref[...] += part

    @pl.when(step == CHUNKS - 1)
    def _():
        for i in range(SIDE):
            out_ref[i] = acc_ref[i * WIDE : i * WIDE + SIDE, :].astype(BF16)


def put_row(ref, rows_ref, row, height, scale):
    for c in range(-(-ref.shape[1] // LANES)):
        width = min(LANES, ref.shape[1] - c * LANES)
        at = c * height + row
        ref[:, c * LANES : c * LANES + width] = rows_ref[at : at + ref.shape[0], 0:width] * scale


def unpack_early_kernel(
    scale, rows_ref, project_ref, restore_ref, reduce_ref, brestore_ref, shift_ref, gain_ref,
    gproject_ref, breduce_ref,
):
    put_row(project_ref, rows_ref, 0, EARLY, scale)
    put_row(restore_ref, rows_ref, C, EARLY, scale)
    put_row(reduce_ref, rows_ref, C + SE_ROWS, EARLY, scale)
    put_row(brestore_ref, rows_ref, C + SE, EARLY, scale)
    put_row(shift_ref, rows_ref, C + SE + 1, EARLY, scale)
    put_row(gain_ref, rows_ref, C + SE + 2, EARLY, scale)
    put_row(gproject_ref, rows_ref, C + SE + 3, EARLY, scale)
    at = 2 * EARLY + C + SE + 3
    breduce_ref[...] = rows_ref[at : at + 1, 0:SE] * scale


def unpack_late_kernel(scale, rows_ref, expand_ref, depth_ref, shift_ref, gain_ref):
    put_row(expand_ref, rows_ref, 0, LATE, scale)
    put_row(depth_ref, rows_ref, C, LATE, scale)
    put_row(shift_ref, rows_ref, C + 25, LATE, scale)
    put_row(gain_ref, rows_ref, C + 26, LATE, scale)


def unpack(kernel, rows, shapes, scale):
    return pl.pallas_call(
        functools.partial(kernel, scale),
        out_shape=tuple(f32(*shape) for shape in shapes),
        compiler_params=pltpu.CompilerParams(vmem_limit_bytes=40 * 2**20),
        cost_estimate=pl.CostEstimate(
            flops=rows.size, bytes_accessed=8 * rows.size, transcendentals=0
        ),
    )(rows)


def whole(shape):
    return pl.BlockSpec(shape, lambda c: (0,) * len(shape))


def lane_block(rows):
    return pl.BlockSpec((rows, LANES), lambda c: (0, c))


def peer_block(peers):
    return pl.BlockSpec((peers, 2, LANES), lambda c: (0, 0, c))


MAP_BLOCK = pl.BlockSpec((pl.squeezed, ROWS, LANES), lambda c: (c, 0, 0))
MAP = jax.ShapeDtypeStruct((CHUNKS, ROWS, LANES), F32)
EDGE = jax.ShapeDtypeStruct((ROWS, C), F32)
EDGE_BF16 = jax.ShapeDtypeStruct((ROWS, C), BF16)


def f32(*shape):
    return jax.ShapeDtypeStruct(shape, F32)


def call(kernel, ins, outs, scratch, flops):
    return pl.pallas_call(
        kernel,
        grid=(CHUNKS,),
        in_specs=ins,
        out_specs=tuple(spec for spec, _ in outs),
        out_shape=tuple(shape for _, shape in outs),
        scratch_shapes=scratch,
        compiler_params=pltpu.CompilerParams(vmem_limit_bytes=40 * 2**20),
        cost_estimate=pl.CostEstimate(
            flops=flops, bytes_accessed=12 * 2**20, transcendentals=ROWS * PADDED
        ),
    )


def exchange(copies, axes):
    return lax.all_to_all(copies, axes, 0, 0, tiled=True)


def plane_parts(rows):
    plane = lax.axis_size(PLANE)
    parts = exchange(rows.reshape(plane, rows.shape[0] // plane, LANES), PLANE)
    return jnp.sum(parts, axis=0)


def depth_parts(mine):
    depth = lax.axis_size("z")
    return jnp.sum(exchange(jnp.broadcast_to(mine[None], (depth,) + mine.shape), "z"), axis=0)


def plane_whole(mine):
    plane = lax.axis_size(PLANE)
    return exchange(jnp.broadcast_to(mine[None], (plane,) + mine.shape), PLANE).reshape(-1, LANES)


def tie(first, second):
    return lax.optimization_barrier((first, second))


def per_device(
    block_input,
    cotangent,
    w_expand,
    gain_expand,
    shift_expand,
    w_depth,
    gain_depth,
    shift_depth,
    w_reduce,
    b_reduce,
    w_restore,
    b_restore,
    w_project,
    gain_project,
    upper_grads,
):
    peers = lax.axis_size(GROUP)
    images_total = lax.axis_size(AXES)
    extra = PADDED - HID
    images, cot = block_input[0, 0], cotangent[0, 0]
    wexp = jnp.pad(w_expand, ((0, 0), (0, extra)))
    wproj = jnp.pad(w_project.T, ((0, 0), (0, extra)))
    wred = jnp.pad(w_reduce.astype(F32).T, ((0, SE_ROWS - SE), (0, extra)))
    wres = jnp.pad(w_restore.astype(F32), ((0, SE_ROWS - SE), (0, extra)))
    bred = jnp.broadcast_to(jnp.pad(b_reduce, (0, SE_ROWS - SE))[:, None], (SE_ROWS, LANES))
    bres = jnp.pad(b_restore, (0, extra))[None]
    table = jnp.concatenate(
        [w_depth.astype(F32)]
        + [v[None] for v in (gain_expand, shift_expand, gain_depth, shift_depth)],
        axis=0,
    )
    table = jnp.pad(table, ((0, TABLE - table.shape[0]), (0, extra)))
    xpad_spec, w_spec = whole((ROWS, C)), lane_block(C)
    se_spec = whole((SE_ROWS, PADDED))
    stat_out = (peer_block(peers), f32(peers, 2, PADDED))
    stat_whole = (whole((peers, 2, PADDED)), f32(peers, 2, PADDED))
    moments = (lane_block(8), f32(8, PADDED))
    map_f32 = pltpu.VMEM((ROWS, LANES), F32)
    map_bf16 = pltpu.VMEM((ROWS, LANES), BF16)
    line = pltpu.VMEM((2, WIDE, C), F32)
    halo = pltpu.VMEM((HALO, LANES), F32)
    matmul = 2 * ROWS * C * PADDED

    xpad, stat = call(
        stats_kernel,
        [whole((SIDE, SIDE, C)), w_spec],
        [(xpad_spec, EDGE_BF16), stat_out],
        [map_f32, line],
        matmul,
    )(images, wexp)
    gathered = exchange(stat, GROUP)
    upper = plane_parts(upper_grads[0].reshape(-1, LANES))
    depth, stat, moment_one = call(
        forward_kernel,
        [xpad_spec, w_spec, peer_block(peers), lane_block(TABLE)],
        [(MAP_BLOCK, MAP), stat_out, moments],
        [map_f32, halo],
        50 * ROWS * PADDED,
    )(xpad, wexp, gathered, table)
    stat, upper = tie(stat, upper)
    gathered = exchange(stat, GROUP)
    upper = depth_parts(upper)
    moment_two, project, cpad, vector, column, stat = call(
        project_kernel,
        [
            MAP_BLOCK,
            peer_block(peers),
            lane_block(TABLE),
            whole((C, PADDED)),
            whole((SIDE, SIDE, C)),
            se_spec,
            se_spec,
            whole((SE_ROWS, LANES)),
            whole((1, PADDED)),
        ],
        [
            moments,
            (whole((ROWS, C)), EDGE),
            (whole((ROWS, C)), EDGE_BF16),
            (whole((8, PADDED)), f32(8, PADDED)),
            (whole((2, SE_ROWS, LANES)), f32(2, SE_ROWS, LANES)),
            (whole((peers, 4, C)), f32(peers, 4, C)),
        ],
        [pltpu.VMEM((CHUNKS, ROWS, LANES), BF16), map_bf16, line],
        matmul,
    )(depth, gathered, table, wproj, cot, wred, wres, bred, bres)
    stat, upper = tie(stat, upper)
    gathered = exchange(stat, GROUP)
    upper = plane_whole(upper)
    first, slope, early, pooled, stat = call(
        back_project_kernel,
        [
            MAP_BLOCK,
            whole((peers, 4, C)),
            lane_block(TABLE),
            lane_block(8),
            whole((ROWS, C)),
            whole((ROWS, C)),
            whole((1, C)),
            w_spec,
            whole((8, PADDED)),
            whole((2, SE_ROWS, LANES)),
            se_spec,
            se_spec,
        ],
        [
            (MAP_BLOCK, MAP),
            (MAP_BLOCK, MAP),
            (whole((EARLY_ROWS, LANES)), f32(EARLY_ROWS, LANES)),
            (whole((8, PADDED)), f32(8, PADDED)),
            stat_whole,
        ],
        [
            pltpu.VMEM((ROWS, C), BF16),
            map_bf16,
            map_f32,
            pltpu.VMEM((8, PADDED), F32),
            pltpu.VMEM((8, 2 * LANES), F32),
        ],
        2 * matmul,
    )(
        depth,
        gathered,
        table,
        moment_two,
        project,
        cpad,
        gain_project[None],
        wproj,
        vector,
        column,
        wred,
        wres,
    )
    stat, upper = tie(stat, upper)
    gathered = exchange(stat, GROUP)
    early = plane_parts(early)
    grad_one, stat, sums = call(
        back_depth_kernel,
        [
            MAP_BLOCK,
            MAP_BLOCK,
            MAP_BLOCK,
            peer_block(peers),
            lane_block(TABLE),
            lane_block(8),
            lane_block(8),
            lane_block(8),
            lane_block(8),
            xpad_spec,
            w_spec,
        ],
        [(MAP_BLOCK, MAP), stat_out, (lane_block(TABLE), f32(TABLE, PADDED))],
        [map_f32, halo, halo, map_f32],
        100 * ROWS * PADDED,
    )(depth, first, slope, gathered, table, moment_two, moment_one, vector, pooled, xpad, wexp)
    stat, early = tie(stat, early)
    gathered = exchange(stat, GROUP)
    early = depth_parts(early)
    input_grad, late = call(
        back_expand_kernel,
        [
            MAP_BLOCK,
            peer_block(peers),
            lane_block(TABLE),
            lane_block(8),
            xpad_spec,
            w_spec,
            lane_block(TABLE),
            xpad_spec,
        ],
        [
            (whole((SIDE, SIDE, C)), jax.ShapeDtypeStruct((SIDE, SIDE, C), BF16)),
            (whole((LATE_ROWS, LANES)), f32(LATE_ROWS, LANES)),
        ],
        [map_f32, map_bf16, pltpu.VMEM((ROWS, C), F32)],
        3 * matmul,
    )(grad_one, gathered, table, moment_one, xpad, wexp, sums, cpad)

    late, early = tie(late, early)
    late = plane_parts(late)
    early = plane_whole(early)
    late, early = tie(late, early)
    late = plane_whole(depth_parts(late))

    scale = 1.0 / images_total
    wide = (1, HID)
    g_project, g_restore, g_reduce, g_brestore, g_shift_two, g_gain_two, g_gproject, g_breduce = (
        unpack(
            unpack_early_kernel,
            early,
            [(C, HID), (SE, HID), (SE, HID), wide, wide, wide, (1, C), (1, SE)],
            scale,
        )
    )
    g_expand, g_depth, g_shift_one, g_gain_one = unpack(
        unpack_late_kernel, late, [(C, HID), (KER * KER, HID), wide, wide], scale
    )
    return (
        input_grad[None, None],
        g_expand,
        g_gain_one[0],
        g_shift_one[0],
        g_depth,
        g_gain_two[0],
        g_shift_two[0],
        g_reduce.T,
        g_breduce[0],
        g_restore,
        g_brestore[0],
        g_project.T,
        g_gproject[0],
        upper.reshape(-1),
    )


def solution(mesh):
    chips = Mesh(mesh.devices.reshape(SHAPE), AXES)
    maps = P(("z", "core"), GROUP, None, None, None)
    return jax.shard_map(
        per_device,
        mesh=chips,
        in_specs=(maps, maps) + (P(),) * 12 + (P(AXES, None),),
        out_specs=(maps,) + (P(),) * 13,
        check_vma=False,
    )
```

time: 1250 us -> 408 us (0.33)
  blocking collectives: 882 us -> 132 us
  other arithmetic: 155 us -> 4.75 us
  Pallas kernels: 0 us -> 106 us
  waiting for transfers between devices: 171 us -> 78.1 us
  starting transfers between devices: 0.04 us -> 57.8 us
  matrix products: 15.9 us -> 0 us
  local copies, waits for them, and re-layouts: 10.5 us -> 26.2 us
  between operations: 15.6 us -> 1.05 us
    psum x10 -> x0, blocking collectives: 882 us -> none  [the longest x3 278 us: norm_back(): lax.psum((jnp.sum(grad_normed, axis=(0, 1, 2)), jnp.sum(grad_normed * nor...]
    psum x1 -> x0, waiting for transfers between devices: 171 us -> none  [per_device(): lax.psum((upper_grads[0], grad_expand, grad_gain_expand, grad_shift_expan...]
    all_to_all x0 -> x7, blocking collectives: none -> 132 us  [exchange(): return lax.all_to_all(copies, axes, 0, 0, tiled=True)]
    reduce_sum x11 -> x6, other arithmetic: 125 us -> 1.64 us  [the longest x3 1.6 us: plane_parts(): return jnp.sum(parts, axis=0)]
    pallas_call x0 -> x8, Pallas kernels: none -> 106 us  [the longest x1 33.9 us: per_device(): call(back_depth_kernel, [MAP_BLOCK, MAP_BLOCK, MAP_BLOCK, peer_block(peer...]
    all_to_all x0 -> x7, waiting for transfers between devices: none -> 78.1 us  [exchange(): return lax.all_to_all(copies, axes, 0, 0, tiled=True)]
    all_to_all x0 -> x7, starting transfers between devices: none -> 57.8 us  [exchange(): return lax.all_to_all(copies, axes, 0, 0, tiled=True)]
    unnamed x177 -> x45, local copies, waits for them, and re-layouts: 3.55 us -> 20.7 us
  transfers between devices with their start and end apart: 1 -> 7, of which waited for: 1 -> 4; matrix products, arithmetic and copies ran while one was open for 1% -> 1% of each run, Pallas kernels for 0% -> 18%
where the time goes in v2:
time: 408 us; the launch traced here: 406 us
  blocking collectives  132 us (32%)
  Pallas kernels  106 us (26%)
  waiting for transfers between devices  78.1 us (19%)
  starting transfers between devices  57.8 us (14%)
  local copies, waits for them, and re-layouts  26.2 us (6%)
  other arithmetic  4.75 us (1%)
    all_to_all x7, blocking collectives, exchange(): return lax.all_to_all(copies, axes, 0, 0, tiled=True)  132 us
    all_to_all x7, waiting for transfers between devices, exchange(): return lax.all_to_all(copies, axes, 0, 0, tiled=True)  78.1 us
    all_to_all x7, starting transfers between devices, exchange(): return lax.all_to_all(copies, axes, 0, 0, tiled=True)  57.8 us
    pallas_call x1, Pallas kernels, per_device(): call(back_depth_kernel, [MAP_BLOCK, MAP_BLOCK, MAP_BLOCK, peer_block(peer...  33.9 us
    pallas_call x1, Pallas kernels, per_device(): call(forward_kernel, [xpad_spec, w_spec, peer_block(peers), lane_block(TA...  21.9 us
    unnamed x45, local copies, waits for them, and re-layouts  20.7 us
    pallas_call x1, Pallas kernels, per_device(): call(back_project_kernel, [MAP_BLOCK, whole((peers, 4, C)), lane_block(TA...  16.3 us
    pallas_call x1, Pallas kernels, per_device(): call(back_expand_kernel, [MAP_BLOCK, peer_block(peers), lane_block(TABLE)...  13.2 us
  transfers between devices with their start and end apart: 7, of which 4 were waited for; matrix products, arithmetic and copies ran while one was open for 1% of the time, Pallas kernels for 18%

profile of v2, /device:TPU:1, one launch (start us, length us, event | category | flops | bytes accessed | tf_op | source)
XLA Modules:
  0.0 406.2 jit_solution(7494486764389690606)
XLA Ops:
  2.8 6.3 %shard_map.254 = (bf16[928,176]{1,0:T(8,128)(2,1)S(1)}, f32[32,2,1152]{2,1,0:T(2,128)S(1)}) custom-call(bf16[29,29,176]{2,1,0:T(8,128)(2,1)S(1)} %bitcast.23, bf16[176,1152]{1,0:T(8,128)(2,1)S(1)} %pad.30.w_ref), custom_call_target="tpu_custom_call" | custom-call | flops 376307712 | bytes 12582912 | tf_op jit(solution)/shard_map/pallas_call | solution.py:671
  9.1 20.3 %all_to_all.70.gathered_ref = f32[32,2,1152]{2,1,0:T(2,128)S(1)} all-to-all(f32[32,2,1152]{2,1,0:T(2,128)S(1)} %get-tuple-element.60), channel_id=1, replica_groups=mesh['x'=4,'y'=8,'z'=8,'core'=2] {'x','y'}, dimensions={0} | all-to-all | bytes 589824 | tf_op jit(solution)/shard_map/all_to_all | solution.py:604
  29.4 8.7 %all-to-all-start.1 = ((f32[64,16,128]{2,1,0:T(8,128)}), f32[64,16,128]{2,1,0:T(8,128)S(1)}, u32[]{:S(2)}, u32[]{:S(2)}) async-start(f32[64,16,128]{2,1,0:T(8,128)} %bitcast.24), calls=%async_computation.1 | async-start | bytes 1048576 | tf_op jit(solution)/shard_map/all_to_all | solution.py:604
  38.3 21.9 %shard_map.255 = (f32[9,928,128]{2,1,0:T(8,128)S(1)}, f32[32,2,1152]{2,1,0:T(2,128)}, f32[8,1152]{1,0:T(8,128)S(1)}) custom-call(bf16[928,176]{1,0:T(8,128)(2,1)S(1)} %get-tuple-element.59.xpad_ref, bf16[176,1152]{1,0:T(8,128)(2,1)S(1)} %pad.30.w_ref, f32[32,2,1152]{2,1,0:T(2,128)S(1)} %all_to_all.70.gathered_ref, f32[32,1152]{1,0:T(8,128)S(1)} %pad.31.table_ref), custom_call_target="tpu_custom_call" | custom-call | flops 53452800 | bytes 12582912 | tf_op jit(solution)/shard_map/pallas_call | solution.py:680
  62.3 17.1 %all_to_all.71 = f32[8,16,128]{2,1,0:T(8,128)S(1)} all-to-all(f32[8,16,128]{2,1,0:T(8,128)S(1)} %broadcast_in_dim.34), channel_id=1, replica_groups=mesh['x'=4,'y'=8,'z'=8,'core'=2] {'z'}, dimensions={0} | all-to-all | bytes 131072 | tf_op jit(solution)/shard_map/all_to_all | solution.py:604
  79.4 9.5 %all-to-all-start.2 = ((f32[32,2,1152]{2,1,0:T(2,128)}), f32[32,2,1152]{2,1,0:T(2,128)S(1)}, u32[]{:S(2)}, u32[]{:S(2)}) async-start(f32[32,2,1152]{2,1,0:T(2,128)} %get-tuple-element.63), calls=%async_computation.2 | async-start | bytes 589824 | tf_op jit(solution)/shard_map/all_to_all | solution.py:604
  90.1 8.7 %all-to-all-done.2.gathered_ref = f32[32,2,1152]{2,1,0:T(2,128)S(1)} async-done(((f32[32,2,1152]{2,1,0:T(2,128)}), f32[32,2,1152]{2,1,0:T(2,128)S(1)}, u32[]{:S(2)}, u32[]{:S(2)}) %all-to-all-start.2) | async-done | bytes 294944 | tf_op jit(solution)/shard_map/all_to_all | solution.py:604
  101.1 12.7 %shard_map.256 = (f32[8,1152]{1,0:T(8,128)S(1)}, f32[928,176]{1,0:T(8,128)S(1)}, bf16[928,176]{1,0:T(8,128)(2,1)S(1)}, f32[8,1152]{1,0:T(8,128)S(1)}, f32[2,48,1...) custom-call(f32[9,928,128]{2,1,0:T(8,128)S(1)} %copy-done.1, f32[32,2,1152]{2,1,0:T(2,128)S(1)} %all-to-all-done.2.gathered_ref, ...), custom_call_target="tpu_custom_call" | custom-call | flops 376307712 | bytes 12582912 | tf_op jit(solution)/shard_map/pallas_call | solution.py:690
  114.7 14.6 %all_to_all.72.gathered_ref = f32[32,4,176]{2,1,0:T(4,128)S(1)} all-to-all(f32[32,4,176]{2,1,0:T(4,128)S(1)} %get-tuple-element.66), channel_id=1, replica_groups=mesh['x'=4,'y'=8,'z'=8,'core'=2] {'x','y'}, dimensions={0} | all-to-all | bytes 180224 | tf_op jit(solution)/shard_map/all_to_all | solution.py:604
  130.1 9.0 %all-to-all-start.5 = ((f32[64,16,128]{2,1,0:T(8,128)}), f32[64,16,128]{2,1,0:T(8,128)}, u32[]{:S(2)}, u32[]{:S(2)}) async-start(f32[64,16,128]{2,1,0:T(8,128)} %broadcast_in_dim.71), calls=%async_computation.5 | async-start | bytes 1048576 | tf_op jit(solution)/shard_map/all_to_all | solution.py:604
  140.3 16.3 %shard_map.257 = (f32[9,928,128]{2,1,0:T(8,128)S(1)}, f32[9,928,128]{2,1,0:T(8,128)S(1)}, f32[2560,128]{1,0:T(8,128)S(1)}, f32[8,1152]{1,0:T(8,128)S(1)}, f32[32,2,1152]{2,1,0:T(2,128)S(1)}) custom-call(f32[9,928,128]{2,1,0:T(8,128)} %copy-done, f32[32,4,176]{2,1,0:T(4,128)S(1)} %all_to_all.72.gathered_ref, f32[32,1152]{1,0:T(8,128)S(1)} %pad.31.table_ref, ...), custom_call_target="tpu_custom_call" | custom-call | flops 752615424 | bytes 12582912 | tf_op jit(solution)/shard_map/pallas_call | solution.py:717
  161.7 19.6 %all_to_all.73.gathered_ref = f32[32,2,1152]{2,1,0:T(2,128)S(1)} all-to-all(f32[32,2,1152]{2,1,0:T(2,128)S(1)} %get-tuple-element.76), channel_id=1, replica_groups=mesh['x'=4,'y'=8,'z'=8,'core'=2] {'x','y'}, dimensions={0} | all-to-all | bytes 589824 | tf_op jit(solution)/shard_map/all_to_all | solution.py:604
  181.3 8.7 %all-to-all-start.7 = ((f32[64,40,128]{2,1,0:T(8,128)}), f32[64,40,128]{2,1,0:T(8,128)}, u32[]{:S(2)}, u32[]{:S(2)}) async-start(f32[64,40,128]{2,1,0:T(8,128)} %bitcast.19), calls=%async_computation.7 | async-start | bytes 2621440 | tf_op jit(solution)/shard_map/all_to_all | solution.py:604
  192.2 33.9 %shard_map.258 = (f32[9,928,128]{2,1,0:T(8,128)S(1)}, f32[32,2,1152]{2,1,0:T(2,128)}, f32[32,1152]{1,0:T(8,128)S(1)}) custom-call(f32[9,928,128]{2,1,0:T(8,128)S(1)} %copy-done.2, f32[9,928,128]{2,1,0:T(8,128)} %copy-done.3, f32[9,928,128]{2,1,0:T(8,128)} %copy-done.4, f32[32,2,1152]{2,1,0:T(2,128)S(1)} %all_to_all.73.gathered_ref, ...), custom_call_target="tpu_custom_call" | custom-call | flops 106905600 | bytes 12582912 | tf_op jit(solution)/shard_map/pallas_call | solution.py:765
  229.5 11.3 %all_to_all.74 = f32[8,40,128]{2,1,0:T(8,128)S(1)} all-to-all(f32[8,40,128]{2,1,0:T(8,128)S(1)} %broadcast_in_dim.73), channel_id=1, replica_groups=mesh['x'=4,'y'=8,'z'=8,'core'=2] {'z'}, dimensions={0} | all-to-all | bytes 327680 | tf_op jit(solution)/shard_map/all_to_all | solution.py:604
  240.8 9.6 %all-to-all-start.8 = ((f32[32,2,1152]{2,1,0:T(2,128)}), f32[32,2,1152]{2,1,0:T(2,128)S(1)}, u32[]{:S(2)}, u32[]{:S(2)}) async-start(f32[32,2,1152]{2,1,0:T(2,128)} %get-tuple-element.82), calls=%async_computation.8 | async-start | bytes 589824 | tf_op jit(solution)/shard_map/all_to_all | solution.py:604
  250.5 9.8 %all-to-all-done.8.gathered_ref = f32[32,2,1152]{2,1,0:T(2,128)S(1)} async-done(((f32[32,2,1152]{2,1,0:T(2,128)}), f32[32,2,1152]{2,1,0:T(2,128)S(1)}, u32[]{:S(2)}, u32[]{:S(2)}) %all-to-all-start.8) | async-done | bytes 294944 | tf_op jit(solution)/shard_map/all_to_all | solution.py:604
  262.4 13.2 %shard_map.259 = (bf16[29,29,176]{2,1,0:T(8,128)(2,1)}, f32[2048,128]{1,0:T(8,128)S(1)}) custom-call(f32[9,928,128]{2,1,0:T(8,128)S(1)} %copy-done.6, f32[32,2,1152]{2,1,0:T(2,128)S(1)} %all-to-all-done.8.gathered_ref, f32[32,1152]{1,0:T(8,128)S(1)} %pad.31.table_ref, f32[8,1152]{1,0:T(8,128)S(1)} %get-tuple-element.77.moment_one_ref.moment_ref, ...), custom_call_target="tpu_custom_call" | custom-call | flops 1128923136 | bytes 12582912 | tf_op jit(solution)/shard_map/pallas_call | solution.py:787
  275.6 37.2 %all_to_all.75 = f32[64,32,128]{2,1,0:T(8,128)S(1)} all-to-all(f32[64,32,128]{2,1,0:T(8,128)S(1)} %bitcast.20), channel_id=1, replica_groups=mesh['x'=4,'y'=8,'z'=8,'core'=2] {'x','y','core'}, dimensions={0} | all-to-all | bytes 2097152 | tf_op jit(solution)/shard_map/all_to_all | solution.py:604
  314.0 6.2 %all-to-all-start.11 = ((f32[64,40,128]{2,1,0:T(8,128)}), f32[64,40,128]{2,1,0:T(8,128)S(1)}, u32[]{:S(2)}, u32[]{:S(2)}) async-start(f32[64,40,128]{2,1,0:T(8,128)} %broadcast_in_dim.74), calls=%async_computation.11 | async-start | bytes 2621440 | tf_op jit(solution)/shard_map/all_to_all | solution.py:604
  320.3 34.1 %all-to-all-done.11 = f32[64,40,128]{2,1,0:T(8,128)S(1)} async-done(((f32[64,40,128]{2,1,0:T(8,128)}), f32[64,40,128]{2,1,0:T(8,128)S(1)}, u32[]{:S(2)}, u32[]{:S(2)}) %all-to-all-start.11) | async-done | bytes 1310752 | tf_op jit(solution)/shard_map/all_to_all | solution.py:604
  354.4 11.9 %all_to_all.76 = f32[8,32,128]{2,1,0:T(8,128)S(1)} all-to-all(f32[8,32,128]{2,1,0:T(8,128)S(1)} %broadcast_in_dim.75), channel_id=1, replica_groups=mesh['x'=4,'y'=8,'z'=8,'core'=2] {'z'}, dimensions={0} | all-to-all | bytes 262144 | tf_op jit(solution)/shard_map/all_to_all | solution.py:604
  367.4 6.2 %all-to-all-start.13 = ((f32[64,32,128]{2,1,0:T(8,128)}), f32[64,32,128]{2,1,0:T(8,128)S(1)}, u32[]{:S(2)}, u32[]{:S(2)}) async-start(f32[64,32,128]{2,1,0:T(8,128)} %broadcast_in_dim.76), calls=%async_computation.13 | async-start | bytes 2097152 | tf_op jit(solution)/shard_map/all_to_all | solution.py:604
  376.5 25.6 %all-to-all-done.13 = f32[64,32,128]{2,1,0:T(8,128)S(1)} async-done(((f32[64,32,128]{2,1,0:T(8,128)}), f32[64,32,128]{2,1,0:T(8,128)S(1)}, u32[]{:S(2)}, u32[]{:S(2)}) %all-to-all-start.13) | async-done | bytes 1048608 | tf_op jit(solution)/shard_map/all_to_all | solution.py:604
  (80 shorter events, 33.0 us)
Async XLA Ops:
  0.6 37.5 %copy-start.16 = (f32[1056]{0:T(1024)S(1)}, f32[1056]{0:T(1024)}, u32[]{:S(2)}) copy-start(f32[1056]{0:T(1024)} %param.18) | copy-start | bytes 12676
  0.7 37.5 %copy-start.17 = (f32[1056]{0:T(1024)S(1)}, f32[1056]{0:T(1024)}, u32[]{:S(2)}) copy-start(f32[1056]{0:T(1024)} %param.19) | copy-start | bytes 12676
  0.7 37.5 %copy-start.18 = (f32[1056]{0:T(1024)S(1)}, f32[1056]{0:T(1024)}, u32[]{:S(2)}) copy-start(f32[1056]{0:T(1024)} %param.21) | copy-start | bytes 12676
  0.7 37.5 %copy-start.19 = (f32[1056]{0:T(1024)S(1)}, f32[1056]{0:T(1024)}, u32[]{:S(2)}) copy-start(f32[1056]{0:T(1024)} %param.22) | copy-start | bytes 12676
  0.7 37.6 %copy-start.15 = (bf16[25,1056]{1,0:T(8,128)(2,1)S(1)}, bf16[25,1056]{1,0:T(8,128)(2,1)}, u32[]{:S(2)}) copy-start(bf16[25,1056]{1,0:T(8,128)(2,1)} %param.20) | copy-start | bytes 158404
  0.7 88.2 %copy-start.21 = (f32[44]{0:T(128)S(1)}, f32[44]{0:T(128)}, u32[]{:S(2)}) copy-start(f32[44]{0:T(128)} %param.24) | copy-start | bytes 532
  0.7 88.2 %copy-start.20 = (f32[1056]{0:T(1024)S(1)}, f32[1056]{0:T(1024)}, u32[]{:S(2)}) copy-start(f32[1056]{0:T(1024)} %param.26) | copy-start | bytes 12676
  2.8 87.2 %copy-start.13 = (bf16[44,1056]{1,0:T(8,128)(2,1)S(1)}, bf16[44,1056]{1,0:T(8,128)(2,1)}, u32[]{:S(2)}) copy-start(bf16[44,1056]{1,0:T(8,128)(2,1)} %param.25) | copy-start | bytes 278788
  2.8 87.2 %copy-start.14 = (bf16[1056,44]{0,1:T(8,128)(2,1)S(1)}, bf16[1056,44]{0,1:T(8,128)(2,1)}, u32[]{:S(2)}) copy-start(bf16[1056,44]{0,1:T(8,128)(2,1)} %param.23) | copy-start | bytes 278788
  2.8 96.0 %copy-start.10 = (bf16[1,1,29,29,176]{4,3,2,1,0:T(8,128)(2,1)S(1)}, bf16[1,1,29,29,176]{4,3,2,1,0:T(8,128)(2,1)}, u32[]{:S(2)}) copy-start(bf16[1,1,29,29,176]{4,3,2,1,0:T(8,128)(2,1)} %param.16) | copy-start | bytes 888100
  29.4 32.8 %all-to-all-start.1 = ((f32[64,16,128]{2,1,0:T(8,128)}), f32[64,16,128]{2,1,0:T(8,128)S(1)}, u32[]{:S(2)}, u32[]{:S(2)}) async-start(f32[64,16,128]{2,1,0:T(8,128)} %bitcast.24), calls=%async_computation.1 | async-start | bytes 1048576 | tf_op jit(solution)/shard_map/all_to_all | solution.py:604
  60.2 2.0 copy-start
  79.4 19.4 %all-to-all-start.2 = ((f32[32,2,1152]{2,1,0:T(2,128)}), f32[32,2,1152]{2,1,0:T(2,128)S(1)}, u32[]{:S(2)}, u32[]{:S(2)}) async-start(f32[32,2,1152]{2,1,0:T(2,128)} %get-tuple-element.63), calls=%async_computation.2 | async-start | bytes 589824 | tf_op jit(solution)/shard_map/all_to_all | solution.py:604
  90.0 49.1 %copy-start.11 = (f32[176]{0:T(256)S(1)}, f32[176]{0:T(256)}, u32[]{:S(2)}) copy-start(f32[176]{0:T(256)} %param.28) | copy-start | bytes 2116
  98.9 2.2 copy-start.1
  130.1 31.6 %all-to-all-start.5 = ((f32[64,16,128]{2,1,0:T(8,128)}), f32[64,16,128]{2,1,0:T(8,128)}, u32[]{:S(2)}, u32[]{:S(2)}) async-start(f32[64,16,128]{2,1,0:T(8,128)} %broadcast_in_dim.71), calls=%async_computation.5 | async-start | bytes 1048576 | tf_op jit(solution)/shard_map/all_to_all | solution.py:604
  156.6 2.0 copy-start.3
  158.6 2.0 copy-start.4
  181.3 46.8 %all-to-all-start.7 = ((f32[64,40,128]{2,1,0:T(8,128)}), f32[64,40,128]{2,1,0:T(8,128)}, u32[]{:S(2)}, u32[]{:S(2)}) async-start(f32[64,40,128]{2,1,0:T(8,128)} %bitcast.19), calls=%async_computation.7 | async-start | bytes 2621440 | tf_op jit(solution)/shard_map/all_to_all | solution.py:604
  190.0 2.2 copy-start.2
  240.8 19.4 %all-to-all-start.8 = ((f32[32,2,1152]{2,1,0:T(2,128)}), f32[32,2,1152]{2,1,0:T(2,128)S(1)}, u32[]{:S(2)}, u32[]{:S(2)}) async-start(f32[32,2,1152]{2,1,0:T(2,128)} %get-tuple-element.82), calls=%async_computation.8 | async-start | bytes 589824 | tf_op jit(solution)/shard_map/all_to_all | solution.py:604
  260.2 2.2 copy-start.6
  314.0 40.4 %all-to-all-start.11 = ((f32[64,40,128]{2,1,0:T(8,128)}), f32[64,40,128]{2,1,0:T(8,128)S(1)}, u32[]{:S(2)}, u32[]{:S(2)}) async-start(f32[64,40,128]{2,1,0:T(8,128)} %broadcast_in_dim.74), calls=%async_computation.11 | async-start | bytes 2621440 | tf_op jit(solution)/shard_map/all_to_all | solution.py:604
  367.4 34.7 %all-to-all-start.13 = ((f32[64,32,128]{2,1,0:T(8,128)}), f32[64,32,128]{2,1,0:T(8,128)S(1)}, u32[]{:S(2)}, u32[]{:S(2)}) async-start(f32[64,32,128]{2,1,0:T(8,128)} %broadcast_in_dim.76), calls=%async_computation.13 | async-start | bytes 2097152 | tf_op jit(solution)/shard_map/all_to_all | solution.py:604
  (5 other events, 6.2 us)

commit v3 on v2

--- a/solution.py
+++ b/solution.py
@@ -12,7 +12,7 @@
 SHAPE = (4, 8, 8, 2)
 AXES = ("x", "y", "z", "core")
 GROUP = ("x", "y")
-PLANE = ("x", "y", "core")
+CHIPS = ("x", "y", "z")
 SIDE = 29
 WIDE = 32
 ROWS = SIDE * WIDE
@@ -28,9 +28,12 @@
 GAIN_ONE, SHIFT_ONE, GAIN_TWO, SHIFT_TWO, BIAS = 25, 26, 27, 28, 29
 TABLE = 32
 EARLY = C + 2 * SE_ROWS
-EARLY_ROWS = 2560
+UPPER_AT = CHUNKS * EARLY
+UPPER_ROWS = 1024
+EARLY_ROWS = 4096
 LATE = C + TABLE
 LATE_ROWS = 2048
+PIECE = 4
 F32 = jnp.float32
 BF16 = jnp.bfloat16
 
@@ -50,11 +53,19 @@
 
 
 def row_at(index):
+    if isinstance(index, int):
+        return slice(index * WIDE, (index + 1) * WIDE)
     return pl.ds(pl.multiple_of(index * WIDE, WIDE), WIDE)
 
 
-def each_row(body, init, unroll=1):
-    return lax.fori_loop(0, SIDE, body, init, unroll=unroll)
+def each_row(body, init):
+    for i in range(SIDE):
+        init = body(i, init)
+    return init
+
+
+def loop_rows(body, init):
+    return lax.fori_loop(0, SIDE, body, init)
 
 
 def col_sum(values):
@@ -115,12 +126,13 @@
     return out
 
 
-def row_taps(halo_ref, taps, i, flip):
+def row_taps(halo_ref, tap_ref, i, flip):
     parts = [None] * KER
     for a in range(KER):
         source = halo_ref[row_at(i + a), :].reshape(WIDE // 8, 8, LANES)
         for b in range(KER):
-            term = source * taps[((KER - 1 - a) if flip else a) * KER + b]
+            k = ((KER - 1 - a) if flip else a) * KER + b
+            term = source * tap_ref[k * 8 : k * 8 + 8, :]
             parts[b] = term if parts[b] is None else parts[b] + term
     return slide([part.reshape(WIDE, LANES) for part in parts], -1 if flip else 1)
 
@@ -131,12 +143,22 @@
     ref[HALO - 2 * WIDE : HALO, :] = edge
 
 
-def tap_rows(table_ref):
-    return [jnp.broadcast_to(table_ref[k : k + 1, :], (8, LANES)) for k in range(KER * KER)]
+def spread_taps(table_ref, tap_ref):
+    for k in range(KER * KER):
+        tap_ref[k * 8 : k * 8 + 8, :] = jnp.broadcast_to(table_ref[k : k + 1, :], (8, LANES))
 
 
 def forward_kernel(
-    xpad_ref, w_ref, gathered_ref, table_ref, depth_ref, stat_ref, moment_ref, pre_ref, halo_ref
+    xpad_ref,
+    w_ref,
+    gathered_ref,
+    table_ref,
+    depth_ref,
+    stat_ref,
+    moment_ref,
+    pre_ref,
+    halo_ref,
+    tap_ref,
 ):
     @pl.when(pl.program_id(0) == 0)
     def _():
@@ -157,14 +179,14 @@
         return 0
 
     each_row(activate, 0)
-    taps = tap_rows(table_ref)
+    spread_taps(table_ref, tap_ref)
 
     def filter_row(i, acc):
-        out = jnp.where(mask, row_taps(halo_ref, taps, i, False), 0.0)
+        out = jnp.where(mask, row_taps(halo_ref, tap_ref, i, False), 0.0)
         depth_ref[row_at(i), :] = out
         return acc + out
 
-    mean = col_sum(each_row(filter_row, zeros())) / SPOTS
+    mean = col_sum(loop_rows(filter_row, zeros())) / SPOTS
     share(pair_rows(mean, spread_of(depth_ref, mean, mask)), stat_ref)
 
 
@@ -222,29 +244,20 @@
         restored = col_sum(wrestore_ref[...] * squeezed[:, 0:1]) + brestore_ref[...]
         vector_ref[1:2, :] = logistic(restored)
 
-        def project(c, _):
+        def fill(c, _):
             excite = vector_ref[1:2, lanes_at(c)]
 
             def scale_row(i, _):
-                hidden_ref[row_at(i), :] = (
+                hidden_ref[row_at(i), lanes_at(c)] = (
                     act_ref[c, row_at(i), :].astype(F32) * excite
                 ).astype(BF16)
                 return 0
 
             each_row(scale_row, 0)
-            part = dot(hidden_ref[...], wproject_ref[:, lanes_at(c)], 1, 1)
-
-            @pl.when(c == 0)
-            def _():
-                project_ref[...] = part
-
-            @pl.when(c > 0)
-            def _():
-                project_ref[...] += part
-
             return 0
 
-        lax.fori_loop(0, CHUNKS, project, 0)
+        lax.fori_loop(0, CHUNKS, fill, 0)
+        project_ref[...] = dot(hidden_ref[...], wproject_ref[...])
 
         def sums(i, accs):
             values, incoming = project_ref[row_at(i), :], cpad_ref[row_at(i), :].astype(F32)
@@ -287,14 +300,13 @@
     wrestore_ref,
     first_ref,
     slope_ref,
-    grads_ref,
-    pooled_ref,
+    hidden_ref,
+    gpp_ref,
+    row_ref,
+    reduce_ref,
     stat_ref,
-    gpp_ref,
-    hidden_ref,
     back_ref,
     sums_ref,
-    gain_sum_ref,
 ):
     step = pl.program_id(0)
     mask = valid_mask()
@@ -322,9 +334,8 @@
             gpp_ref[row_at(i), :] = jnp.where(wide, grad, 0.0).astype(BF16)
             return acc + incoming * normed
 
-        gain_sum_ref[...] = jnp.zeros_like(gain_sum_ref)
-        gain_sum_ref[0:1, 0:C] = col_sum(each_row(body, zeros(C)))
-        grads_ref[CHUNKS * EARLY :, :] = jnp.zeros((EARLY_ROWS - CHUNKS * EARLY, LANES), F32)
+        row_ref[...] = jnp.zeros_like(row_ref)
+        row_ref[4:5, 0:C] = col_sum(each_row(body, zeros(C)))
 
     center, scale = moment_ref[0:1, :], moment_ref[1:2, :]
     gain = table_ref[GAIN_TWO : GAIN_TWO + 1, :]
@@ -354,35 +365,52 @@
     totals = each_row(body, tuple(zeros() for _ in range(5)))
     for k in range(5):
         sums_ref[k : k + 1, lanes_at(step)] = col_sum(totals[k])
-    base = pl.multiple_of(step * EARLY, 16)
-    grads_ref[pl.ds(base, C), :] = dot(gpp_ref[...], hidden_ref[...], 0, 0)
 
     @pl.when(step == CHUNKS - 1)
     def _():
-        pooled, excite = vector_ref[0:1, :], vector_ref[1:2, :]
-        logit, squeezed = column_ref[0], column_ref[1]
+        excite = vector_ref[1:2, :]
+        logit = column_ref[0]
         grad_logit = sums_ref[0:1, :] * excite * (1.0 - excite)
         grad_squeezed = jnp.sum(wrestore_ref[...] * grad_logit, axis=1, keepdims=True)
         sig = logistic(logit)
         grad_reduce = grad_squeezed * (sig * (1.0 + logit * (1.0 - sig)))
         grad_pooled = col_sum(wreduce_ref[...] * grad_reduce[:, 0:1]) / SPOTS
-        pooled_ref[0:1, :] = grad_pooled
         shift_sum = excite * sums_ref[1:2, :] + grad_pooled * sums_ref[3:4, :]
         gain_sum = excite * sums_ref[2:3, :] + grad_pooled * sums_ref[4:5, :]
         share(pair_rows(shift_sum, gain_sum), stat_ref)
-        lane = lax.broadcasted_iota(jnp.int32, (SE_ROWS, LANES), 1)
-        row = lax.broadcasted_iota(jnp.int32, (SE_ROWS, LANES), 0)
-        bias_row = col_sum(jnp.where(lane == row, grad_reduce, 0.0))
-        for c in range(CHUNKS):
-            cut = slice(c * LANES, (c + 1) * LANES)
-            block = squeezed * grad_logit[:, cut]
-            block = jnp.where(row == SE, grad_logit[:, cut], block)
-            block = jnp.where(row == SE + 1, shift_sum[:, cut], block)
-            block = jnp.where(row == SE + 2, gain_sum[:, cut], block)
-            extra = gain_sum_ref[0:1, cut] if c < 2 else bias_row
-            block = jnp.where(row == SE + 3, extra, block)
-            grads_ref[c * EARLY + C : c * EARLY + C + SE_ROWS, :] = block
-            grads_ref[c * EARLY + C + SE_ROWS : (c + 1) * EARLY, :] = grad_reduce * pooled[:, cut]
+        row_ref[0:1, :] = grad_pooled
+        row_ref[1:2, :] = grad_logit
+        row_ref[2:3, :] = shift_sum
+        row_ref[3:4, :] = gain_sum
+        reduce_ref[...] = grad_reduce
+
+
+def early_kernel(
+    gpp_ref, hidden_ref, row_ref, reduce_ref, vector_ref, column_ref, upper_ref, grads_ref
+):
+    step = pl.program_id(0)
+    base = pl.multiple_of(step * EARLY, 16)
+    grads_ref[pl.ds(base, C), :] = dot(gpp_ref[...], hidden_ref[...], 0, 0)
+    lane = lax.broadcasted_iota(jnp.int32, (SE_ROWS, LANES), 1)
+    row = lax.broadcasted_iota(jnp.int32, (SE_ROWS, LANES), 0)
+    squeezed, grad_reduce = column_ref[1], reduce_ref[...]
+    block = squeezed * row_ref[1:2, :]
+    block = jnp.where(row == SE, row_ref[1:2, :], block)
+    block = jnp.where(row == SE + 1, row_ref[2:3, :], block)
+    block = jnp.where(row == SE + 2, row_ref[3:4, :], block)
+    bias_row = col_sum(jnp.where(lane == row, grad_reduce, 0.0))
+    extra = jnp.where(step < 2, row_ref[4:5, :], bias_row)
+    block = jnp.where(row == SE + 3, extra, block)
+    grads_ref[pl.ds(pl.multiple_of(base + C, 16), SE_ROWS), :] = block
+    grads_ref[pl.ds(pl.multiple_of(base + C + SE_ROWS, 16), SE_ROWS), :] = (
+        grad_reduce * vector_ref[0:1, :]
+    )
+
+    @pl.when(step == 0)
+    def _():
+        grads_ref[UPPER_AT : UPPER_AT + UPPER_ROWS, :] = upper_ref[...]
+        rest = EARLY_ROWS - UPPER_AT - UPPER_ROWS
+        grads_ref[UPPER_AT + UPPER_ROWS :, :] = jnp.zeros((rest, LANES), F32)
 
 
 def back_depth_kernel(
@@ -400,14 +428,15 @@
     grad_ref,
     stat_ref,
     sums_ref,
+    field_ref,
+    back_ref,
     pre_ref,
-    halo_ref,
     ghalo_ref,
     side_ref,
+    tap_ref,
 ):
     @pl.when(pl.program_id(0) == 0)
     def _():
-        clear_halo(halo_ref)
         clear_halo(ghalo_ref)
 
     mask = valid_mask()
@@ -427,19 +456,40 @@
     def prepare(i, _):
         normed = (depth_ref[row_at(i), :] - center) * scale
         grad = first_ref[row_at(i), :] * excite + slope_ref[row_at(i), :] * pooled
-        grad = scale * (grad - mean_first - normed * mean_second)
-        ghalo_ref[row_at(i + 2), :] = jnp.where(mask, grad, 0.0)
+        grad = jnp.where(mask, scale * (grad - mean_first - normed * mean_second), 0.0)
+        ghalo_ref[row_at(i + 2), :] = grad
+        back_ref[row_at(i), :] = grad
         act = pre_ref[row_at(i), :] * slope_one + offset_one
         sig = logistic(act)
-        silu = (act * sig).astype(BF16).astype(F32)
-        halo_ref[row_at(i + 2), :] = jnp.where(mask, silu, 0.0)
+        field_ref[row_at(i), :] = jnp.where(mask, act * sig, 0.0).astype(BF16)
         side_ref[row_at(i), :] = jnp.where(mask, sig * (1.0 + act * (1.0 - sig)), 0.0)
         return 0
 
     each_row(prepare, 0)
+    spread_taps(table_ref, tap_ref)
+
+    def input_grad(i, accs):
+        grad = row_taps(ghalo_ref, tap_ref, i, True) * side_ref[row_at(i), :]
+        grad_ref[row_at(i), :] = grad
+        normed = (pre_ref[row_at(i), :] - center_one) * scale_one
+        return accs[0] + grad, accs[1] + grad * normed
+
+    shift_sum, gain_sum = (col_sum(a) for a in loop_rows(input_grad, (zeros(), zeros())))
+    share(pair_rows(shift_sum, gain_sum), stat_ref)
+    sums_ref[...] = jnp.zeros_like(sums_ref)
+    sums_ref[0:1, :] = shift_sum
+    sums_ref[1:2, :] = gain_sum
+
+
+def kernel_grad_kernel(field_ref, back_ref, sums_ref, out_ref, halo_ref):
+    @pl.when(pl.program_id(0) == 0)
+    def _():
+        clear_halo(halo_ref)
+
+    halo_ref[2 * WIDE : 2 * WIDE + ROWS, :] = field_ref[...].astype(F32)
 
     def kernel_grad(i, accs):
-        grad = ghalo_ref[row_at(i + 2), :]
+        grad = back_ref[row_at(i), :]
         shifted = [
             (grad if b == 2 else pltpu.roll(grad, (b - 2) % WIDE, 0)).reshape(
                 WIDE // 8, 8, LANES
@@ -454,22 +504,10 @@
         return tuple(accs)
 
     start = tuple(jnp.zeros((8, LANES), F32) for _ in range(KER * KER))
-    accs = each_row(kernel_grad, start)
+    accs = loop_rows(kernel_grad, start)
     for k in range(KER * KER):
-        sums_ref[k : k + 1, :] = col_sum(accs[k])
-    taps = tap_rows(table_ref)
-
-    def input_grad(i, accs):
-        grad = row_taps(ghalo_ref, taps, i, True) * side_ref[row_at(i), :]
-        grad_ref[row_at(i), :] = grad
-        normed = (pre_ref[row_at(i), :] - center_one) * scale_one
-        return accs[0] + grad, accs[1] + grad * normed
-
-    shift_sum, gain_sum = (col_sum(a) for a in each_row(input_grad, (zeros(), zeros())))
-    share(pair_rows(shift_sum, gain_sum), stat_ref)
-    sums_ref[KER * KER : TABLE, :] = jnp.zeros((TABLE - KER * KER, LANES), F32)
-    sums_ref[25:26, :] = shift_sum
-    sums_ref[26:27, :] = gain_sum
+        out_ref[k : k + 1, :] = col_sum(accs[k])
+    out_ref[25:TABLE, :] = sums_ref[0 : TABLE - 25, :]
 
 
 def back_expand_kernel(
@@ -481,6 +519,8 @@
     w_ref,
     sums_ref,
     cpad_ref,
+    xturn_ref,
+    wturn_ref,
     out_ref,
     grads_ref,
     pre_ref,
@@ -499,26 +539,18 @@
     def body(i, _):
         normed = (pre_ref[row_at(i), :] - center) * scale
         grad = factor * (grad_ref[row_at(i), :] - mean_first - normed * mean_second)
-        gpe_ref[row_at(i), :] = jnp.where(mask, grad, 0.0).astype(BF16)
+        gpe_ref[row_at(i), lanes_at(step)] = jnp.where(mask, grad, 0.0).astype(BF16)
         return 0
 
     each_row(body, 0)
     base = pl.multiple_of(step * LATE, 16)
-    grads_ref[pl.ds(base, C), :] = dot(xpad_ref[...], gpe_ref[...], 0, 0)
+    grads_ref[pl.ds(base, C), :] = dot(xturn_ref[...], gpe_ref[:, lanes_at(step)])
     grads_ref[pl.ds(pl.multiple_of(base + C, 16), TABLE), :] = sums_ref[...]
-    part = dot(gpe_ref[...], w_ref[...], 1, 1)
-
-    @pl.when(step == 0)
-    def _():
-        acc_ref[...] = cpad_ref[...].astype(F32) + part
-        grads_ref[CHUNKS * LATE :, :] = jnp.zeros((LATE_ROWS - CHUNKS * LATE, LANES), F32)
-
-    @pl.when(step > 0)
-    def _():
-        acc_ref[...] += part
 
     @pl.when(step == CHUNKS - 1)
     def _():
+        grads_ref[CHUNKS * LATE :, :] = jnp.zeros((LATE_ROWS - CHUNKS * LATE, LANES), F32)
+        acc_ref[...] = cpad_ref[...].astype(F32) + dot(gpe_ref[...], wturn_ref[...])
         for i in range(SIDE):
             out_ref[i] = acc_ref[i * WIDE : i * WIDE + SIDE, :].astype(BF16)
 
@@ -531,8 +563,17 @@
 
 
 def unpack_early_kernel(
-    scale, rows_ref, project_ref, restore_ref, reduce_ref, brestore_ref, shift_ref, gain_ref,
-    gproject_ref, breduce_ref,
+    scale,
+    rows_ref,
+    project_ref,
+    restore_ref,
+    reduce_ref,
+    brestore_ref,
+    shift_ref,
+    gain_ref,
+    gproject_ref,
+    breduce_ref,
+    upper_ref,
 ):
     put_row(project_ref, rows_ref, 0, EARLY, scale)
     put_row(restore_ref, rows_ref, C, EARLY, scale)
@@ -543,6 +584,7 @@
     put_row(gproject_ref, rows_ref, C + SE + 3, EARLY, scale)
     at = 2 * EARLY + C + SE + 3
     breduce_ref[...] = rows_ref[at : at + 1, 0:SE] * scale
+    upper_ref[...] = rows_ref[UPPER_AT : UPPER_AT + UPPER_ROWS, :]
 
 
 def unpack_late_kernel(scale, rows_ref, expand_ref, depth_ref, shift_ref, gain_ref):
@@ -556,7 +598,7 @@
     return pl.pallas_call(
         functools.partial(kernel, scale),
         out_shape=tuple(f32(*shape) for shape in shapes),
-        compiler_params=pltpu.CompilerParams(vmem_limit_bytes=40 * 2**20),
+        compiler_params=pltpu.CompilerParams(vmem_limit_bytes=20 * 2**20),
         cost_estimate=pl.CostEstimate(
             flops=rows.size, bytes_accessed=8 * rows.size, transcendentals=0
         ),
@@ -577,6 +619,7 @@
 
 MAP_BLOCK = pl.BlockSpec((pl.squeezed, ROWS, LANES), lambda c: (c, 0, 0))
 MAP = jax.ShapeDtypeStruct((CHUNKS, ROWS, LANES), F32)
+MAP_BF16 = jax.ShapeDtypeStruct((CHUNKS, ROWS, LANES), BF16)
 EDGE = jax.ShapeDtypeStruct((ROWS, C), F32)
 EDGE_BF16 = jax.ShapeDtypeStruct((ROWS, C), BF16)
 
@@ -593,7 +636,7 @@
         out_specs=tuple(spec for spec, _ in outs),
         out_shape=tuple(shape for _, shape in outs),
         scratch_shapes=scratch,
-        compiler_params=pltpu.CompilerParams(vmem_limit_bytes=40 * 2**20),
+        compiler_params=pltpu.CompilerParams(vmem_limit_bytes=20 * 2**20),
         cost_estimate=pl.CostEstimate(
             flops=flops, bytes_accessed=12 * 2**20, transcendentals=ROWS * PADDED
         ),
@@ -604,20 +647,28 @@
     return lax.all_to_all(copies, axes, 0, 0, tiled=True)
 
 
-def plane_parts(rows):
-    plane = lax.axis_size(PLANE)
-    parts = exchange(rows.reshape(plane, rows.shape[0] // plane, LANES), PLANE)
-    return jnp.sum(parts, axis=0)
-
-
-def depth_parts(mine):
-    depth = lax.axis_size("z")
-    return jnp.sum(exchange(jnp.broadcast_to(mine[None], (depth,) + mine.shape), "z"), axis=0)
-
-
-def plane_whole(mine):
-    plane = lax.axis_size(PLANE)
-    return exchange(jnp.broadcast_to(mine[None], (plane,) + mine.shape), PLANE).reshape(-1, LANES)
+def swap(rows):
+    return lax.ppermute(rows, "core", [(i, i ^ 1) for i in range(lax.axis_size("core"))])
+
+
+def pair_sum(rows):
+    chips = lax.axis_size(CHIPS)
+    near = lax.axis_index("core") == 0
+    halves = rows.reshape(2, chips, -1, PIECE, LANES)
+    mine = jnp.where(near, halves[0], halves[1])
+    return mine + swap(jnp.where(near, halves[1], halves[0]))
+
+
+def chip_sum(mine):
+    return jnp.sum(exchange(mine, CHIPS), axis=0)
+
+
+def all_parts(mine):
+    chips = lax.axis_size(CHIPS)
+    near = lax.axis_index("core") == 0
+    half = exchange(jnp.broadcast_to(mine[None], (chips,) + mine.shape), CHIPS)
+    other = swap(half)
+    return jnp.stack([jnp.where(near, half, other), jnp.where(near, other, half)])
 
 
 def tie(first, second):
@@ -646,7 +697,9 @@
     extra = PADDED - HID
     images, cot = block_input[0, 0], cotangent[0, 0]
     wexp = jnp.pad(w_expand, ((0, 0), (0, extra)))
-    wproj = jnp.pad(w_project.T, ((0, 0), (0, extra)))
+    wproj = jnp.pad(w_project, ((0, extra), (0, 0)))
+    wproj_turn = jnp.pad(w_project.T, ((0, 0), (0, extra)))
+    wexp_turn = jnp.pad(w_expand.T, ((0, extra), (0, 0)))
     wred = jnp.pad(w_reduce.astype(F32).T, ((0, SE_ROWS - SE), (0, extra)))
     wres = jnp.pad(w_restore.astype(F32), ((0, SE_ROWS - SE), (0, extra)))
     bred = jnp.broadcast_to(jnp.pad(b_reduce, (0, SE_ROWS - SE))[:, None], (SE_ROWS, LANES))
@@ -665,6 +718,7 @@
     map_f32 = pltpu.VMEM((ROWS, LANES), F32)
     map_bf16 = pltpu.VMEM((ROWS, LANES), BF16)
     line = pltpu.VMEM((2, WIDE, C), F32)
+    taps = pltpu.VMEM((KER * KER * 8, LANES), F32)
     halo = pltpu.VMEM((HALO, LANES), F32)
     matmul = 2 * ROWS * C * PADDED
 
@@ -676,24 +730,21 @@
         matmul,
     )(images, wexp)
     gathered = exchange(stat, GROUP)
-    upper = plane_parts(upper_grads[0].reshape(-1, LANES))
     depth, stat, moment_one = call(
         forward_kernel,
         [xpad_spec, w_spec, peer_block(peers), lane_block(TABLE)],
         [(MAP_BLOCK, MAP), stat_out, moments],
-        [map_f32, halo],
+        [map_f32, halo, taps],
         50 * ROWS * PADDED,
     )(xpad, wexp, gathered, table)
-    stat, upper = tie(stat, upper)
     gathered = exchange(stat, GROUP)
-    upper = depth_parts(upper)
     moment_two, project, cpad, vector, column, stat = call(
         project_kernel,
         [
             MAP_BLOCK,
             peer_block(peers),
             lane_block(TABLE),
-            whole((C, PADDED)),
+            whole((PADDED, C)),
             whole((SIDE, SIDE, C)),
             se_spec,
             se_spec,
@@ -708,13 +759,15 @@
             (whole((2, SE_ROWS, LANES)), f32(2, SE_ROWS, LANES)),
             (whole((peers, 4, C)), f32(peers, 4, C)),
         ],
-        [pltpu.VMEM((CHUNKS, ROWS, LANES), BF16), map_bf16, line],
+        [
+            pltpu.VMEM((CHUNKS, ROWS, LANES), BF16),
+            pltpu.VMEM((ROWS, PADDED), BF16),
+            line,
+        ],
         matmul,
     )(depth, gathered, table, wproj, cot, wred, wres, bred, bres)
-    stat, upper = tie(stat, upper)
     gathered = exchange(stat, GROUP)
-    upper = plane_whole(upper)
-    first, slope, early, pooled, stat = call(
+    first, slope, hidden, gpp, rows, reduce, stat = call(
         back_project_kernel,
         [
             MAP_BLOCK,
@@ -733,17 +786,13 @@
         [
             (MAP_BLOCK, MAP),
             (MAP_BLOCK, MAP),
-            (whole((EARLY_ROWS, LANES)), f32(EARLY_ROWS, LANES)),
+            (MAP_BLOCK, MAP_BF16),
+            (whole((ROWS, C)), EDGE_BF16),
             (whole((8, PADDED)), f32(8, PADDED)),
+            (whole((SE_ROWS, LANES)), f32(SE_ROWS, LANES)),
             stat_whole,
         ],
-        [
-            pltpu.VMEM((ROWS, C), BF16),
-            map_bf16,
-            map_f32,
-            pltpu.VMEM((8, PADDED), F32),
-            pltpu.VMEM((8, 2 * LANES), F32),
-        ],
+        [map_f32, pltpu.VMEM((8, PADDED), F32)],
         2 * matmul,
     )(
         depth,
@@ -753,16 +802,31 @@
         project,
         cpad,
         gain_project[None],
-        wproj,
+        wproj_turn,
         vector,
         column,
         wred,
         wres,
     )
-    stat, upper = tie(stat, upper)
     gathered = exchange(stat, GROUP)
-    early = plane_parts(early)
-    grad_one, stat, sums = call(
+    (early,) = call(
+        early_kernel,
+        [
+            whole((ROWS, C)),
+            MAP_BLOCK,
+            lane_block(8),
+            whole((SE_ROWS, LANES)),
+            lane_block(8),
+            whole((2, SE_ROWS, LANES)),
+            whole((UPPER_ROWS, LANES)),
+        ],
+        [(whole((EARLY_ROWS, LANES)), f32(EARLY_ROWS, LANES))],
+        [],
+        10 * matmul,
+    )(gpp, hidden, rows, reduce, vector, column, upper_grads[0].reshape(-1, LANES))
+    early, gathered = tie(pair_sum(early), gathered)
+    early = chip_sum(early)
+    grad_one, stat, sums, field, back = call(
         back_depth_kernel,
         [
             MAP_BLOCK,
@@ -777,13 +841,25 @@
             xpad_spec,
             w_spec,
         ],
-        [(MAP_BLOCK, MAP), stat_out, (lane_block(TABLE), f32(TABLE, PADDED))],
-        [map_f32, halo, halo, map_f32],
+        [
+            (MAP_BLOCK, MAP),
+            stat_out,
+            (lane_block(8), f32(8, PADDED)),
+            (MAP_BLOCK, MAP_BF16),
+            (MAP_BLOCK, MAP),
+        ],
+        [map_f32, halo, map_f32, taps],
         100 * ROWS * PADDED,
-    )(depth, first, slope, gathered, table, moment_two, moment_one, vector, pooled, xpad, wexp)
-    stat, early = tie(stat, early)
+    )(depth, first, slope, gathered, table, moment_two, moment_one, vector, rows, xpad, wexp)
+    stat, early, field = lax.optimization_barrier((stat, early, field))
     gathered = exchange(stat, GROUP)
-    early = depth_parts(early)
+    (sums,) = call(
+        kernel_grad_kernel,
+        [MAP_BLOCK, MAP_BLOCK, lane_block(8)],
+        [(lane_block(TABLE), f32(TABLE, PADDED))],
+        [halo],
+        50 * ROWS * PADDED,
+    )(field, back, sums)
     input_grad, late = call(
         back_expand_kernel,
         [
@@ -795,28 +871,30 @@
             w_spec,
             lane_block(TABLE),
             xpad_spec,
+            whole((C, ROWS)),
+            whole((PADDED, C)),
         ],
         [
             (whole((SIDE, SIDE, C)), jax.ShapeDtypeStruct((SIDE, SIDE, C), BF16)),
             (whole((LATE_ROWS, LANES)), f32(LATE_ROWS, LANES)),
         ],
-        [map_f32, map_bf16, pltpu.VMEM((ROWS, C), F32)],
+        [map_f32, pltpu.VMEM((ROWS, PADDED), BF16), pltpu.VMEM((ROWS, C), F32)],
         3 * matmul,
-    )(grad_one, gathered, table, moment_one, xpad, wexp, sums, cpad)
-
-    late, early = tie(late, early)
-    late = plane_parts(late)
-    early = plane_whole(early)
-    late, early = tie(late, early)
-    late = plane_whole(depth_parts(late))
+    )(grad_one, gathered, table, moment_one, xpad, wexp, sums, cpad, xpad.T, wexp_turn)
+
+    late = chip_sum(pair_sum(late))
+    split = early.shape[0]
+    full = all_parts(jnp.concatenate([early, late]))
+    early = full[:, :, :split].reshape(EARLY_ROWS, LANES)
+    late = full[:, :, split:].reshape(LATE_ROWS, LANES)
 
     scale = 1.0 / images_total
     wide = (1, HID)
-    g_project, g_restore, g_reduce, g_brestore, g_shift_two, g_gain_two, g_gproject, g_breduce = (
+    g_project, g_restore, g_reduce, g_brestore, g_shift_two, g_gain_two, g_gproject, g_breduce, upper = (
         unpack(
             unpack_early_kernel,
             early,
-            [(C, HID), (SE, HID), (SE, HID), wide, wide, wide, (1, C), (1, SE)],
+            [(C, HID), (SE, HID), (SE, HID), wide, wide, wide, (1, C), (1, SE), (UPPER_ROWS, LANES)],
             scale,
         )
     )

time: 408 us -> 314 us (0.77)
  blocking collectives: 132 us -> 87.1 us
  waiting for transfers between devices: 78.1 us -> 39.3 us
  Pallas kernels: 106 us -> 73.4 us
  starting transfers between devices: 57.8 us -> 69.7 us
  local copies, waits for them, and re-layouts: 26.2 us -> 32.4 us
  other arithmetic: 4.75 us -> 9.65 us
    all_to_all x7 -> x2, blocking collectives: 132 us -> 87.1 us  [exchange(): return lax.all_to_all(copies, axes, 0, 0, tiled=True)]
    all_to_all x7 -> x6, waiting for transfers between devices: 78.1 us -> 34.8 us  [exchange(): return lax.all_to_all(copies, axes, 0, 0, tiled=True)]
    pallas_call x1, Pallas kernels: 33.9 us -> 17.8 us  [per_device(): call(back_depth_kernel, [MAP_BLOCK, MAP_BLOCK, MAP_BLOCK, peer_block(peer...]
    ppermute x0 -> x3, starting transfers between devices: none -> 13.9 us  [swap(): lax.ppermute(rows, 'core', [(i, i ^ 1) for i in range(lax.axis_size('core...]
    pallas_call x0 -> x2, Pallas kernels: none -> 13.6 us  [the longest x1 10.7 us: per_device(): call(kernel_grad_kernel, [MAP_BLOCK, MAP_BLOCK, lane_block(8)], [(lane_bl...]
    pallas_call x1, Pallas kernels: 16.3 us -> 6.42 us  [per_device(): call(back_project_kernel, [MAP_BLOCK, whole((peers, 4, C)), lane_block(TA...]
    unnamed x45 -> x58, local copies, waits for them, and re-layouts: 20.7 us -> 29.5 us
    pallas_call x1, Pallas kernels: 12.7 us -> 5.02 us  [per_device(): call(project_kernel, [MAP_BLOCK, peer_block(peers), lane_block(TABLE), wh...]
  transfers between devices with their start and end apart: 7 -> 9, of which waited for: 4 -> 6; matrix products, arithmetic and copies ran while one was open for 1% -> 2% of each run, Pallas kernels for 18% -> 9%
where the time goes in v3:
time: 314 us; the launch traced here: 313 us
  blocking collectives  87.1 us (28%)
  Pallas kernels  73.4 us (23%)
  starting transfers between devices  69.7 us (22%)
  waiting for transfers between devices  39.3 us (13%)
  local copies, waits for them, and re-layouts  32.4 us (10%)
  other arithmetic  9.65 us (3%)
    all_to_all x2, blocking collectives, exchange(): return lax.all_to_all(copies, axes, 0, 0, tiled=True)  87.1 us
    all_to_all x6, starting transfers between devices, exchange(): return lax.all_to_all(copies, axes, 0, 0, tiled=True)  55.9 us
    all_to_all x6, waiting for transfers between devices, exchange(): return lax.all_to_all(copies, axes, 0, 0, tiled=True)  34.8 us
    unnamed x58, local copies, waits for them, and re-layouts  29.5 us
    pallas_call x1, Pallas kernels, per_device(): call(back_depth_kernel, [MAP_BLOCK, MAP_BLOCK, MAP_BLOCK, peer_block(peer...  17.8 us
    pallas_call x1, Pallas kernels, per_device(): call(forward_kernel, [xpad_spec, w_spec, peer_block(peers), lane_block(TA...  15.6 us
    ppermute x3, starting transfers between devices, swap(): lax.ppermute(rows, 'core', [(i, i ^ 1) for i in range(lax.axis_size('core...  13.9 us
    pallas_call x1, Pallas kernels, per_device(): call(kernel_grad_kernel, [MAP_BLOCK, MAP_BLOCK, lane_block(8)], [(lane_bl...  10.7 us
  transfers between devices with their start and end apart: 9, of which 6 were waited for; matrix products, arithmetic and copies ran while one was open for 2% of the time, Pallas kernels for 9%

profile of v3, /device:TPU:1, one launch (start us, length us, event | category | flops | bytes accessed | tf_op | source)
XLA Modules:
  0.0 312.7 jit_solution(10565246713874469654)
XLA Ops:
  2.8 5.1 %shard_map.254 = (bf16[928,176]{1,0:T(8,128)(2,1)S(1)}, f32[32,2,1152]{2,1,0:T(2,128)}) custom-call(bf16[29,29,176]{2,1,0:T(8,128)(2,1)S(1)} %bitcast.35, bf16[176,1152]{1,0:T(8,128)(2,1)S(1)} %pad.37.w_ref), custom_call_target="tpu_custom_call" | custom-call | flops 376307712 | bytes 12582912 | tf_op jit(solution)/shard_map/pallas_call | solution.py:725
  7.9 10.6 %all-to-all-start = ((f32[32,2,1152]{2,1,0:T(2,128)}), f32[32,2,1152]{2,1,0:T(2,128)S(1)}, u32[]{:S(2)}, u32[]{:S(2)}) async-start(f32[32,2,1152]{2,1,0:T(2,128)} %get-tuple-element.58), calls=%async_computation | async-start | bytes 589824 | tf_op jit(solution)/shard_map/all_to_all | solution.py:647
  18.7 9.8 %all-to-all-done.gathered_ref = f32[32,2,1152]{2,1,0:T(2,128)S(1)} async-done(((f32[32,2,1152]{2,1,0:T(2,128)}), f32[32,2,1152]{2,1,0:T(2,128)S(1)}, u32[]{:S(2)}, u32[]{:S(2)}) %all-to-all-start) | async-done | bytes 294944 | tf_op jit(solution)/shard_map/all_to_all | solution.py:647
  28.5 15.6 %shard_map.255 = (f32[9,928,128]{2,1,0:T(8,128)S(1)}, f32[32,2,1152]{2,1,0:T(2,128)}, f32[8,1152]{1,0:T(8,128)S(1)}) custom-call(bf16[928,176]{1,0:T(8,128)(2,1)S(1)} %get-tuple-element.57.xpad_ref, bf16[176,1152]{1,0:T(8,128)(2,1)S(1)} %pad.37.w_ref, f32[32,2,1152]{2,1,0:T(2,128)S(1)} %all-to-all-done.gathered_ref, f32[32,1152]{1,0:T(8,128)S(1)} %pad.38.table_ref), custom_call_target="tpu_custom_call" | custom-call | flops 53452800 | bytes 12582912 | tf_op jit(solution)/shard_map/pallas_call | solution.py:733
  46.1 6.9 %all-to-all-start.1 = ((f32[32,2,1152]{2,1,0:T(2,128)}), f32[32,2,1152]{2,1,0:T(2,128)S(1)}, u32[]{:S(2)}, u32[]{:S(2)}) async-start(f32[32,2,1152]{2,1,0:T(2,128)} %get-tuple-element.60), calls=%async_computation.1 | async-start | bytes 589824 | tf_op jit(solution)/shard_map/all_to_all | solution.py:647
  54.4 8.4 %all-to-all-done.1.gathered_ref = f32[32,2,1152]{2,1,0:T(2,128)S(1)} async-done(((f32[32,2,1152]{2,1,0:T(2,128)}), f32[32,2,1152]{2,1,0:T(2,128)S(1)}, u32[]{:S(2)}, u32[]{:S(2)}) %all-to-all-start.1) | async-done | bytes 294944 | tf_op jit(solution)/shard_map/all_to_all | solution.py:647
  65.1 5.0 %shard_map.256 = (f32[8,1152]{1,0:T(8,128)S(1)}, f32[928,176]{1,0:T(8,128)S(1)}, bf16[928,176]{1,0:T(8,128)(2,1)S(1)}, f32[8,1152]{1,0:T(8,128)S(1)}, f32[2,48,128]{2,1,0:T(8,128)S(1)}, /*index=5*/f32[32,4,176]{2,1,0:T(4,128)}) custom-call(f32[9,928,128]{2,1,0:T(8,128)S(1)} %copy-done.1, f32[32,2,1152]{2,1,0:T(2,128)S(1)} %all-to-all-done.1.gathered_ref, ...), custom_call_target="tpu_custom_call" | custom-call | flops 376307712 | bytes 12582912 | tf_op jit(solution)/shard_map/pallas_call | solution.py:741
  71.1 6.4 %all-to-all-start.2 = ((f32[32,4,176]{2,1,0:T(4,128)}), f32[32,4,176]{2,1,0:T(4,128)S(1)}, u32[]{:S(2)}, u32[]{:S(2)}) async-start(f32[32,4,176]{2,1,0:T(4,128)} %get-tuple-element.61), calls=%async_computation.2 | async-start | bytes 262144 | tf_op jit(solution)/shard_map/all_to_all | solution.py:647
  78.5 8.1 %all-to-all-done.2.gathered_ref = f32[32,4,176]{2,1,0:T(4,128)S(1)} async-done(((f32[32,4,176]{2,1,0:T(4,128)}), f32[32,4,176]{2,1,0:T(4,128)S(1)}, u32[]{:S(2)}, u32[]{:S(2)}) %all-to-all-start.2) | async-done | bytes 90144 | tf_op jit(solution)/shard_map/all_to_all | solution.py:647
  90.1 6.4 %shard_map.257 = (f32[9,928,128]{2,1,0:T(8,128)S(1)}, f32[9,928,128]{2,1,0:T(8,128)S(1)}, bf16[9,928,128]{2,1,0:T(8,128)(2,1)S(1)}, bf16[928,176]{1,0:T(8,128)(2...) custom-call(f32[9,928,128]{2,1,0:T(8,128)S(1)} %copy-done.2, ...), custom_call_target="tpu_custom_call" | custom-call | flops 752615424 | bytes 12582912 | tf_op jit(solution)/shard_map/pallas_call | solution.py:770
  96.5 2.9 shard_map.258
  101.0 5.4 %collective-permute-start = (f32[256,2,4,128]{3,2,1,0:T(4,128)}, f32[256,2,4,128]{3,2,1,0:T(4,128)}, u32[]{:S(2)}, u32[]{:S(2)}) collective-permute-start(f32[256,2,4,128]{3,2,1,0:T(4,128)} %bitcast.7), channel_id=1, source_target_pairs={{0,1},{1,0},{2,3},{3,2},{4,5},{5,4},{6,7},{7,6},{8,9},{9,8},{10,11... | collective-permute-start | bytes 3145736 | tf_op jit(solution)/shard_map/ppermute | solution.py:651
  106.4 3.9 %all-to-all-start.3 = ((f32[32,2,1152]{2,1,0:T(2,128)}), f32[32,2,1152]{2,1,0:T(2,128)S(1)}, u32[]{:S(2)}, u32[]{:S(2)}) async-start(f32[32,2,1152]{2,1,0:T(2,128)} %get-tuple-element.73), calls=%async_computation.3 | async-start | bytes 589824 | tf_op jit(solution)/shard_map/all_to_all | solution.py:647
  112.8 8.5 %all-to-all-done.3.gathered_ref = f32[32,2,1152]{2,1,0:T(2,128)S(1)} async-done(((f32[32,2,1152]{2,1,0:T(2,128)}), f32[32,2,1152]{2,1,0:T(2,128)S(1)}, u32[]{:S(2)}, u32[]{:S(2)}) %all-to-all-start.3) | async-done | bytes 294944 | tf_op jit(solution)/shard_map/all_to_all | solution.py:647
  121.3 19.3 %all-to-all-start.4 = ((f32[256,2,4,128]{3,2,1,0:T(4,128)}), f32[256,2,4,128]{3,2,1,0:T(4,128)S(1)}, u32[]{:S(2)}, u32[]{:S(2)}) async-start(f32[256,2,4,128]{3,2,1,0:T(4,128)} %add.24), calls=%async_computation.4 | async-start | bytes 2097152 | tf_op jit(solution)/shard_map/all_to_all | solution.py:647
  147.2 17.8 %shard_map.259 = (f32[9,928,128]{2,1,0:T(8,128)S(1)}, f32[32,2,1152]{2,1,0:T(2,128)}, f32[8,1152]{1,0:T(8,128)S(1)}, bf16[9,928,128]{2,1,0:T(8,128)(2,1)S(1)}, f32[9,928,128]{2,1,0:T(8,128)S(1)}) custom-call(f32[9,928,128]{2,1,0:T(8,128)S(1)} %copy-done.3, f32[9,928,128]{2,1,0:T(8,128)S(1)} %copy-done.5, f32[9,928,128]{2,1,0:T(8,128)S(1)} %copy-done.7, ...), custom_call_target="tpu_custom_call" | custom-call | flops 106905600 | bytes 12582912 | tf_op jit(solution)/shard_map/pallas_call | solution.py:829
  170.7 8.8 %all-to-all-start.5 = ((f32[32,2,1152]{2,1,0:T(2,128)}), f32[32,2,1152]{2,1,0:T(2,128)S(1)}, u32[]{:S(2)}, u32[]{:S(2)}) async-start(f32[32,2,1152]{2,1,0:T(2,128)} %get-tuple-element.80), calls=%async_computation.5 | async-start | bytes 589824 | tf_op jit(solution)/shard_map/all_to_all | solution.py:647
  184.8 10.7 %shard_map.260.sums_ref = f32[32,1152]{1,0:T(8,128)S(1)} custom-call(bf16[9,928,128]{2,1,0:T(8,128)(2,1)S(1)} %copy-done.13, f32[9,928,128]{2,1,0:T(8,128)S(1)} %copy-done.11, f32[8,1152]{1,0:T(8,128)S(1)} %get-tuple-element.83.sums_ref), custom_call_target="tpu_custom_call" | custom-call | flops 53452800 | bytes 12582912 | tf_op jit(solution)/shard_map/pallas_call | solution.py:856
  197.8 7.5 %shard_map.261 = (bf16[29,29,176]{2,1,0:T(8,128)(2,1)}, f32[2048,128]{1,0:T(8,128)S(1)}) custom-call(f32[9,928,128]{2,1,0:T(8,128)S(1)} %copy-done.9, f32[32,2,1152]{2,1,0:T(2,128)S(1)} %all-to-all-done.5.gathered_ref, f32[32,1152]{1,0:T(8,128)S(1)} %pad.38.table_ref, f32[8,1152]{1,0:T(8,128)S(1)} %get-tuple-element.75.moment_one_ref.moment_ref, ...), custom_call_target="tpu_custom_call" | custom-call | flops 1128923136 | bytes 12582912 | tf_op jit(solution)/shard_map/pallas_call | solution.py:863
  205.4 3.4 %collective-permute-start.1 = (f32[256,1,4,128]{3,2,1,0:T(4,128)S(1)}, f32[256,1,4,128]{3,2,1,0:T(4,128)S(1)}, u32[]{:S(2)}, u32[]{:S(2)}) collective-permute-start(f32[256,1,4,128]{3,2,1,0:T(4,128)S(1)} %bitcast.40), channel_id=1, source_target_pairs={{0,1},{1,0},{2,3},{3,2},{4,5},{5,4},{6,7},{7,6},{8,9},{9,8},{10,11... | collective-permute-start | bytes 1572872 | tf_op jit(solution)/shard_map/ppermute | solution.py:651
  210.4 36.7 %all_to_all.40 = f32[256,1,4,128]{3,2,1,0:T(4,128)S(1)} all-to-all(f32[256,1,4,128]{3,2,1,0:T(4,128)S(1)} %add.25), channel_id=1, replica_groups=mesh['x'=4,'y'=8,'z'=8,'core'=2] {'x','y','z'}, dimensions={0} | all-to-all | bytes 1048576 | tf_op jit(solution)/shard_map/all_to_all | solution.py:647
  247.7 50.4 %all_to_all.41 = f32[256,3,4,128]{3,2,1,0:T(4,128)S(1)} all-to-all(f32[256,3,4,128]{3,2,1,0:T(4,128)S(1)} %broadcast_in_dim.41), channel_id=1, replica_groups=mesh['x'=4,'y'=8,'z'=8,'core'=2] {'x','y','z'}, dimensions={0} | all-to-all | bytes 3145728 | tf_op jit(solution)/shard_map/all_to_all | solution.py:647
  298.0 5.0 %collective-permute-start.2 = (f32[256,3,4,128]{3,2,1,0:T(4,128)S(1)}, f32[256,3,4,128]{3,2,1,0:T(4,128)S(1)}, u32[]{:S(2)}, u32[]{:S(2)}) collective-permute-start(f32[256,3,4,128]{3,2,1,0:T(4,128)S(1)} %all_to_all.41), channel_id=1, source_target_pairs={{0,1},{1,0},{2,3},{3,2},{4,5},{5,4},{6,7},{7,6},{8,9},{9,8},{10,11... | collective-permute-start | bytes 4718600 | tf_op jit(solution)/shard_map/ppermute | solution.py:651
  303.1 3.0 collective-permute-done.2
  (96 shorter events, 45.9 us)
Async XLA Ops:
  0.6 17.9 %copy-start.22 = (f32[1056]{0:T(1024)S(1)}, f32[1056]{0:T(1024)}, u32[]{:S(2)}) copy-start(f32[1056]{0:T(1024)} %param.18) | copy-start | bytes 12676
  0.7 17.9 %copy-start.23 = (f32[1056]{0:T(1024)S(1)}, f32[1056]{0:T(1024)}, u32[]{:S(2)}) copy-start(f32[1056]{0:T(1024)} %param.19) | copy-start | bytes 12676
  0.7 17.9 %copy-start.24 = (f32[1056]{0:T(1024)S(1)}, f32[1056]{0:T(1024)}, u32[]{:S(2)}) copy-start(f32[1056]{0:T(1024)} %param.21) | copy-start | bytes 12676
  0.7 17.9 %copy-start.25 = (f32[1056]{0:T(1024)S(1)}, f32[1056]{0:T(1024)}, u32[]{:S(2)}) copy-start(f32[1056]{0:T(1024)} %param.22) | copy-start | bytes 12676
  0.7 17.9 %copy-start.21 = (bf16[25,1056]{1,0:T(8,128)(2,1)S(1)}, bf16[25,1056]{1,0:T(8,128)(2,1)}, u32[]{:S(2)}) copy-start(bf16[25,1056]{1,0:T(8,128)(2,1)} %param.20) | copy-start | bytes 158404
  7.9 45.1 %copy-start.20 = (bf16[1056,176]{0,1:T(8,128)(2,1)S(1)}, bf16[1056,176]{0,1:T(8,128)(2,1)}, u32[]{:S(2)}) copy-start(bf16[1056,176]{0,1:T(8,128)(2,1)} %param.27) | copy-start | bytes 1115140
  7.9 20.6 %all-to-all-start = ((f32[32,2,1152]{2,1,0:T(2,128)}), f32[32,2,1152]{2,1,0:T(2,128)S(1)}, u32[]{:S(2)}, u32[]{:S(2)}) async-start(f32[32,2,1152]{2,1,0:T(2,128)} %get-tuple-element.58), calls=%async_computation | async-start | bytes 589824 | tf_op jit(solution)/shard_map/all_to_all | solution.py:647
  28.5 24.8 %copy-start.27 = (f32[44]{0:T(128)S(1)}, f32[44]{0:T(128)}, u32[]{:S(2)}) copy-start(f32[44]{0:T(128)} %param.24) | copy-start | bytes 532
  28.5 24.9 %copy-start.26 = (f32[1056]{0:T(1024)S(1)}, f32[1056]{0:T(1024)}, u32[]{:S(2)}) copy-start(f32[1056]{0:T(1024)} %param.26) | copy-start | bytes 12676
  46.1 16.7 %copy-start.16 = (bf16[1,1,29,29,176]{4,3,2,1,0:T(8,128)(2,1)S(1)}, bf16[1,1,29,29,176]{4,3,2,1,0:T(8,128)(2,1)}, u32[]{:S(2)}) copy-start(bf16[1,1,29,29,176]{4,3,2,1,0:T(8,128)(2,1)} %param.16) | copy-start | bytes 888100
  46.1 16.7 %all-to-all-start.1 = ((f32[32,2,1152]{2,1,0:T(2,128)}), f32[32,2,1152]{2,1,0:T(2,128)S(1)}, u32[]{:S(2)}, u32[]{:S(2)}) async-start(f32[32,2,1152]{2,1,0:T(2,128)} %get-tuple-element.60), calls=%async_computation.1 | async-start | bytes 589824 | tf_op jit(solution)/shard_map/all_to_all | solution.py:647
  62.8 2.2 copy-start.1
  65.1 21.6 %copy-start.17 = (f32[176]{0:T(256)S(1)}, f32[176]{0:T(256)}, u32[]{:S(2)}) copy-start(f32[176]{0:T(256)} %param.28) | copy-start | bytes 2116
  71.1 15.6 %all-to-all-start.2 = ((f32[32,4,176]{2,1,0:T(4,128)}), f32[32,4,176]{2,1,0:T(4,128)S(1)}, u32[]{:S(2)}, u32[]{:S(2)}) async-start(f32[32,4,176]{2,1,0:T(4,128)} %get-tuple-element.61), calls=%async_computation.2 | async-start | bytes 262144 | tf_op jit(solution)/shard_map/all_to_all | solution.py:647
  86.7 2.2 copy-start.2
  90.1 6.4 %copy-start.18 = (f32[1,131072]{1,0:T(1,128)S(1)}, f32[1,131072]{1,0:T(1,128)}, u32[]{:S(2)}) copy-start(f32[1,131072]{1,0:T(1,128)} %param.29) | copy-start | bytes 1572868
  96.5 3.0 copy-start.4
  96.5 3.3 %copy-start.6 = (f32[9,928,128]{2,1,0:T(8,128)}, f32[9,928,128]{2,1,0:T(8,128)S(1)}, u32[]{:S(2)}) copy-start(f32[9,928,128]{2,1,0:T(8,128)S(1)} %get-tuple-element.68.slope_ref) | copy-start | bytes 12828676
  101.0 9.3 %collective-permute-start = (f32[256,2,4,128]{3,2,1,0:T(4,128)}, f32[256,2,4,128]{3,2,1,0:T(4,128)}, u32[]{:S(2)}, u32[]{:S(2)}) collective-permute-start(f32[256,2,4,128]{3,2,1,0:T(4,128)} %bitcast.7), channel_id=1, source_target_pairs={{0,1},{1,0},{2,3},{3,2},{4,5},{5,4},{6,7},{7,6},{8,9},{9,8},{10,11... | collective-permute-start | bytes 3145736 | tf_op jit(solution)/shard_map/ppermute | solution.py:651
  106.4 14.9 %all-to-all-start.3 = ((f32[32,2,1152]{2,1,0:T(2,128)}), f32[32,2,1152]{2,1,0:T(2,128)S(1)}, u32[]{:S(2)}, u32[]{:S(2)}) async-start(f32[32,2,1152]{2,1,0:T(2,128)} %get-tuple-element.73), calls=%async_computation.3 | async-start | bytes 589824 | tf_op jit(solution)/shard_map/all_to_all | solution.py:647
  121.3 49.1 %all-to-all-start.4 = ((f32[256,2,4,128]{3,2,1,0:T(4,128)}), f32[256,2,4,128]{3,2,1,0:T(4,128)S(1)}, u32[]{:S(2)}, u32[]{:S(2)}) async-start(f32[256,2,4,128]{3,2,1,0:T(4,128)} %add.24), calls=%async_computation.4 | async-start | bytes 2097152 | tf_op jit(solution)/shard_map/all_to_all | solution.py:647
  170.7 24.8 %all-to-all-start.5 = ((f32[32,2,1152]{2,1,0:T(2,128)}), f32[32,2,1152]{2,1,0:T(2,128)S(1)}, u32[]{:S(2)}, u32[]{:S(2)}) async-start(f32[32,2,1152]{2,1,0:T(2,128)} %get-tuple-element.80), calls=%async_computation.5 | async-start | bytes 589824 | tf_op jit(solution)/shard_map/all_to_all | solution.py:647
  205.4 4.9 %collective-permute-start.1 = (f32[256,1,4,128]{3,2,1,0:T(4,128)S(1)}, f32[256,1,4,128]{3,2,1,0:T(4,128)S(1)}, u32[]{:S(2)}, u32[]{:S(2)}) collective-permute-start(f32[256,1,4,128]{3,2,1,0:T(4,128)S(1)} %bitcast.40), channel_id=1, source_target_pairs={{0,1},{1,0},{2,3},{3,2},{4,5},{5,4},{6,7},{7,6},{8,9},{9,8},{10,11... | collective-permute-start | bytes 1572872 | tf_op jit(solution)/shard_map/ppermute | solution.py:651
  298.0 8.0 %collective-permute-start.2 = (f32[256,3,4,128]{3,2,1,0:T(4,128)S(1)}, f32[256,3,4,128]{3,2,1,0:T(4,128)S(1)}, u32[]{:S(2)}, u32[]{:S(2)}) collective-permute-start(f32[256,3,4,128]{3,2,1,0:T(4,128)S(1)} %all_to_all.41), channel_id=1, source_target_pairs={{0,1},{1,0},{2,3},{3,2},{4,5},{5,4},{6,7},{7,6},{8,9},{9,8},{10,11... | collective-permute-start | bytes 4718600 | tf_op jit(solution)/shard_map/ppermute | solution.py:651
  (13 other events, 23.3 us)

commit v4 on v3

--- a/solution.py
+++ b/solution.py
@@ -12,7 +12,7 @@
 SHAPE = (4, 8, 8, 2)
 AXES = ("x", "y", "z", "core")
 GROUP = ("x", "y")
-CHIPS = ("x", "y", "z")
+PLANE = ("y", "z")
 SIDE = 29
 WIDE = 32
 ROWS = SIDE * WIDE
@@ -33,7 +33,6 @@
 EARLY_ROWS = 4096
 LATE = C + TABLE
 LATE_ROWS = 2048
-PIECE = 4
 F32 = jnp.float32
 BF16 = jnp.bfloat16
 
@@ -598,7 +597,7 @@
     return pl.pallas_call(
         functools.partial(kernel, scale),
         out_shape=tuple(f32(*shape) for shape in shapes),
-        compiler_params=pltpu.CompilerParams(vmem_limit_bytes=20 * 2**20),
+        compiler_params=pltpu.CompilerParams(vmem_limit_bytes=56 * 2**20),
         cost_estimate=pl.CostEstimate(
             flops=rows.size, bytes_accessed=8 * rows.size, transcendentals=0
         ),
@@ -636,7 +635,7 @@
         out_specs=tuple(spec for spec, _ in outs),
         out_shape=tuple(shape for _, shape in outs),
         scratch_shapes=scratch,
-        compiler_params=pltpu.CompilerParams(vmem_limit_bytes=20 * 2**20),
+        compiler_params=pltpu.CompilerParams(vmem_limit_bytes=56 * 2**20),
         cost_estimate=pl.CostEstimate(
             flops=flops, bytes_accessed=12 * 2**20, transcendentals=ROWS * PADDED
         ),
@@ -652,21 +651,22 @@
 
 
 def pair_sum(rows):
-    chips = lax.axis_size(CHIPS)
+    plane = lax.axis_size(PLANE)
     near = lax.axis_index("core") == 0
-    halves = rows.reshape(2, chips, -1, PIECE, LANES)
+    halves = rows.reshape(2, plane, -1, LANES)
     mine = jnp.where(near, halves[0], halves[1])
     return mine + swap(jnp.where(near, halves[1], halves[0]))
 
 
-def chip_sum(mine):
-    return jnp.sum(exchange(mine, CHIPS), axis=0)
+def plane_sum(mine):
+    return jnp.sum(exchange(mine, PLANE), axis=0)
 
 
 def all_parts(mine):
-    chips = lax.axis_size(CHIPS)
+    plane, line = lax.axis_size(PLANE), lax.axis_size("x")
     near = lax.axis_index("core") == 0
-    half = exchange(jnp.broadcast_to(mine[None], (chips,) + mine.shape), CHIPS)
+    mine = jnp.sum(exchange(jnp.broadcast_to(mine[None], (line,) + mine.shape), "x"), axis=0)
+    half = exchange(jnp.broadcast_to(mine[None], (plane,) + mine.shape), PLANE)
     other = swap(half)
     return jnp.stack([jnp.where(near, half, other), jnp.where(near, other, half)])
 
@@ -825,7 +825,7 @@
         10 * matmul,
     )(gpp, hidden, rows, reduce, vector, column, upper_grads[0].reshape(-1, LANES))
     early, gathered = tie(pair_sum(early), gathered)
-    early = chip_sum(early)
+    early = plane_sum(early)
     grad_one, stat, sums, field, back = call(
         back_depth_kernel,
         [
@@ -882,7 +882,7 @@
         3 * matmul,
     )(grad_one, gathered, table, moment_one, xpad, wexp, sums, cpad, xpad.T, wexp_turn)
 
-    late = chip_sum(pair_sum(late))
+    late = plane_sum(pair_sum(late))
     split = early.shape[0]
     full = all_parts(jnp.concatenate([early, late]))
     early = full[:, :, :split].reshape(EARLY_ROWS, LANES)

time: 314 us -> 322 us (1.025)
  Pallas kernels: 73.4 us -> 104 us
  local copies, waits for them, and re-layouts: 32.4 us -> 10.2 us
  blocking collectives: 87.1 us -> 77.3 us
  other arithmetic: 9.65 us -> 15.8 us
  waiting for transfers between devices: 39.3 us -> 44.5 us
    unnamed x58 -> x36, local copies, waits for them, and re-layouts: 29.5 us -> 2.57 us
    all_to_all x2 -> x3, blocking collectives: 87.1 us -> 77.3 us  [exchange(): return lax.all_to_all(copies, axes, 0, 0, tiled=True)]
    all_to_all x6, starting transfers between devices: 55.9 us -> 49.7 us  [exchange(): return lax.all_to_all(copies, axes, 0, 0, tiled=True)]
    pallas_call x1, Pallas kernels: 6.42 us -> 12.3 us  [per_device(): call(back_project_kernel, [MAP_BLOCK, whole((peers, 4, C)), lane_block(TA...]
    pallas_call x1, Pallas kernels: 2.94 us -> 8.21 us  [per_device(): call(early_kernel, [whole((ROWS, C)), MAP_BLOCK, lane_block(8), whole((SE...]
    pallas_call x1, Pallas kernels: 5.02 us -> 10.3 us  [per_device(): call(project_kernel, [MAP_BLOCK, peer_block(peers), lane_block(TABLE), wh...]
    all_to_all x6, waiting for transfers between devices: 34.8 us -> 39.9 us  [exchange(): return lax.all_to_all(copies, axes, 0, 0, tiled=True)]
    pallas_call x1, Pallas kernels: 7.52 us -> 11.1 us  [per_device(): call(back_expand_kernel, [MAP_BLOCK, peer_block(peers), lane_block(TABLE)...]
  transfers between devices with their start and end apart: 9 -> 9, of which waited for: 6 -> 7; matrix products, arithmetic and copies ran while one was open for 2% -> 3% of each run, Pallas kernels for 9% -> 10%
where the time goes in v4:
time: 322 us; the launch traced here: 319 us
  Pallas kernels  104 us (32%)
  blocking collectives  77.3 us (24%)
  starting transfers between devices  66.9 us (21%)
  waiting for transfers between devices  44.5 us (14%)
  other arithmetic  15.8 us (5%)
  local copies, waits for them, and re-layouts  10.2 us (3%)
    all_to_all x3, blocking collectives, exchange(): return lax.all_to_all(copies, axes, 0, 0, tiled=True)  77.3 us
    all_to_all x6, starting transfers between devices, exchange(): return lax.all_to_all(copies, axes, 0, 0, tiled=True)  49.7 us
    all_to_all x6, waiting for transfers between devices, exchange(): return lax.all_to_all(copies, axes, 0, 0, tiled=True)  39.9 us
    pallas_call x1, Pallas kernels, per_device(): call(back_depth_kernel, [MAP_BLOCK, MAP_BLOCK, MAP_BLOCK, peer_block(peer...  20.1 us
    ppermute x3, starting transfers between devices, swap(): lax.ppermute(rows, 'core', [(i, i ^ 1) for i in range(lax.axis_size('core...  17.2 us
    pallas_call x1, Pallas kernels, per_device(): call(forward_kernel, [xpad_spec, w_spec, peer_block(peers), lane_block(TA...  16.8 us
    pallas_call x1, Pallas kernels, per_device(): call(kernel_grad_kernel, [MAP_BLOCK, MAP_BLOCK, lane_block(8)], [(lane_bl...  12.7 us
    pallas_call x1, Pallas kernels, per_device(): call(back_project_kernel, [MAP_BLOCK, whole((peers, 4, C)), lane_block(TA...  12.3 us
  transfers between devices with their start and end apart: 9, of which 7 were waited for; matrix products, arithmetic and copies ran while one was open for 3% of the time, Pallas kernels for 10%

profile of v4, /device:TPU:1, one launch (start us, length us, event | category | flops | bytes accessed | tf_op | source)
XLA Modules:
  0.0 319.2 jit_solution(5078097733723611986)
XLA Ops:
  2.6 6.9 %shard_map.254 = (bf16[928,176]{1,0:T(8,128)(2,1)}, f32[32,2,1152]{2,1,0:T(2,128)}) custom-call(bf16[29,29,176]{2,1,0:T(8,128)(2,1)} %bitcast.39, bf16[176,1152]{1,0:T(8,128)(2,1)} %pad.37.w_ref), custom_call_target="tpu_custom_call" | custom-call | flops 376307712 | bytes 12582912 | tf_op jit(solution)/shard_map/pallas_call | solution.py:725
  9.5 10.6 %all-to-all-start = ((f32[32,2,1152]{2,1,0:T(2,128)}), f32[32,2,1152]{2,1,0:T(2,128)S(1)}, u32[]{:S(2)}, u32[]{:S(2)}) async-start(f32[32,2,1152]{2,1,0:T(2,128)} %get-tuple-element.58), calls=%async_computation | async-start | bytes 589824 | tf_op jit(solution)/shard_map/all_to_all | solution.py:646
  20.9 9.1 %all-to-all-done.gathered_ref = f32[32,2,1152]{2,1,0:T(2,128)S(1)} async-done(((f32[32,2,1152]{2,1,0:T(2,128)}), f32[32,2,1152]{2,1,0:T(2,128)S(1)}, u32[]{:S(2)}, u32[]{:S(2)}) %all-to-all-start) | async-done | bytes 294944 | tf_op jit(solution)/shard_map/all_to_all | solution.py:646
  30.8 16.8 %shard_map.255 = (f32[9,928,128]{2,1,0:T(8,128)}, f32[32,2,1152]{2,1,0:T(2,128)}, f32[8,1152]{1,0:T(8,128)}) custom-call(bf16[928,176]{1,0:T(8,128)(2,1)} %get-tuple-element.57.xpad_ref, bf16[176,1152]{1,0:T(8,128)(2,1)} %pad.37.w_ref, f32[32,2,1152]{2,1,0:T(2,128)} %copy-done.7, f32[32,1152]{1,0:T(8,128)} %pad.38.table_ref), custom_call_target="tpu_custom_call" | custom-call | flops 53452800 | bytes 12582912 | tf_op jit(solution)/shard_map/pallas_call | solution.py:733
  47.6 6.5 %all-to-all-start.1 = ((f32[32,2,1152]{2,1,0:T(2,128)}), f32[32,2,1152]{2,1,0:T(2,128)S(1)}, u32[]{:S(2)}, u32[]{:S(2)}) async-start(f32[32,2,1152]{2,1,0:T(2,128)} %get-tuple-element.60), calls=%async_computation.1 | async-start | bytes 589824 | tf_op jit(solution)/shard_map/all_to_all | solution.py:646
  56.7 7.3 %all-to-all-done.1.gathered_ref = f32[32,2,1152]{2,1,0:T(2,128)S(1)} async-done(((f32[32,2,1152]{2,1,0:T(2,128)}), f32[32,2,1152]{2,1,0:T(2,128)S(1)}, u32[]{:S(2)}, u32[]{:S(2)}) %all-to-all-start.1) | async-done | bytes 294944 | tf_op jit(solution)/shard_map/all_to_all | solution.py:646
  64.7 10.3 %shard_map.256 = (f32[8,1152]{1,0:T(8,128)}, f32[928,176]{1,0:T(8,128)}, bf16[928,176]{1,0:T(8,128)(2,1)}, f32[8,1152]{1,0:T(8,128)}, f32[2,48,128]{2,1,0:T(8,128)}, /*index=5*/f32[32,4,176]{2,1,0:T(4,128)}) custom-call(f32[9,928,128]{2,1,0:T(8,128)} %get-tuple-element.59.depth_ref, f32[32,2,1152]{2,1,0:T(2,128)} %copy-done.5, f32[32,1152]{1,0:T(8,128)} %pad.38.table_ref, ...), custom_call_target="tpu_custom_call" | custom-call | flops 376307712 | bytes 12582912 | tf_op jit(solution)/shard_map/pallas_call | solution.py:741
  75.0 5.7 %all-to-all-start.2 = ((f32[32,4,176]{2,1,0:T(4,128)}), f32[32,4,176]{2,1,0:T(4,128)S(1)}, u32[]{:S(2)}, u32[]{:S(2)}) async-start(f32[32,4,176]{2,1,0:T(4,128)} %get-tuple-element.61), calls=%async_computation.2 | async-start | bytes 262144 | tf_op jit(solution)/shard_map/all_to_all | solution.py:646
  81.5 8.4 %all-to-all-done.2.gathered_ref = f32[32,4,176]{2,1,0:T(4,128)S(1)} async-done(((f32[32,4,176]{2,1,0:T(4,128)}), f32[32,4,176]{2,1,0:T(4,128)S(1)}, u32[]{:S(2)}, u32[]{:S(2)}) %all-to-all-start.2) | async-done | bytes 90144 | tf_op jit(solution)/shard_map/all_to_all | solution.py:646
  90.5 12.3 %shard_map.257 = (f32[9,928,128]{2,1,0:T(8,128)}, f32[9,928,128]{2,1,0:T(8,128)}, bf16[9,928,128]{2,1,0:T(8,128)(2,1)}, bf16[928,176]{1,0:T(8,128)(2,1)}, f32[8,...) custom-call(f32[9,928,128]{2,1,0:T(8,128)} %get-tuple-element.59.depth_ref, f32[32,4,176]{2,1,0:T(4,128)} %copy-done.6, ...), custom_call_target="tpu_custom_call" | custom-call | flops 752615424 | bytes 12582912 | tf_op jit(solution)/shard_map/pallas_call | solution.py:770
  102.9 8.2 %shard_map.258 = f32[4096,128]{1,0:T(8,128)} custom-call(bf16[928,176]{1,0:T(8,128)(2,1)} %get-tuple-element.69.gpp_ref, bf16[9,928,128]{2,1,0:T(8,128)(2,1)} %get-tuple-element.70.hidden_ref, f32[8,1152]{1,0:T(8,128)} %get-tuple-element.71.row_ref.pooled_ref, f32[48,128]{1,0:T(8,128)} %get-tuple-element.72.reduce_ref, ...), custom_call_target="tpu_custom_call" | custom-call | flops 3763077120 | bytes 12582912 | tf_op jit(solution)/shard_map/pallas_call | solution.py:812
  112.8 6.0 %collective-permute-start = (f32[64,32,128]{2,1,0:T(8,128)S(1)}, f32[64,32,128]{2,1,0:T(8,128)}, u32[]{:S(2)}, u32[]{:S(2)}) collective-permute-start(f32[64,32,128]{2,1,0:T(8,128)S(1)} %bitcast.31), channel_id=1, source_target_pairs={{0,1},{1,0},{2,3},{3,2},{4,5},{5,4},{6,7},{7,6},{8,9},{9,8},{10,11... | collective-permute-start | bytes 3145736 | tf_op jit(solution)/shard_map/ppermute | solution.py:650
  125.1 8.6 %all-to-all-done.3.gathered_ref = f32[32,2,1152]{2,1,0:T(2,128)S(1)} async-done(((f32[32,2,1152]{2,1,0:T(2,128)}), f32[32,2,1152]{2,1,0:T(2,128)S(1)}, u32[]{:S(2)}, u32[]{:S(2)}) %all-to-all-start.3) | async-done | bytes 294944 | tf_op jit(solution)/shard_map/all_to_all | solution.py:646
  133.7 15.1 %all-to-all-start.4 = ((f32[64,32,128]{2,1,0:T(8,128)}), f32[64,32,128]{2,1,0:T(8,128)S(1)}, u32[]{:S(2)}, u32[]{:S(2)}) async-start(f32[64,32,128]{2,1,0:T(8,128)} %add.24), calls=%async_computation.4 | async-start | bytes 2097152 | tf_op jit(solution)/shard_map/all_to_all | solution.py:646
  148.8 20.1 %shard_map.259 = (f32[9,928,128]{2,1,0:T(8,128)}, f32[32,2,1152]{2,1,0:T(2,128)}, f32[8,1152]{1,0:T(8,128)}, bf16[9,928,128]{2,1,0:T(8,128)(2,1)}, f32[9,928,128]{2,1,0:T(8,128)}) custom-call(f32[9,928,128]{2,1,0:T(8,128)} %get-tuple-element.59.depth_ref, f32[9,928,128]{2,1,0:T(8,128)} %get-tuple-element.67.first_ref, ...), custom_call_target="tpu_custom_call" | custom-call | flops 106905600 | bytes 12582912 | tf_op jit(solution)/shard_map/pallas_call | solution.py:829
  168.9 6.6 %all-to-all-done.4 = f32[64,32,128]{2,1,0:T(8,128)S(1)} async-done(((f32[64,32,128]{2,1,0:T(8,128)}), f32[64,32,128]{2,1,0:T(8,128)S(1)}, u32[]{:S(2)}, u32[]{:S(2)}) %all-to-all-start.4) | async-done | bytes 1048608 | tf_op jit(solution)/shard_map/all_to_all | solution.py:646
  175.5 7.8 %all-to-all-start.5 = ((f32[32,2,1152]{2,1,0:T(2,128)}), f32[32,2,1152]{2,1,0:T(2,128)S(1)}, u32[]{:S(2)}, u32[]{:S(2)}) async-start(f32[32,2,1152]{2,1,0:T(2,128)} %get-tuple-element.80), calls=%async_computation.5 | async-start | bytes 589824 | tf_op jit(solution)/shard_map/all_to_all | solution.py:646
  185.5 12.7 %shard_map.260.sums_ref = f32[32,1152]{1,0:T(8,128)} custom-call(bf16[9,928,128]{2,1,0:T(8,128)(2,1)} %get-tuple-element.81.field_ref, f32[9,928,128]{2,1,0:T(8,128)} %get-tuple-element.82.back_ref, f32[8,1152]{1,0:T(8,128)} %get-tuple-element.83.sums_ref), custom_call_target="tpu_custom_call" | custom-call | flops 53452800 | bytes 12582912 | tf_op jit(solution)/shard_map/pallas_call | solution.py:856
  198.8 11.1 %shard_map.261 = (bf16[29,29,176]{2,1,0:T(8,128)(2,1)}, f32[2048,128]{1,0:T(8,128)}) custom-call(f32[9,928,128]{2,1,0:T(8,128)} %get-tuple-element.76.grad_ref, f32[32,2,1152]{2,1,0:T(2,128)} %copy-done.4, f32[32,1152]{1,0:T(8,128)} %pad.38.table_ref, f32[8,1152]{1,0:T(8,128)} %get-tuple-element.75.moment_one_ref.moment_ref, ...), custom_call_target="tpu_custom_call" | custom-call | flops 1128923136 | bytes 12582912 | tf_op jit(solution)/shard_map/pallas_call | solution.py:863
  211.2 4.0 %collective-permute-start.1 = (f32[64,16,128]{2,1,0:T(8,128)S(1)}, f32[64,16,128]{2,1,0:T(8,128)S(1)}, u32[]{:S(2)}, u32[]{:S(2)}) collective-permute-start(f32[64,16,128]{2,1,0:T(8,128)S(1)} %bitcast.32), channel_id=1, source_target_pairs={{0,1},{1,0},{2,3},{3,2},{4,5},{5,4},{6,7},{7,6},{8,9},{9,8},{10,11... | collective-permute-start | bytes 1572872 | tf_op jit(solution)/shard_map/ppermute | solution.py:650
  216.9 25.2 %all_to_all.45 = f32[64,16,128]{2,1,0:T(8,128)S(1)} all-to-all(f32[64,16,128]{2,1,0:T(8,128)S(1)} %add.25), channel_id=1, replica_groups=mesh['x'=4,'y'=8,'z'=8,'core'=2] {'y','z'}, dimensions={0} | all-to-all | bytes 1048576 | tf_op jit(solution)/shard_map/all_to_all | solution.py:646
  242.1 8.5 %all_to_all.46 = f32[4,48,128]{2,1,0:T(8,128)S(1)} all-to-all(f32[4,48,128]{2,1,0:T(8,128)S(1)} %broadcast_in_dim.47), channel_id=1, replica_groups=mesh['x'=4,'y'=8,'z'=8,'core'=2] {'x'}, dimensions={0} | all-to-all | bytes 196608 | tf_op jit(solution)/shard_map/all_to_all | solution.py:646
  250.8 43.7 %all_to_all.47 = f32[64,48,128]{2,1,0:T(8,128)S(1)} all-to-all(f32[64,48,128]{2,1,0:T(8,128)S(1)} %broadcast_in_dim.48), channel_id=1, replica_groups=mesh['x'=4,'y'=8,'z'=8,'core'=2] {'y','z'}, dimensions={0} | all-to-all | bytes 3145728 | tf_op jit(solution)/shard_map/all_to_all | solution.py:646
  294.4 7.1 %collective-permute-start.2 = (f32[64,48,128]{2,1,0:T(8,128)S(1)}, f32[64,48,128]{2,1,0:T(8,128)S(1)}, u32[]{:S(2)}, u32[]{:S(2)}) collective-permute-start(f32[64,48,128]{2,1,0:T(8,128)S(1)} %all_to_all.47), channel_id=1, source_target_pairs={{0,1},{1,0},{2,3},{3,2},{4,5},{5,4},{6,7},{7,6},{8,9},{9,8},{10,11... | collective-permute-start | bytes 4718600 | tf_op jit(solution)/shard_map/ppermute | solution.py:650
  (77 shorter events, 39.6 us)
Async XLA Ops:
  0.6 19.5 %copy-start.11 = (f32[1056]{0:T(1024)S(1)}, f32[1056]{0:T(1024)}, u32[]{:S(2)}) copy-start(f32[1056]{0:T(1024)} %param.18) | copy-start | bytes 12676
  0.7 19.5 %copy-start.12 = (f32[1056]{0:T(1024)S(1)}, f32[1056]{0:T(1024)}, u32[]{:S(2)}) copy-start(f32[1056]{0:T(1024)} %param.19) | copy-start | bytes 12676
  0.7 19.5 %copy-start.13 = (f32[1056]{0:T(1024)S(1)}, f32[1056]{0:T(1024)}, u32[]{:S(2)}) copy-start(f32[1056]{0:T(1024)} %param.21) | copy-start | bytes 12676
  0.7 19.5 %copy-start.14 = (f32[1056]{0:T(1024)S(1)}, f32[1056]{0:T(1024)}, u32[]{:S(2)}) copy-start(f32[1056]{0:T(1024)} %param.22) | copy-start | bytes 12676
  0.7 19.5 %copy-start.10 = (bf16[25,1056]{1,0:T(8,128)(2,1)S(1)}, bf16[25,1056]{1,0:T(8,128)(2,1)}, u32[]{:S(2)}) copy-start(bf16[25,1056]{1,0:T(8,128)(2,1)} %param.20) | copy-start | bytes 158404
  9.5 44.7 %copy-start.1 = (bf16[1056,176]{0,1:T(8,128)(2,1)S(1)}, bf16[1056,176]{0,1:T(8,128)(2,1)}, u32[]{:S(2)}) copy-start(bf16[1056,176]{0,1:T(8,128)(2,1)} %param.27) | copy-start | bytes 1115140
  9.5 20.6 %all-to-all-start = ((f32[32,2,1152]{2,1,0:T(2,128)}), f32[32,2,1152]{2,1,0:T(2,128)S(1)}, u32[]{:S(2)}, u32[]{:S(2)}) async-start(f32[32,2,1152]{2,1,0:T(2,128)} %get-tuple-element.58), calls=%async_computation | async-start | bytes 589824 | tf_op jit(solution)/shard_map/all_to_all | solution.py:646
  30.0 0.7 copy-start.7
  30.8 24.5 %copy-start.16 = (f32[44]{0:T(128)S(1)}, f32[44]{0:T(128)}, u32[]{:S(2)}) copy-start(f32[44]{0:T(128)} %param.24) | copy-start | bytes 532
  30.8 24.5 %copy-start.15 = (f32[1056]{0:T(1024)S(1)}, f32[1056]{0:T(1024)}, u32[]{:S(2)}) copy-start(f32[1056]{0:T(1024)} %param.26) | copy-start | bytes 12676
  30.8 25.1 %copy-start.8 = (bf16[44,1056]{1,0:T(8,128)(2,1)S(1)}, bf16[44,1056]{1,0:T(8,128)(2,1)}, u32[]{:S(2)}) copy-start(bf16[44,1056]{1,0:T(8,128)(2,1)} %param.25) | copy-start | bytes 278788
  30.8 25.1 %copy-start.9 = (bf16[1056,44]{0,1:T(8,128)(2,1)S(1)}, bf16[1056,44]{0,1:T(8,128)(2,1)}, u32[]{:S(2)}) copy-start(bf16[1056,44]{0,1:T(8,128)(2,1)} %param.23) | copy-start | bytes 278788
  47.6 16.4 %all-to-all-start.1 = ((f32[32,2,1152]{2,1,0:T(2,128)}), f32[32,2,1152]{2,1,0:T(2,128)S(1)}, u32[]{:S(2)}, u32[]{:S(2)}) async-start(f32[32,2,1152]{2,1,0:T(2,128)} %get-tuple-element.60), calls=%async_computation.1 | async-start | bytes 589824 | tf_op jit(solution)/shard_map/all_to_all | solution.py:646
  64.0 0.7 copy-start.5
  75.0 14.9 %all-to-all-start.2 = ((f32[32,4,176]{2,1,0:T(4,128)}), f32[32,4,176]{2,1,0:T(4,128)S(1)}, u32[]{:S(2)}, u32[]{:S(2)}) async-start(f32[32,4,176]{2,1,0:T(4,128)} %get-tuple-element.61), calls=%async_computation.2 | async-start | bytes 262144 | tf_op jit(solution)/shard_map/all_to_all | solution.py:646
  112.8 9.9 %collective-permute-start = (f32[64,32,128]{2,1,0:T(8,128)S(1)}, f32[64,32,128]{2,1,0:T(8,128)}, u32[]{:S(2)}, u32[]{:S(2)}) collective-permute-start(f32[64,32,128]{2,1,0:T(8,128)S(1)} %bitcast.31), channel_id=1, source_target_pairs={{0,1},{1,0},{2,3},{3,2},{4,5},{5,4},{6,7},{7,6},{8,9},{9,8},{10,11... | collective-permute-start | bytes 3145736 | tf_op jit(solution)/shard_map/ppermute | solution.py:650
  118.8 14.9 %all-to-all-start.3 = ((f32[32,2,1152]{2,1,0:T(2,128)}), f32[32,2,1152]{2,1,0:T(2,128)S(1)}, u32[]{:S(2)}, u32[]{:S(2)}) async-start(f32[32,2,1152]{2,1,0:T(2,128)} %get-tuple-element.73), calls=%async_computation.3 | async-start | bytes 589824 | tf_op jit(solution)/shard_map/all_to_all | solution.py:646
  133.7 15.1 %copy-start.3 = (f32[32,2,1152]{2,1,0:T(2,128)}, f32[32,2,1152]{2,1,0:T(2,128)S(1)}, u32[]{:S(2)}) copy-start(f32[32,2,1152]{2,1,0:T(2,128)S(1)} %all-to-all-done.3.gathered_ref) | copy-start | bytes 884740
  133.7 41.8 %all-to-all-start.4 = ((f32[64,32,128]{2,1,0:T(8,128)}), f32[64,32,128]{2,1,0:T(8,128)S(1)}, u32[]{:S(2)}, u32[]{:S(2)}) async-start(f32[64,32,128]{2,1,0:T(8,128)} %add.24), calls=%async_computation.4 | async-start | bytes 2097152 | tf_op jit(solution)/shard_map/all_to_all | solution.py:646
  148.8 34.6 %copy-start = (bf16[928,176]{1,0:T(8,128)(2,1)S(1)}, bf16[928,176]{1,0:T(8,128)(2,1)}, u32[]{:S(2)}) copy-start(bf16[928,176]{1,0:T(8,128)(2,1)} %get-tuple-element.57.xpad_ref) | copy-start | bytes 979972
  168.8 15.5 %copy-start.2 = (bf16[176,1056]{1,0:T(8,128)(2,1)S(1)}, bf16[176,1056]{1,0:T(8,128)(2,1)}, u32[]{:S(2)}) copy-start(bf16[176,1056]{1,0:T(8,128)(2,1)} %param.17) | copy-start | bytes 1115140
  175.5 22.6 %all-to-all-start.5 = ((f32[32,2,1152]{2,1,0:T(2,128)}), f32[32,2,1152]{2,1,0:T(2,128)S(1)}, u32[]{:S(2)}, u32[]{:S(2)}) async-start(f32[32,2,1152]{2,1,0:T(2,128)} %get-tuple-element.80), calls=%async_computation.5 | async-start | bytes 589824 | tf_op jit(solution)/shard_map/all_to_all | solution.py:646
  211.2 5.6 %collective-permute-start.1 = (f32[64,16,128]{2,1,0:T(8,128)S(1)}, f32[64,16,128]{2,1,0:T(8,128)S(1)}, u32[]{:S(2)}, u32[]{:S(2)}) collective-permute-start(f32[64,16,128]{2,1,0:T(8,128)S(1)} %bitcast.32), channel_id=1, source_target_pairs={{0,1},{1,0},{2,3},{3,2},{4,5},{5,4},{6,7},{7,6},{8,9},{9,8},{10,11... | collective-permute-start | bytes 1572872 | tf_op jit(solution)/shard_map/ppermute | solution.py:650
  294.4 10.2 %collective-permute-start.2 = (f32[64,48,128]{2,1,0:T(8,128)S(1)}, f32[64,48,128]{2,1,0:T(8,128)S(1)}, u32[]{:S(2)}, u32[]{:S(2)}) collective-permute-start(f32[64,48,128]{2,1,0:T(8,128)S(1)} %all_to_all.47), channel_id=1, source_target_pairs={{0,1},{1,0},{2,3},{3,2},{4,5},{5,4},{6,7},{7,6},{8,9},{9,8},{10,11... | collective-permute-start | bytes 4718600 | tf_op jit(solution)/shard_map/ppermute | solution.py:650
  (2 other events, 1.3 us)

commit v5 on v4

--- a/solution.py
+++ b/solution.py
@@ -30,9 +30,12 @@
 EARLY = C + 2 * SE_ROWS
 UPPER_AT = CHUNKS * EARLY
 UPPER_ROWS = 1024
-EARLY_ROWS = 4096
+EARLY_ROWS = 3584
 LATE = C + TABLE
 LATE_ROWS = 2048
+PIECE = 4
+RESIDENT = 20 * 2**20
+STREAMED = 56 * 2**20
 F32 = jnp.float32
 BF16 = jnp.bfloat16
 
@@ -297,8 +300,6 @@
     column_ref,
     wreduce_ref,
     wrestore_ref,
-    first_ref,
-    slope_ref,
     hidden_ref,
     gpp_ref,
     row_ref,
@@ -351,8 +352,6 @@
         hidden_ref[row_at(i), :] = jnp.where(mask, silu * excite, 0.0).astype(BF16)
         back = back_ref[row_at(i), :]
         first = back * slope
-        first_ref[row_at(i), :] = first
-        slope_ref[row_at(i), :] = slope
         return (
             accs[0] + back * silu,
             accs[1] + first,
@@ -414,8 +413,8 @@
 
 def back_depth_kernel(
     depth_ref,
-    first_ref,
-    slope_ref,
+    gpp_ref,
+    wproject_ref,
     gathered_ref,
     table_ref,
     moment_two_ref,
@@ -433,6 +432,7 @@
     ghalo_ref,
     side_ref,
     tap_ref,
+    product_ref,
 ):
     @pl.when(pl.program_id(0) == 0)
     def _():
@@ -445,8 +445,10 @@
     mean_first = gain * total[0:1] / count
     mean_second = gain * total[1:2] / count
     center, scale = moment_two_ref[0:1, :], moment_two_ref[1:2, :]
+    shift = table_ref[SHIFT_TWO : SHIFT_TWO + 1, :]
     excite = vector_ref[1:2, :] * gain
     pooled = pooled_ref[0:1, :] * gain
+    product_ref[...] = dot(gpp_ref[...], wproject_ref[...])
     center_one, scale_one = moment_one_ref[0:1, :], moment_one_ref[1:2, :]
     slope_one = scale_one * table_ref[GAIN_ONE : GAIN_ONE + 1, :]
     offset_one = table_ref[SHIFT_ONE : SHIFT_ONE + 1, :] - center_one * slope_one
@@ -454,10 +456,12 @@
 
     def prepare(i, _):
         normed = (depth_ref[row_at(i), :] - center) * scale
-        grad = first_ref[row_at(i), :] * excite + slope_ref[row_at(i), :] * pooled
+        act = normed * gain + shift
+        sig = logistic(act)
+        grad = (product_ref[row_at(i), :] * excite + pooled) * (sig * (1.0 + act * (1.0 - sig)))
         grad = jnp.where(mask, scale * (grad - mean_first - normed * mean_second), 0.0)
         ghalo_ref[row_at(i + 2), :] = grad
-        back_ref[row_at(i), :] = grad
+        back_ref[row_at(i), :] = grad.astype(BF16)
         act = pre_ref[row_at(i), :] * slope_one + offset_one
         sig = logistic(act)
         field_ref[row_at(i), :] = jnp.where(mask, act * sig, 0.0).astype(BF16)
@@ -488,7 +492,7 @@
     halo_ref[2 * WIDE : 2 * WIDE + ROWS, :] = field_ref[...].astype(F32)
 
     def kernel_grad(i, accs):
-        grad = back_ref[row_at(i), :]
+        grad = back_ref[row_at(i), :].astype(F32)
         shifted = [
             (grad if b == 2 else pltpu.roll(grad, (b - 2) % WIDE, 0)).reshape(
                 WIDE // 8, 8, LANES
@@ -555,9 +559,12 @@
 
 
 def put_row(ref, rows_ref, row, height, scale):
-    for c in range(-(-ref.shape[1] // LANES)):
-        width = min(LANES, ref.shape[1] - c * LANES)
+    for c in range(-(-ref.shape[-1] // LANES)):
+        width = min(LANES, ref.shape[-1] - c * LANES)
         at = c * height + row
+        if len(ref.shape) == 1:
+            ref[c * LANES : c * LANES + width] = rows_ref[at, 0:width] * scale
+            continue
         ref[:, c * LANES : c * LANES + width] = rows_ref[at : at + ref.shape[0], 0:width] * scale
 
 
@@ -582,7 +589,7 @@
     put_row(gain_ref, rows_ref, C + SE + 2, EARLY, scale)
     put_row(gproject_ref, rows_ref, C + SE + 3, EARLY, scale)
     at = 2 * EARLY + C + SE + 3
-    breduce_ref[...] = rows_ref[at : at + 1, 0:SE] * scale
+    breduce_ref[...] = rows_ref[at, 0:SE] * scale
     upper_ref[...] = rows_ref[UPPER_AT : UPPER_AT + UPPER_ROWS, :]
 
 
@@ -597,7 +604,7 @@
     return pl.pallas_call(
         functools.partial(kernel, scale),
         out_shape=tuple(f32(*shape) for shape in shapes),
-        compiler_params=pltpu.CompilerParams(vmem_limit_bytes=56 * 2**20),
+        compiler_params=pltpu.CompilerParams(vmem_limit_bytes=RESIDENT),
         cost_estimate=pl.CostEstimate(
             flops=rows.size, bytes_accessed=8 * rows.size, transcendentals=0
         ),
@@ -627,7 +634,7 @@
     return jax.ShapeDtypeStruct(shape, F32)
 
 
-def call(kernel, ins, outs, scratch, flops):
+def call(kernel, ins, outs, scratch, flops, vmem=RESIDENT):
     return pl.pallas_call(
         kernel,
         grid=(CHUNKS,),
@@ -635,7 +642,7 @@
         out_specs=tuple(spec for spec, _ in outs),
         out_shape=tuple(shape for _, shape in outs),
         scratch_shapes=scratch,
-        compiler_params=pltpu.CompilerParams(vmem_limit_bytes=56 * 2**20),
+        compiler_params=pltpu.CompilerParams(vmem_limit_bytes=vmem),
         cost_estimate=pl.CostEstimate(
             flops=flops, bytes_accessed=12 * 2**20, transcendentals=ROWS * PADDED
         ),
@@ -653,7 +660,7 @@
 def pair_sum(rows):
     plane = lax.axis_size(PLANE)
     near = lax.axis_index("core") == 0
-    halves = rows.reshape(2, plane, -1, LANES)
+    halves = rows.reshape(2, plane, -1, PIECE, LANES)
     mine = jnp.where(near, halves[0], halves[1])
     return mine + swap(jnp.where(near, halves[1], halves[0]))
 
@@ -767,7 +774,7 @@
         matmul,
     )(depth, gathered, table, wproj, cot, wred, wres, bred, bres)
     gathered = exchange(stat, GROUP)
-    first, slope, hidden, gpp, rows, reduce, stat = call(
+    hidden, gpp, rows, reduce, stat = call(
         back_project_kernel,
         [
             MAP_BLOCK,
@@ -784,8 +791,6 @@
             se_spec,
         ],
         [
-            (MAP_BLOCK, MAP),
-            (MAP_BLOCK, MAP),
             (MAP_BLOCK, MAP_BF16),
             (whole((ROWS, C)), EDGE_BF16),
             (whole((8, PADDED)), f32(8, PADDED)),
@@ -830,8 +835,8 @@
         back_depth_kernel,
         [
             MAP_BLOCK,
-            MAP_BLOCK,
-            MAP_BLOCK,
+            xpad_spec,
+            w_spec,
             peer_block(peers),
             lane_block(TABLE),
             lane_block(8),
@@ -846,11 +851,24 @@
             stat_out,
             (lane_block(8), f32(8, PADDED)),
             (MAP_BLOCK, MAP_BF16),
-            (MAP_BLOCK, MAP),
+            (MAP_BLOCK, MAP_BF16),
         ],
-        [map_f32, halo, map_f32, taps],
+        [map_f32, halo, map_f32, taps, map_f32],
         100 * ROWS * PADDED,
-    )(depth, first, slope, gathered, table, moment_two, moment_one, vector, rows, xpad, wexp)
+        STREAMED,
+    )(
+        depth,
+        gpp,
+        wproj_turn,
+        gathered,
+        table,
+        moment_two,
+        moment_one,
+        vector,
+        rows,
+        xpad,
+        wexp,
+    )
     stat, early, field = lax.optimization_barrier((stat, early, field))
     gathered = exchange(stat, GROUP)
     (sums,) = call(
@@ -859,6 +877,7 @@
         [(lane_block(TABLE), f32(TABLE, PADDED))],
         [halo],
         50 * ROWS * PADDED,
+        STREAMED,
     )(field, back, sums)
     input_grad, late = call(
         back_expand_kernel,
@@ -889,12 +908,12 @@
     late = full[:, :, split:].reshape(LATE_ROWS, LANES)
 
     scale = 1.0 / images_total
-    wide = (1, HID)
+    wide = (HID,)
     g_project, g_restore, g_reduce, g_brestore, g_shift_two, g_gain_two, g_gproject, g_breduce, upper = (
         unpack(
             unpack_early_kernel,
             early,
-            [(C, HID), (SE, HID), (SE, HID), wide, wide, wide, (1, C), (1, SE), (UPPER_ROWS, LANES)],
+            [(C, HID), (SE, HID), (SE, HID), wide, wide, wide, (C,), (SE,), (UPPER_ROWS, LANES)],
             scale,
         )
     )
@@ -904,17 +923,17 @@
     return (
         input_grad[None, None],
         g_expand,
-        g_gain_one[0],
-        g_shift_one[0],
+        g_gain_one,
+        g_shift_one,
         g_depth,
-        g_gain_two[0],
-        g_shift_two[0],
+        g_gain_two,
+        g_shift_two,
         g_reduce.T,
-        g_breduce[0],
+        g_breduce,
         g_restore,
-        g_brestore[0],
+        g_brestore,
         g_project.T,
-        g_gproject[0],
+        g_gproject,
         upper.reshape(-1),
     )
 

time: 322 us -> 286 us (0.89)
  Pallas kernels: 104 us -> 77.8 us
  other arithmetic: 15.8 us -> 4.14 us
  local copies, waits for them, and re-layouts: 10.2 us -> 16.1 us
    unnamed x36 -> x74, local copies, waits for them, and re-layouts: 2.57 us -> 13.3 us
    pallas_call x5 -> x0, other arithmetic: 6.52 us -> none  [unpack(): pl.pallas_call(functools.partial(kernel, scale), out_shape=tuple((f32(*sh...]
    pallas_call x1, Pallas kernels: 12.3 us -> 6.38 us  [per_device(): call(back_project_kernel, [MAP_BLOCK, whole((peers, 4, C)), lane_block(TA...]
    pallas_call x1, Pallas kernels: 10.3 us -> 4.37 us  [per_device(): call(project_kernel, [MAP_BLOCK, peer_block(peers), lane_block(TABLE), wh...]
    pallas_call x1, Pallas kernels: 8.21 us -> 2.96 us  [per_device(): call(early_kernel, [whole((ROWS, C)), MAP_BLOCK, lane_block(8), whole((SE...]
    pallas_call x1, Pallas kernels: 11.1 us -> 7.51 us  [per_device(): call(back_expand_kernel, [MAP_BLOCK, peer_block(peers), lane_block(TABLE)...]
  transfers between devices with their start and end apart: 9 -> 9, of which waited for: 7 -> 7; matrix products, arithmetic and copies ran while one was open for 3% -> 2% of each run, Pallas kernels for 10% -> 12%
where the time goes in v5:
time: 286 us; the launch traced here: 285 us
  Pallas kernels  77.8 us (27%)
  blocking collectives  75.1 us (26%)
  starting transfers between devices  66.2 us (23%)
  waiting for transfers between devices  43.9 us (15%)
  local copies, waits for them, and re-layouts  16.1 us (6%)
  other arithmetic  4.14 us (1%)
    all_to_all x3, blocking collectives, exchange(): return lax.all_to_all(copies, axes, 0, 0, tiled=True)  75.1 us
    all_to_all x6, starting transfers between devices, exchange(): return lax.all_to_all(copies, axes, 0, 0, tiled=True)  50.1 us
    all_to_all x6, waiting for transfers between devices, exchange(): return lax.all_to_all(copies, axes, 0, 0, tiled=True)  39.6 us
    pallas_call x1, Pallas kernels, per_device(): call(back_depth_kernel, [MAP_BLOCK, xpad_spec, w_spec, peer_block(peers),...  20.3 us
    ppermute x3, starting transfers between devices, swap(): lax.ppermute(rows, 'core', [(i, i ^ 1) for i in range(lax.axis_size('core...  16.1 us
    pallas_call x1, Pallas kernels, per_device(): call(forward_kernel, [xpad_spec, w_spec, peer_block(peers), lane_block(TA...  15.6 us
    unnamed x74, local copies, waits for them, and re-layouts  13.3 us
    pallas_call x1, Pallas kernels, per_device(): call(kernel_grad_kernel, [MAP_BLOCK, MAP_BLOCK, lane_block(8)], [(lane_bl...  13.2 us
  transfers between devices with their start and end apart: 9, of which 7 were waited for; matrix products, arithmetic and copies ran while one was open for 2% of the time, Pallas kernels for 12%

profile of v5, /device:TPU:1, one launch (start us, length us, event | category | flops | bytes accessed | tf_op | source)
XLA Modules:
  0.0 284.5 jit_solution(6367173176260438480)
XLA Ops:
  2.9 5.1 %shard_map.254 = (bf16[928,176]{1,0:T(8,128)(2,1)S(1)}, f32[32,2,1152]{2,1,0:T(2,128)}) custom-call(bf16[29,29,176]{2,1,0:T(8,128)(2,1)S(1)} %bitcast.28, bf16[176,1152]{1,0:T(8,128)(2,1)S(1)} %pad.37.w_ref), custom_call_target="tpu_custom_call" | custom-call | flops 376307712 | bytes 12582912 | tf_op jit(solution)/shard_map/pallas_call | solution.py:732
  8.0 10.5 %all-to-all-start = ((f32[32,2,1152]{2,1,0:T(2,128)}), f32[32,2,1152]{2,1,0:T(2,128)S(1)}, u32[]{:S(2)}, u32[]{:S(2)}) async-start(f32[32,2,1152]{2,1,0:T(2,128)} %get-tuple-element.56), calls=%async_computation | async-start | bytes 589824 | tf_op jit(solution)/shard_map/all_to_all | solution.py:653
  18.7 9.7 %all-to-all-done.gathered_ref = f32[32,2,1152]{2,1,0:T(2,128)S(1)} async-done(((f32[32,2,1152]{2,1,0:T(2,128)}), f32[32,2,1152]{2,1,0:T(2,128)S(1)}, u32[]{:S(2)}, u32[]{:S(2)}) %all-to-all-start) | async-done | bytes 294944 | tf_op jit(solution)/shard_map/all_to_all | solution.py:653
  28.5 15.6 %shard_map.255 = (f32[9,928,128]{2,1,0:T(8,128)S(1)}, f32[32,2,1152]{2,1,0:T(2,128)}, f32[8,1152]{1,0:T(8,128)S(1)}) custom-call(bf16[928,176]{1,0:T(8,128)(2,1)S(1)} %get-tuple-element.55.xpad_ref, bf16[176,1152]{1,0:T(8,128)(2,1)S(1)} %pad.37.w_ref, f32[32,2,1152]{2,1,0:T(2,128)S(1)} %all-to-all-done.gathered_ref, f32[32,1152]{1,0:T(8,128)S(1)} %pad.38.table_ref), custom_call_target="tpu_custom_call" | custom-call | flops 53452800 | bytes 12582912 | tf_op jit(solution)/shard_map/pallas_call | solution.py:740
  46.7 6.9 %all-to-all-start.1 = ((f32[32,2,1152]{2,1,0:T(2,128)}), f32[32,2,1152]{2,1,0:T(2,128)S(1)}, u32[]{:S(2)}, u32[]{:S(2)}) async-start(f32[32,2,1152]{2,1,0:T(2,128)} %get-tuple-element.58), calls=%async_computation.1 | async-start | bytes 589824 | tf_op jit(solution)/shard_map/all_to_all | solution.py:653
  54.1 9.3 %all-to-all-done.1.gathered_ref = f32[32,2,1152]{2,1,0:T(2,128)S(1)} async-done(((f32[32,2,1152]{2,1,0:T(2,128)}), f32[32,2,1152]{2,1,0:T(2,128)S(1)}, u32[]{:S(2)}, u32[]{:S(2)}) %all-to-all-start.1) | async-done | bytes 294944 | tf_op jit(solution)/shard_map/all_to_all | solution.py:653
  65.7 4.4 %shard_map.256 = (f32[8,1152]{1,0:T(8,128)S(1)}, f32[928,176]{1,0:T(8,128)S(1)}, bf16[928,176]{1,0:T(8,128)(2,1)S(1)}, f32[8,1152]{1,0:T(8,128)S(1)}, f32[2,48,1...) custom-call(f32[9,928,128]{2,1,0:T(8,128)S(1)} %copy-done.1, f32[32,2,1152]{2,1,0:T(2,128)S(1)} %all-to-all-done.1.gathered_ref, ...), custom_call_target="tpu_custom_call" | custom-call | flops 376307712 | bytes 12582912 | tf_op jit(solution)/shard_map/pallas_call | solution.py:748
  70.7 6.4 %all-to-all-start.2 = ((f32[32,4,176]{2,1,0:T(4,128)}), f32[32,4,176]{2,1,0:T(4,128)S(1)}, u32[]{:S(2)}, u32[]{:S(2)}) async-start(f32[32,4,176]{2,1,0:T(4,128)} %copy-done.19), calls=%async_computation.2 | async-start | bytes 262144 | tf_op jit(solution)/shard_map/all_to_all | solution.py:653
  78.2 8.1 %all-to-all-done.2.gathered_ref = f32[32,4,176]{2,1,0:T(4,128)S(1)} async-done(((f32[32,4,176]{2,1,0:T(4,128)}), f32[32,4,176]{2,1,0:T(4,128)S(1)}, u32[]{:S(2)}, u32[]{:S(2)}) %all-to-all-start.2) | async-done | bytes 90144 | tf_op jit(solution)/shard_map/all_to_all | solution.py:653
  89.3 6.4 %shard_map.257 = (bf16[9,928,128]{2,1,0:T(8,128)(2,1)S(1)}, bf16[928,176]{1,0:T(8,128)(2,1)S(1)}, f32[8,1152]{1,0:T(8,128)S(1)}, f32[48,128]{1,0:T(8,128)S(1)}, f32[32,2,1152]{2,1,0:T(2,128)}) custom-call(f32[9,928,128]{2,1,0:T(8,128)S(1)} %copy-done.2, f32[32,4,176]{2,1,0:T(4,128)S(1)} %all-to-all-done.2.gathered_ref, f32[32,1152]{1,0:T(8,128)S(1)} %pad.38.table_ref, ...), custom_call_target="tpu_custom_call" | custom-call | flops 752615424 | bytes 12582912 | tf_op jit(solution)/shard_map/pallas_call | solution.py:777
  98.8 5.5 %collective-permute-start = (f32[64,7,4,128]{3,2,1,0:T(4,128)S(1)}, f32[64,7,4,128]{3,2,1,0:T(4,128)}, u32[]{:S(2)}, u32[]{:S(2)}) collective-permute-start(f32[64,7,4,128]{3,2,1,0:T(4,128)S(1)} %bitcast.33), channel_id=1, source_target_pairs={{0,1},{1,0},{2,3},{3,2},{4,5},{5,4},{6,7},{7,6},{8,9},{9,8},{10,11... | collective-permute-start | bytes 2752520 | tf_op jit(solution)/shard_map/ppermute | solution.py:657
  104.3 3.9 %all-to-all-start.3 = ((f32[32,2,1152]{2,1,0:T(2,128)}), f32[32,2,1152]{2,1,0:T(2,128)S(1)}, u32[]{:S(2)}, u32[]{:S(2)}) async-start(f32[32,2,1152]{2,1,0:T(2,128)} %get-tuple-element.69), calls=%async_computation.3 | async-start | bytes 589824 | tf_op jit(solution)/shard_map/all_to_all | solution.py:653
  110.5 8.6 %all-to-all-done.3.gathered_ref = f32[32,2,1152]{2,1,0:T(2,128)S(1)} async-done(((f32[32,2,1152]{2,1,0:T(2,128)}), f32[32,2,1152]{2,1,0:T(2,128)S(1)}, u32[]{:S(2)}, u32[]{:S(2)}) %all-to-all-start.3) | async-done | bytes 294944 | tf_op jit(solution)/shard_map/all_to_all | solution.py:653
  119.2 14.8 %all-to-all-start.4 = ((f32[64,7,4,128]{3,2,1,0:T(4,128)}), f32[64,7,4,128]{3,2,1,0:T(4,128)S(1)}, u32[]{:S(2)}, u32[]{:S(2)}) async-start(f32[64,7,4,128]{3,2,1,0:T(4,128)} %add.24), calls=%async_computation.4 | async-start | bytes 1835008 | tf_op jit(solution)/shard_map/all_to_all | solution.py:653
  134.0 20.3 %shard_map.259 = (f32[9,928,128]{2,1,0:T(8,128)}, f32[32,2,1152]{2,1,0:T(2,128)}, f32[8,1152]{1,0:T(8,128)}, bf16[9,928,128]{2,1,0:T(8,128)(2,1)}, bf16[9,928,128]{2,1,0:T(8,128)(2,1)}) custom-call(f32[9,928,128]{2,1,0:T(8,128)} %copy-done, bf16[928,176]{1,0:T(8,128)(2,1)} %copy-done.13, bf16[176,1152]{1,0:T(8,128)(2,1)} %copy-done.10, ...), custom_call_target="tpu_custom_call" | custom-call | flops 106905600 | bytes 12582912 | tf_op jit(solution)/shard_map/pallas_call | solution.py:834
  154.3 3.8 %all-to-all-done.4 = f32[64,7,4,128]{3,2,1,0:T(4,128)S(1)} async-done(((f32[64,7,4,128]{3,2,1,0:T(4,128)}), f32[64,7,4,128]{3,2,1,0:T(4,128)S(1)}, u32[]{:S(2)}, u32[]{:S(2)}) %all-to-all-start.4) | async-done | bytes 917536 | tf_op jit(solution)/shard_map/all_to_all | solution.py:653
  158.3 7.7 %all-to-all-start.5 = ((f32[32,2,1152]{2,1,0:T(2,128)}), f32[32,2,1152]{2,1,0:T(2,128)S(1)}, u32[]{:S(2)}, u32[]{:S(2)}) async-start(f32[32,2,1152]{2,1,0:T(2,128)} %get-tuple-element.76), calls=%async_computation.5 | async-start | bytes 589824 | tf_op jit(solution)/shard_map/all_to_all | solution.py:653
  166.5 13.2 %shard_map.260.sums_ref = f32[32,1152]{1,0:T(8,128)} custom-call(bf16[9,928,128]{2,1,0:T(8,128)(2,1)} %get-tuple-element.77.field_ref, bf16[9,928,128]{2,1,0:T(8,128)(2,1)} %get-tuple-element.78.back_ref, f32[8,1152]{1,0:T(8,128)} %get-tuple-element.79.sums_ref), custom_call_target="tpu_custom_call" | custom-call | flops 53452800 | bytes 12582912 | tf_op jit(solution)/shard_map/pallas_call | solution.py:874
  182.9 7.5 %shard_map.261 = (bf16[29,29,176]{2,1,0:T(8,128)(2,1)}, f32[2048,128]{1,0:T(8,128)S(1)}) custom-call(f32[9,928,128]{2,1,0:T(8,128)S(1)} %copy-done.3, f32[32,2,1152]{2,1,0:T(2,128)S(1)} %all-to-all-done.5.gathered_ref, f32[32,1152]{1,0:T(8,128)S(1)} %copy-done.7, f32[8,1152]{1,0:T(8,128)S(1)} %copy-done.15, bf16[928,176]{1,0:T(8,128)(2,1)S(1)} %copy-done.5, ...), custom_call_target="tpu_custom_call" | custom-call | flops 1128923136 | bytes 12582912 | tf_op jit(solution)/shard_map/pallas_call | solution.py:882
  190.5 4.0 %collective-permute-start.1 = (f32[64,4,4,128]{3,2,1,0:T(4,128)S(1)}, f32[64,4,4,128]{3,2,1,0:T(4,128)S(1)}, u32[]{:S(2)}, u32[]{:S(2)}) collective-permute-start(f32[64,4,4,128]{3,2,1,0:T(4,128)S(1)} %bitcast.34), channel_id=1, source_target_pairs={{0,1},{1,0},{2,3},{3,2},{4,5},{5,4},{6,7},{7,6},{8,9},{9,8},{10,11... | collective-permute-start | bytes 1572872 | tf_op jit(solution)/shard_map/ppermute | solution.py:657
  196.1 25.1 %all_to_all.45 = f32[64,4,4,128]{3,2,1,0:T(4,128)S(1)} all-to-all(f32[64,4,4,128]{3,2,1,0:T(4,128)S(1)} %add.25), channel_id=1, replica_groups=mesh['x'=4,'y'=8,'z'=8,'core'=2] {'y','z'}, dimensions={0} | all-to-all | bytes 1048576 | tf_op jit(solution)/shard_map/all_to_all | solution.py:653
  221.4 8.5 %all_to_all.46 = f32[4,11,4,128]{3,2,1,0:T(4,128)S(1)} all-to-all(f32[4,11,4,128]{3,2,1,0:T(4,128)S(1)} %broadcast_in_dim.47), channel_id=1, replica_groups=mesh['x'=4,'y'=8,'z'=8,'core'=2] {'x'}, dimensions={0} | all-to-all | bytes 180224 | tf_op jit(solution)/shard_map/all_to_all | solution.py:653
  230.1 41.5 %all_to_all.47 = f32[64,11,4,128]{3,2,1,0:T(4,128)S(1)} all-to-all(f32[64,11,4,128]{3,2,1,0:T(4,128)S(1)} %broadcast_in_dim.48), channel_id=1, replica_groups=mesh['x'=4,'y'=8,'z'=8,'core'=2] {'y','z'}, dimensions={0} | all-to-all | bytes 2883584 | tf_op jit(solution)/shard_map/all_to_all | solution.py:653
  271.6 6.6 %collective-permute-start.2 = (f32[64,11,4,128]{3,2,1,0:T(4,128)S(1)}, f32[64,11,4,128]{3,2,1,0:T(4,128)S(1)}, u32[]{:S(2)}, u32[]{:S(2)}) collective-permute-start(f32[64,11,4,128]{3,2,1,0:T(4,128)S(1)} %all_to_all.47), channel_id=1, source_target_pairs={{0,1},{1,0},{2,3},{3,2},{4,5},{5,4},{6,7},{7,6},{8,9},{9,8},{10,11... | collective-permute-start | bytes 4325384 | tf_op jit(solution)/shard_map/ppermute | solution.py:657
  (110 shorter events, 30.0 us)
Async XLA Ops:
  1.7 26.8 %copy-start.8 = (bf16[176,1152]{1,0:T(8,128)(2,1)}, bf16[176,1152]{1,0:T(8,128)(2,1)S(1)}, u32[]{:S(2)}) copy-start(bf16[176,1152]{1,0:T(8,128)(2,1)S(1)} %pad.37.w_ref) | copy-start | bytes 1216516
  2.9 15.6 %copy-start.30 = (f32[1056]{0:T(1024)S(1)}, f32[1056]{0:T(1024)}, u32[]{:S(2)}) copy-start(f32[1056]{0:T(1024)} %param.18) | copy-start | bytes 12676
  2.9 15.7 %copy-start.31 = (f32[1056]{0:T(1024)S(1)}, f32[1056]{0:T(1024)}, u32[]{:S(2)}) copy-start(f32[1056]{0:T(1024)} %param.19) | copy-start | bytes 12676
  2.9 15.7 %copy-start.32 = (f32[1056]{0:T(1024)S(1)}, f32[1056]{0:T(1024)}, u32[]{:S(2)}) copy-start(f32[1056]{0:T(1024)} %param.21) | copy-start | bytes 12676
  2.9 15.7 %copy-start.33 = (f32[1056]{0:T(1024)S(1)}, f32[1056]{0:T(1024)}, u32[]{:S(2)}) copy-start(f32[1056]{0:T(1024)} %param.22) | copy-start | bytes 12676
  2.9 15.7 %copy-start.29 = (bf16[25,1056]{1,0:T(8,128)(2,1)S(1)}, bf16[25,1056]{1,0:T(8,128)(2,1)}, u32[]{:S(2)}) copy-start(bf16[25,1056]{1,0:T(8,128)(2,1)} %param.20) | copy-start | bytes 158404
  8.0 36.1 %copy-start.4 = (bf16[928,176]{1,0:T(8,128)(2,1)}, bf16[928,176]{1,0:T(8,128)(2,1)S(1)}, u32[]{:S(2)}) copy-start(bf16[928,176]{1,0:T(8,128)(2,1)S(1)} %get-tuple-element.55.xpad_ref) | copy-start | bytes 979972
  8.0 20.5 %all-to-all-start = ((f32[32,2,1152]{2,1,0:T(2,128)}), f32[32,2,1152]{2,1,0:T(2,128)S(1)}, u32[]{:S(2)}, u32[]{:S(2)}) async-start(f32[32,2,1152]{2,1,0:T(2,128)} %get-tuple-element.56), calls=%async_computation | async-start | bytes 589824 | tf_op jit(solution)/shard_map/all_to_all | solution.py:653
  18.7 34.9 %copy-start.24 = (bf16[1056,176]{0,1:T(8,128)(2,1)S(1)}, bf16[1056,176]{0,1:T(8,128)(2,1)}, u32[]{:S(2)}) copy-start(bf16[1056,176]{0,1:T(8,128)(2,1)} %param.27) | copy-start | bytes 1115140
  18.7 67.6 %copy-start.6 = (f32[32,1152]{1,0:T(8,128)}, f32[32,1152]{1,0:T(8,128)S(1)}, u32[]{:S(2)}) copy-start(f32[32,1152]{1,0:T(8,128)S(1)} %pad.38.table_ref) | copy-start | bytes 442372
  46.7 16.7 %all-to-all-start.1 = ((f32[32,2,1152]{2,1,0:T(2,128)}), f32[32,2,1152]{2,1,0:T(2,128)S(1)}, u32[]{:S(2)}, u32[]{:S(2)}) async-start(f32[32,2,1152]{2,1,0:T(2,128)} %get-tuple-element.58), calls=%async_computation.1 | async-start | bytes 589824 | tf_op jit(solution)/shard_map/all_to_all | solution.py:653
  65.7 20.6 %copy-start.21 = (f32[176]{0:T(256)S(1)}, f32[176]{0:T(256)}, u32[]{:S(2)}) copy-start(f32[176]{0:T(256)} %param.28) | copy-start | bytes 2116
  70.7 24.9 %copy-start.16 = (f32[8,1152]{1,0:T(8,128)}, f32[8,1152]{1,0:T(8,128)S(1)}, u32[]{:S(2)}) copy-start(f32[8,1152]{1,0:T(8,128)S(1)} %get-tuple-element.60.moment_ref.moment_two_ref) | copy-start | bytes 110596
  70.7 15.6 %all-to-all-start.2 = ((f32[32,4,176]{2,1,0:T(4,128)}), f32[32,4,176]{2,1,0:T(4,128)S(1)}, u32[]{:S(2)}, u32[]{:S(2)}) async-start(f32[32,4,176]{2,1,0:T(4,128)} %copy-done.19), calls=%async_computation.2 | async-start | bytes 262144 | tf_op jit(solution)/shard_map/all_to_all | solution.py:653
  78.2 17.5 %copy-start.10 = (bf16[176,1152]{1,0:T(8,128)(2,1)}, bf16[176,1152]{1,0:T(8,128)(2,1)S(1)}, u32[]{:S(2)}) copy-start(bf16[176,1152]{1,0:T(8,128)(2,1)S(1)} %pad.46.wproject_ref) | copy-start | bytes 1216516
  98.8 9.4 %collective-permute-start = (f32[64,7,4,128]{3,2,1,0:T(4,128)S(1)}, f32[64,7,4,128]{3,2,1,0:T(4,128)}, u32[]{:S(2)}, u32[]{:S(2)}) collective-permute-start(f32[64,7,4,128]{3,2,1,0:T(4,128)S(1)} %bitcast.33), channel_id=1, source_target_pairs={{0,1},{1,0},{2,3},{3,2},{4,5},{5,4},{6,7},{7,6},{8,9},{9,8},{10,11... | collective-permute-start | bytes 2752520 | tf_op jit(solution)/shard_map/ppermute | solution.py:657
  104.3 14.9 %all-to-all-start.3 = ((f32[32,2,1152]{2,1,0:T(2,128)}), f32[32,2,1152]{2,1,0:T(2,128)S(1)}, u32[]{:S(2)}, u32[]{:S(2)}) async-start(f32[32,2,1152]{2,1,0:T(2,128)} %get-tuple-element.69), calls=%async_computation.3 | async-start | bytes 589824 | tf_op jit(solution)/shard_map/all_to_all | solution.py:653
  119.2 14.8 %copy-start.26 = (f32[32,2,1152]{2,1,0:T(2,128)}, f32[32,2,1152]{2,1,0:T(2,128)S(1)}, u32[]{:S(2)}) copy-start(f32[32,2,1152]{2,1,0:T(2,128)S(1)} %all-to-all-done.3.gathered_ref) | copy-start | bytes 884740
  119.2 38.9 %all-to-all-start.4 = ((f32[64,7,4,128]{3,2,1,0:T(4,128)}), f32[64,7,4,128]{3,2,1,0:T(4,128)S(1)}, u32[]{:S(2)}, u32[]{:S(2)}) async-start(f32[64,7,4,128]{3,2,1,0:T(4,128)} %add.24), calls=%async_computation.4 | async-start | bytes 1835008 | tf_op jit(solution)/shard_map/all_to_all | solution.py:653
  158.3 21.5 %all-to-all-start.5 = ((f32[32,2,1152]{2,1,0:T(2,128)}), f32[32,2,1152]{2,1,0:T(2,128)S(1)}, u32[]{:S(2)}, u32[]{:S(2)}) async-start(f32[32,2,1152]{2,1,0:T(2,128)} %get-tuple-element.76), calls=%async_computation.5 | async-start | bytes 589824 | tf_op jit(solution)/shard_map/all_to_all | solution.py:653
  166.5 13.3 %copy-start.7 = (f32[32,1152]{1,0:T(8,128)S(1)}, f32[32,1152]{1,0:T(8,128)}, u32[]{:S(2)}) copy-start(f32[32,1152]{1,0:T(8,128)} %copy-done.6) | copy-start | bytes 442372
  166.5 13.3 %copy-start.9 = (bf16[176,1152]{1,0:T(8,128)(2,1)S(1)}, bf16[176,1152]{1,0:T(8,128)(2,1)}, u32[]{:S(2)}) copy-start(bf16[176,1152]{1,0:T(8,128)(2,1)} %copy-done.8) | copy-start | bytes 1216516
  190.5 5.5 %collective-permute-start.1 = (f32[64,4,4,128]{3,2,1,0:T(4,128)S(1)}, f32[64,4,4,128]{3,2,1,0:T(4,128)S(1)}, u32[]{:S(2)}, u32[]{:S(2)}) collective-permute-start(f32[64,4,4,128]{3,2,1,0:T(4,128)S(1)} %bitcast.34), channel_id=1, source_target_pairs={{0,1},{1,0},{2,3},{3,2},{4,5},{5,4},{6,7},{7,6},{8,9},{9,8},{10,11... | collective-permute-start | bytes 1572872 | tf_op jit(solution)/shard_map/ppermute | solution.py:657
  271.6 9.4 %collective-permute-start.2 = (f32[64,11,4,128]{3,2,1,0:T(4,128)S(1)}, f32[64,11,4,128]{3,2,1,0:T(4,128)S(1)}, u32[]{:S(2)}, u32[]{:S(2)}) collective-permute-start(f32[64,11,4,128]{3,2,1,0:T(4,128)S(1)} %all_to_all.47), channel_id=1, source_target_pairs={{0,1},{1,0},{2,3},{3,2},{4,5},{5,4},{6,7},{7,6},{8,9},{9,8},{10,11... | collective-permute-start | bytes 4325384 | tf_op jit(solution)/shard_map/ppermute | solution.py:657
  (21 other events, 107.3 us)

commit v6 on v5

--- a/solution.py
+++ b/solution.py
@@ -34,6 +34,7 @@
 LATE = C + TABLE
 LATE_ROWS = 2048
 PIECE = 4
+BATCH = 4
 RESIDENT = 20 * 2**20
 STREAMED = 56 * 2**20
 F32 = jnp.float32
@@ -67,7 +68,15 @@
 
 
 def loop_rows(body, init):
-    return lax.fori_loop(0, SIDE, body, init)
+    def several(k, carry):
+        for j in range(BATCH):
+            carry = body(k * BATCH + j, carry)
+        return carry
+
+    init = lax.fori_loop(0, SIDE // BATCH, several, init)
+    for i in range(SIDE // BATCH * BATCH, SIDE):
+        init = body(i, init)
+    return init
 
 
 def col_sum(values):
@@ -743,6 +752,7 @@
         [(MAP_BLOCK, MAP), stat_out, moments],
         [map_f32, halo, taps],
         50 * ROWS * PADDED,
+        STREAMED,
     )(xpad, wexp, gathered, table)
     gathered = exchange(stat, GROUP)
     moment_two, project, cpad, vector, column, stat = call(

time: 286 us -> 282 us (0.986)
  Pallas kernels: 77.8 us -> 73.3 us
    unnamed x74 -> x72, local copies, waits for them, and re-layouts: 13.3 us -> 12.2 us
  transfers between devices with their start and end apart: 9 -> 9, of which waited for: 7 -> 7; matrix products, arithmetic and copies ran while one was open for 2% -> 2% of each run, Pallas kernels for 12% -> 11%
where the time goes in v6:
time: 282 us; the launch traced here: 281 us
  blocking collectives  75.3 us (27%)
  Pallas kernels  73.3 us (26%)
  starting transfers between devices  66.2 us (23%)
  waiting for transfers between devices  45 us (16%)
  local copies, waits for them, and re-layouts  15.7 us (6%)
  other arithmetic  4.15 us (1%)
    all_to_all x3, blocking collectives, exchange(): return lax.all_to_all(copies, axes, 0, 0, tiled=True)  75.3 us
    all_to_all x6, starting transfers between devices, exchange(): return lax.all_to_all(copies, axes, 0, 0, tiled=True)  50.2 us
    all_to_all x6, waiting for transfers between devices, exchange(): return lax.all_to_all(copies, axes, 0, 0, tiled=True)  40.6 us
    pallas_call x1, Pallas kernels, per_device(): call(back_depth_kernel, [MAP_BLOCK, xpad_spec, w_spec, peer_block(peers),...  18.6 us
    ppermute x3, starting transfers between devices, swap(): lax.ppermute(rows, 'core', [(i, i ^ 1) for i in range(lax.axis_size('core...  16 us
    pallas_call x1, Pallas kernels, per_device(): call(forward_kernel, [xpad_spec, w_spec, peer_block(peers), lane_block(TA...  14.8 us
    unnamed x72, local copies, waits for them, and re-layouts  12.2 us
    pallas_call x1, Pallas kernels, per_device(): call(kernel_grad_kernel, [MAP_BLOCK, MAP_BLOCK, lane_block(8)], [(lane_bl...  11.3 us
  transfers between devices with their start and end apart: 9, of which 7 were waited for; matrix products, arithmetic and copies ran while one was open for 2% of the time, Pallas kernels for 11%

profile of v6, /device:TPU:1, one launch (start us, length us, event | category | flops | bytes accessed | tf_op | source)
XLA Modules:
  0.0 280.9 jit_solution(3101059781422031640)
XLA Ops:
  2.9 5.1 %shard_map.254 = (bf16[928,176]{1,0:T(8,128)(2,1)S(1)}, f32[32,2,1152]{2,1,0:T(2,128)}) custom-call(bf16[29,29,176]{2,1,0:T(8,128)(2,1)S(1)} %bitcast.28, bf16[176,1152]{1,0:T(8,128)(2,1)S(1)} %pad.37.w_ref), custom_call_target="tpu_custom_call" | custom-call | flops 376307712 | bytes 12582912 | tf_op jit(solution)/shard_map/pallas_call | solution.py:741
  8.8 10.5 %all-to-all-start = ((f32[32,2,1152]{2,1,0:T(2,128)}), f32[32,2,1152]{2,1,0:T(2,128)S(1)}, u32[]{:S(2)}, u32[]{:S(2)}) async-start(f32[32,2,1152]{2,1,0:T(2,128)} %get-tuple-element.56), calls=%async_computation | async-start | bytes 589824 | tf_op jit(solution)/shard_map/all_to_all | solution.py:662
  20.1 9.1 %all-to-all-done.gathered_ref = f32[32,2,1152]{2,1,0:T(2,128)S(1)} async-done(((f32[32,2,1152]{2,1,0:T(2,128)}), f32[32,2,1152]{2,1,0:T(2,128)S(1)}, u32[]{:S(2)}, u32[]{:S(2)}) %all-to-all-start) | async-done | bytes 294944 | tf_op jit(solution)/shard_map/all_to_all | solution.py:662
  29.9 14.8 %shard_map.255 = (f32[9,928,128]{2,1,0:T(8,128)}, f32[32,2,1152]{2,1,0:T(2,128)}, f32[8,1152]{1,0:T(8,128)}) custom-call(bf16[928,176]{1,0:T(8,128)(2,1)} %copy-done.3, bf16[176,1152]{1,0:T(8,128)(2,1)} %copy-done.7, f32[32,2,1152]{2,1,0:T(2,128)} %copy-done.25, f32[32,1152]{1,0:T(8,128)} %pad.38.table_ref), custom_call_target="tpu_custom_call" | custom-call | flops 53452800 | bytes 12582912 | tf_op jit(solution)/shard_map/pallas_call | solution.py:749
  44.7 6.9 %all-to-all-start.1 = ((f32[32,2,1152]{2,1,0:T(2,128)}), f32[32,2,1152]{2,1,0:T(2,128)S(1)}, u32[]{:S(2)}, u32[]{:S(2)}) async-start(f32[32,2,1152]{2,1,0:T(2,128)} %get-tuple-element.58), calls=%async_computation.1 | async-start | bytes 589824 | tf_op jit(solution)/shard_map/all_to_all | solution.py:662
  52.2 9.3 %all-to-all-done.1.gathered_ref = f32[32,2,1152]{2,1,0:T(2,128)S(1)} async-done(((f32[32,2,1152]{2,1,0:T(2,128)}), f32[32,2,1152]{2,1,0:T(2,128)S(1)}, u32[]{:S(2)}, u32[]{:S(2)}) %all-to-all-start.1) | async-done | bytes 294944 | tf_op jit(solution)/shard_map/all_to_all | solution.py:662
  63.8 4.4 %shard_map.256 = (f32[8,1152]{1,0:T(8,128)S(1)}, f32[928,176]{1,0:T(8,128)S(1)}, bf16[928,176]{1,0:T(8,128)(2,1)S(1)}, f32[8,1152]{1,0:T(8,128)S(1)}, f32[2,48,1...) custom-call(f32[9,928,128]{2,1,0:T(8,128)S(1)} %copy-done, f32[32,2,1152]{2,1,0:T(2,128)S(1)} %all-to-all-done.1.gathered_ref, ...), custom_call_target="tpu_custom_call" | custom-call | flops 376307712 | bytes 12582912 | tf_op jit(solution)/shard_map/pallas_call | solution.py:758
  68.8 6.4 %all-to-all-start.2 = ((f32[32,4,176]{2,1,0:T(4,128)}), f32[32,4,176]{2,1,0:T(4,128)S(1)}, u32[]{:S(2)}, u32[]{:S(2)}) async-start(f32[32,4,176]{2,1,0:T(4,128)} %copy-done.17), calls=%async_computation.2 | async-start | bytes 262144 | tf_op jit(solution)/shard_map/all_to_all | solution.py:662
  76.3 8.1 %all-to-all-done.2.gathered_ref = f32[32,4,176]{2,1,0:T(4,128)S(1)} async-done(((f32[32,4,176]{2,1,0:T(4,128)}), f32[32,4,176]{2,1,0:T(4,128)S(1)}, u32[]{:S(2)}, u32[]{:S(2)}) %all-to-all-start.2) | async-done | bytes 90144 | tf_op jit(solution)/shard_map/all_to_all | solution.py:662
  87.4 6.4 %shard_map.257 = (bf16[9,928,128]{2,1,0:T(8,128)(2,1)S(1)}, bf16[928,176]{1,0:T(8,128)(2,1)S(1)}, f32[8,1152]{1,0:T(8,128)S(1)}, f32[48,128]{1,0:T(8,128)S(1)}, f32[32,2,1152]{2,1,0:T(2,128)}) custom-call(f32[9,928,128]{2,1,0:T(8,128)S(1)} %copy-done.1, f32[32,4,176]{2,1,0:T(4,128)S(1)} %all-to-all-done.2.gathered_ref, f32[32,1152]{1,0:T(8,128)S(1)} %copy-done.5, ...), custom_call_target="tpu_custom_call" | custom-call | flops 752615424 | bytes 12582912 | tf_op jit(solution)/shard_map/pallas_call | solution.py:787
  96.9 5.4 %collective-permute-start = (f32[64,7,4,128]{3,2,1,0:T(4,128)S(1)}, f32[64,7,4,128]{3,2,1,0:T(4,128)}, u32[]{:S(2)}, u32[]{:S(2)}) collective-permute-start(f32[64,7,4,128]{3,2,1,0:T(4,128)S(1)} %bitcast.33), channel_id=1, source_target_pairs={{0,1},{1,0},{2,3},{3,2},{4,5},{5,4},{6,7},{7,6},{8,9},{9,8},{10,11... | collective-permute-start | bytes 2752520 | tf_op jit(solution)/shard_map/ppermute | solution.py:666
  102.4 3.9 %all-to-all-start.3 = ((f32[32,2,1152]{2,1,0:T(2,128)}), f32[32,2,1152]{2,1,0:T(2,128)S(1)}, u32[]{:S(2)}, u32[]{:S(2)}) async-start(f32[32,2,1152]{2,1,0:T(2,128)} %get-tuple-element.69), calls=%async_computation.3 | async-start | bytes 589824 | tf_op jit(solution)/shard_map/all_to_all | solution.py:662
  108.6 8.6 %all-to-all-done.3.gathered_ref = f32[32,2,1152]{2,1,0:T(2,128)S(1)} async-done(((f32[32,2,1152]{2,1,0:T(2,128)}), f32[32,2,1152]{2,1,0:T(2,128)S(1)}, u32[]{:S(2)}, u32[]{:S(2)}) %all-to-all-start.3) | async-done | bytes 294944 | tf_op jit(solution)/shard_map/all_to_all | solution.py:662
  117.3 14.8 %all-to-all-start.4 = ((f32[64,7,4,128]{3,2,1,0:T(4,128)}), f32[64,7,4,128]{3,2,1,0:T(4,128)S(1)}, u32[]{:S(2)}, u32[]{:S(2)}) async-start(f32[64,7,4,128]{3,2,1,0:T(4,128)} %add.24), calls=%async_computation.4 | async-start | bytes 1835008 | tf_op jit(solution)/shard_map/all_to_all | solution.py:662
  132.1 18.6 %shard_map.259 = (f32[9,928,128]{2,1,0:T(8,128)}, f32[32,2,1152]{2,1,0:T(2,128)}, f32[8,1152]{1,0:T(8,128)}, bf16[9,928,128]{2,1,0:T(8,128)(2,1)}, bf16[9,928,128]{2,1,0:T(8,128)(2,1)}) custom-call(f32[9,928,128]{2,1,0:T(8,128)} %get-tuple-element.57.depth_ref, bf16[928,176]{1,0:T(8,128)(2,1)} %copy-done.12, bf16[176,1152]{1,0:T(8,128)(2,1)} %copy-done.9, ...), custom_call_target="tpu_custom_call" | custom-call | flops 106905600 | bytes 12582912 | tf_op jit(solution)/shard_map/pallas_call | solution.py:844
  150.7 5.5 %all-to-all-done.4 = f32[64,7,4,128]{3,2,1,0:T(4,128)S(1)} async-done(((f32[64,7,4,128]{3,2,1,0:T(4,128)}), f32[64,7,4,128]{3,2,1,0:T(4,128)S(1)}, u32[]{:S(2)}, u32[]{:S(2)}) %all-to-all-start.4) | async-done | bytes 917536 | tf_op jit(solution)/shard_map/all_to_all | solution.py:662
  156.4 7.7 %all-to-all-start.5 = ((f32[32,2,1152]{2,1,0:T(2,128)}), f32[32,2,1152]{2,1,0:T(2,128)S(1)}, u32[]{:S(2)}, u32[]{:S(2)}) async-start(f32[32,2,1152]{2,1,0:T(2,128)} %get-tuple-element.76), calls=%async_computation.5 | async-start | bytes 589824 | tf_op jit(solution)/shard_map/all_to_all | solution.py:662
  164.6 11.3 %shard_map.260.sums_ref = f32[32,1152]{1,0:T(8,128)} custom-call(bf16[9,928,128]{2,1,0:T(8,128)(2,1)} %get-tuple-element.77.field_ref, bf16[9,928,128]{2,1,0:T(8,128)(2,1)} %get-tuple-element.78.back_ref, f32[8,1152]{1,0:T(8,128)} %get-tuple-element.79.sums_ref), custom_call_target="tpu_custom_call" | custom-call | flops 53452800 | bytes 12582912 | tf_op jit(solution)/shard_map/pallas_call | solution.py:884
  179.0 7.5 %shard_map.261 = (bf16[29,29,176]{2,1,0:T(8,128)(2,1)}, f32[2048,128]{1,0:T(8,128)S(1)}) custom-call(f32[9,928,128]{2,1,0:T(8,128)S(1)} %copy-done.2, f32[32,2,1152]{2,1,0:T(2,128)S(1)} %all-to-all-done.5.gathered_ref, f32[32,1152]{1,0:T(8,128)S(1)} %copy-done.6, f32[8,1152]{1,0:T(8,128)S(1)} %copy-done.13, bf16[928,176]{1,0:T(8,128)(2,1)S(1)} %copy-done.4, ...), custom_call_target="tpu_custom_call" | custom-call | flops 1128923136 | bytes 12582912 | tf_op jit(solution)/shard_map/pallas_call | solution.py:892
  186.6 4.0 %collective-permute-start.1 = (f32[64,4,4,128]{3,2,1,0:T(4,128)S(1)}, f32[64,4,4,128]{3,2,1,0:T(4,128)S(1)}, u32[]{:S(2)}, u32[]{:S(2)}) collective-permute-start(f32[64,4,4,128]{3,2,1,0:T(4,128)S(1)} %bitcast.34), channel_id=1, source_target_pairs={{0,1},{1,0},{2,3},{3,2},{4,5},{5,4},{6,7},{7,6},{8,9},{9,8},{10,11... | collective-permute-start | bytes 1572872 | tf_op jit(solution)/shard_map/ppermute | solution.py:666
  192.3 25.3 %all_to_all.45 = f32[64,4,4,128]{3,2,1,0:T(4,128)S(1)} all-to-all(f32[64,4,4,128]{3,2,1,0:T(4,128)S(1)} %add.25), channel_id=1, replica_groups=mesh['x'=4,'y'=8,'z'=8,'core'=2] {'y','z'}, dimensions={0} | all-to-all | bytes 1048576 | tf_op jit(solution)/shard_map/all_to_all | solution.py:662
  217.7 8.5 %all_to_all.46 = f32[4,11,4,128]{3,2,1,0:T(4,128)S(1)} all-to-all(f32[4,11,4,128]{3,2,1,0:T(4,128)S(1)} %broadcast_in_dim.47), channel_id=1, replica_groups=mesh['x'=4,'y'=8,'z'=8,'core'=2] {'x'}, dimensions={0} | all-to-all | bytes 180224 | tf_op jit(solution)/shard_map/all_to_all | solution.py:662
  226.4 41.5 %all_to_all.47 = f32[64,11,4,128]{3,2,1,0:T(4,128)S(1)} all-to-all(f32[64,11,4,128]{3,2,1,0:T(4,128)S(1)} %broadcast_in_dim.48), channel_id=1, replica_groups=mesh['x'=4,'y'=8,'z'=8,'core'=2] {'y','z'}, dimensions={0} | all-to-all | bytes 2883584 | tf_op jit(solution)/shard_map/all_to_all | solution.py:662
  267.9 6.6 %collective-permute-start.2 = (f32[64,11,4,128]{3,2,1,0:T(4,128)S(1)}, f32[64,11,4,128]{3,2,1,0:T(4,128)S(1)}, u32[]{:S(2)}, u32[]{:S(2)}) collective-permute-start(f32[64,11,4,128]{3,2,1,0:T(4,128)S(1)} %all_to_all.47), channel_id=1, source_target_pairs={{0,1},{1,0},{2,3},{3,2},{4,5},{5,4},{6,7},{7,6},{8,9},{9,8},{10,11... | collective-permute-start | bytes 4325384 | tf_op jit(solution)/shard_map/ppermute | solution.py:666
  (108 shorter events, 29.5 us)
Async XLA Ops:
  1.7 17.8 %copy-start.7 = (bf16[176,1152]{1,0:T(8,128)(2,1)}, bf16[176,1152]{1,0:T(8,128)(2,1)S(1)}, u32[]{:S(2)}) copy-start(bf16[176,1152]{1,0:T(8,128)(2,1)S(1)} %pad.37.w_ref) | copy-start | bytes 1216516
  2.9 16.4 %copy-start.29 = (f32[1056]{0:T(1024)S(1)}, f32[1056]{0:T(1024)}, u32[]{:S(2)}) copy-start(f32[1056]{0:T(1024)} %param.18) | copy-start | bytes 12676
  2.9 16.4 %copy-start.30 = (f32[1056]{0:T(1024)S(1)}, f32[1056]{0:T(1024)}, u32[]{:S(2)}) copy-start(f32[1056]{0:T(1024)} %param.19) | copy-start | bytes 12676
  2.9 16.5 %copy-start.31 = (f32[1056]{0:T(1024)S(1)}, f32[1056]{0:T(1024)}, u32[]{:S(2)}) copy-start(f32[1056]{0:T(1024)} %param.21) | copy-start | bytes 12676
  2.9 16.5 %copy-start.32 = (f32[1056]{0:T(1024)S(1)}, f32[1056]{0:T(1024)}, u32[]{:S(2)}) copy-start(f32[1056]{0:T(1024)} %param.22) | copy-start | bytes 12676
  2.9 16.5 %copy-start.28 = (bf16[25,1056]{1,0:T(8,128)(2,1)S(1)}, bf16[25,1056]{1,0:T(8,128)(2,1)}, u32[]{:S(2)}) copy-start(bf16[25,1056]{1,0:T(8,128)(2,1)} %param.20) | copy-start | bytes 158404
  8.8 20.5 %all-to-all-start = ((f32[32,2,1152]{2,1,0:T(2,128)}), f32[32,2,1152]{2,1,0:T(2,128)S(1)}, u32[]{:S(2)}, u32[]{:S(2)}) async-start(f32[32,2,1152]{2,1,0:T(2,128)} %get-tuple-element.56), calls=%async_computation | async-start | bytes 589824 | tf_op jit(solution)/shard_map/all_to_all | solution.py:662
  19.5 32.2 %copy-start.22 = (bf16[1056,176]{0,1:T(8,128)(2,1)S(1)}, bf16[1056,176]{0,1:T(8,128)(2,1)}, u32[]{:S(2)}) copy-start(bf16[1056,176]{0,1:T(8,128)(2,1)} %param.27) | copy-start | bytes 1115140
  44.7 16.7 %all-to-all-start.1 = ((f32[32,2,1152]{2,1,0:T(2,128)}), f32[32,2,1152]{2,1,0:T(2,128)S(1)}, u32[]{:S(2)}, u32[]{:S(2)}) async-start(f32[32,2,1152]{2,1,0:T(2,128)} %get-tuple-element.58), calls=%async_computation.1 | async-start | bytes 589824 | tf_op jit(solution)/shard_map/all_to_all | solution.py:662
  63.8 20.7 %copy-start.19 = (f32[176]{0:T(256)S(1)}, f32[176]{0:T(256)}, u32[]{:S(2)}) copy-start(f32[176]{0:T(256)} %param.28) | copy-start | bytes 2116
  68.8 25.0 %copy-start.14 = (f32[8,1152]{1,0:T(8,128)}, f32[8,1152]{1,0:T(8,128)S(1)}, u32[]{:S(2)}) copy-start(f32[8,1152]{1,0:T(8,128)S(1)} %get-tuple-element.60.moment_ref.moment_two_ref) | copy-start | bytes 110596
  68.8 15.6 %all-to-all-start.2 = ((f32[32,4,176]{2,1,0:T(4,128)}), f32[32,4,176]{2,1,0:T(4,128)S(1)}, u32[]{:S(2)}, u32[]{:S(2)}) async-start(f32[32,4,176]{2,1,0:T(4,128)} %copy-done.17), calls=%async_computation.2 | async-start | bytes 262144 | tf_op jit(solution)/shard_map/all_to_all | solution.py:662
  76.3 17.5 %copy-start.9 = (bf16[176,1152]{1,0:T(8,128)(2,1)}, bf16[176,1152]{1,0:T(8,128)(2,1)S(1)}, u32[]{:S(2)}) copy-start(bf16[176,1152]{1,0:T(8,128)(2,1)S(1)} %pad.46.wproject_ref) | copy-start | bytes 1216516
  96.9 9.3 %collective-permute-start = (f32[64,7,4,128]{3,2,1,0:T(4,128)S(1)}, f32[64,7,4,128]{3,2,1,0:T(4,128)}, u32[]{:S(2)}, u32[]{:S(2)}) collective-permute-start(f32[64,7,4,128]{3,2,1,0:T(4,128)S(1)} %bitcast.33), channel_id=1, source_target_pairs={{0,1},{1,0},{2,3},{3,2},{4,5},{5,4},{6,7},{7,6},{8,9},{9,8},{10,11... | collective-permute-start | bytes 2752520 | tf_op jit(solution)/shard_map/ppermute | solution.py:666
  102.4 14.9 %all-to-all-start.3 = ((f32[32,2,1152]{2,1,0:T(2,128)}), f32[32,2,1152]{2,1,0:T(2,128)S(1)}, u32[]{:S(2)}, u32[]{:S(2)}) async-start(f32[32,2,1152]{2,1,0:T(2,128)} %get-tuple-element.69), calls=%async_computation.3 | async-start | bytes 589824 | tf_op jit(solution)/shard_map/all_to_all | solution.py:662
  117.3 14.8 %copy-start.24 = (f32[32,2,1152]{2,1,0:T(2,128)}, f32[32,2,1152]{2,1,0:T(2,128)S(1)}, u32[]{:S(2)}) copy-start(f32[32,2,1152]{2,1,0:T(2,128)S(1)} %all-to-all-done.3.gathered_ref) | copy-start | bytes 884740
  117.3 38.9 %all-to-all-start.4 = ((f32[64,7,4,128]{3,2,1,0:T(4,128)}), f32[64,7,4,128]{3,2,1,0:T(4,128)S(1)}, u32[]{:S(2)}, u32[]{:S(2)}) async-start(f32[64,7,4,128]{3,2,1,0:T(4,128)} %add.24), calls=%async_computation.4 | async-start | bytes 1835008 | tf_op jit(solution)/shard_map/all_to_all | solution.py:662
  150.6 13.4 %copy-start.4 = (bf16[928,176]{1,0:T(8,128)(2,1)S(1)}, bf16[928,176]{1,0:T(8,128)(2,1)}, u32[]{:S(2)}) copy-start(bf16[928,176]{1,0:T(8,128)(2,1)} %copy-done.3) | copy-start | bytes 979972
  150.7 13.6 %copy-start.23 = (bf16[176,1056]{1,0:T(8,128)(2,1)S(1)}, bf16[176,1056]{1,0:T(8,128)(2,1)}, u32[]{:S(2)}) copy-start(bf16[176,1056]{1,0:T(8,128)(2,1)} %param.17) | copy-start | bytes 1115140
  156.4 19.5 %all-to-all-start.5 = ((f32[32,2,1152]{2,1,0:T(2,128)}), f32[32,2,1152]{2,1,0:T(2,128)S(1)}, u32[]{:S(2)}, u32[]{:S(2)}) async-start(f32[32,2,1152]{2,1,0:T(2,128)} %get-tuple-element.76), calls=%async_computation.5 | async-start | bytes 589824 | tf_op jit(solution)/shard_map/all_to_all | solution.py:662
  164.6 11.3 %copy-start.6 = (f32[32,1152]{1,0:T(8,128)S(1)}, f32[32,1152]{1,0:T(8,128)}, u32[]{:S(2)}) copy-start(f32[32,1152]{1,0:T(8,128)} %pad.38.table_ref) | copy-start | bytes 442372
  164.6 11.3 %copy-start.8 = (bf16[176,1152]{1,0:T(8,128)(2,1)S(1)}, bf16[176,1152]{1,0:T(8,128)(2,1)}, u32[]{:S(2)}) copy-start(bf16[176,1152]{1,0:T(8,128)(2,1)} %copy-done.7) | copy-start | bytes 1216516
  186.6 5.5 %collective-permute-start.1 = (f32[64,4,4,128]{3,2,1,0:T(4,128)S(1)}, f32[64,4,4,128]{3,2,1,0:T(4,128)S(1)}, u32[]{:S(2)}, u32[]{:S(2)}) collective-permute-start(f32[64,4,4,128]{3,2,1,0:T(4,128)S(1)} %bitcast.34), channel_id=1, source_target_pairs={{0,1},{1,0},{2,3},{3,2},{4,5},{5,4},{6,7},{7,6},{8,9},{9,8},{10,11... | collective-permute-start | bytes 1572872 | tf_op jit(solution)/shard_map/ppermute | solution.py:666
  267.9 9.4 %collective-permute-start.2 = (f32[64,11,4,128]{3,2,1,0:T(4,128)S(1)}, f32[64,11,4,128]{3,2,1,0:T(4,128)S(1)}, u32[]{:S(2)}, u32[]{:S(2)}) collective-permute-start(f32[64,11,4,128]{3,2,1,0:T(4,128)S(1)} %all_to_all.47), channel_id=1, source_target_pairs={{0,1},{1,0},{2,3},{3,2},{4,5},{5,4},{6,7},{7,6},{8,9},{9,8},{10,11... | collective-permute-start | bytes 4325384 | tf_op jit(solution)/shard_map/ppermute | solution.py:666
  (20 other events, 91.0 us)
